TPU v7x, 32 devices: a whole 2x2x4 slice. The times are simulated.
32 devices in a mesh: cell: 16 (over z, y, x), aux: 2 (over core).
Axes of the slice: x: 2, y: 2, z: 4, core: 2. Of those that a mesh axis runs over, the one named last changes fastest.
Arguments:
- blocks: float32 [16, 8, 300, 300], P('cell', 'aux'), may hold values from -0.75 to 0.75
- cell_offsets: int32 [3, 16], replicated, may hold values from -2 to 1, as said below
- occ_coeff: float32 [2, 300, 60], replicated, may hold values from -0.25 to 0.25
- vir_coeff: float32 [16, 2, 300, 240], P('cell', None, None, 'aux'), may hold values from -0.25 to 0.25
- transfer_index: int32 [16], replicated, may hold values from 0 to 15, as said below
Outputs:
- pair_ints: float32 [2, 8, 16, 14400], P(None, 'aux', None, 'cell')
Inputs may be any that keep to these rules, and one draw needn't show every extreme that they name: `cell_offsets`: column R is the integer lattice vector of cell R; the columns are the 16 cells of the centred 4 x 4 x 1 supercell, each once, in an order drawn from the seed. `transfer_index`: entry k is the index (a 4 + b) + c of the k-point k - k1 folded into the 4 x 4 x 1 mesh, for one k1 drawn from the seed; every index appears once.
All inputs are finite; a program needn't handle non-finite values.
Results may differ from a plain program's by a relative error of at most 0.00007.
Values sent between devices are 32-bit elements; how exact they have to be, the bound alone decides.
No kernel may reach another device: no remote copies, remote signals or barrier semaphores. Data moves between devices by JAX's collectives and lax.ppermute only.
A program may use at most 64 MiB of HBM per device.

v0:
```python
import functools
import math

import jax
import jax.numpy as jnp
from jax import lax
from jax.experimental import pallas as pl
from jax.experimental.pallas import tpu as pltpu
from jax.sharding import PartitionSpec as P

KX = 4
KY = 4
LANES = 128
HALF_LANES = 64
BF16 = jnp.bfloat16
F32 = jnp.float32


def phase_tables(cell_offsets, cell_count):
    depth = cell_count // (KX * KY)
    points = jnp.arange(cell_count, dtype=jnp.int32)
    along_a = points // (KY * depth)
    along_b = points // depth % KY
    along_c = points % depth
    turns = (
        along_a[:, None] * cell_offsets[0][None, :] * (KY * depth)
        + along_b[:, None] * cell_offsets[1][None, :] * (KX * depth)
        + along_c[:, None] * cell_offsets[2][None, :] * (KX * KY)
    ) % cell_count
    angles = 2.0 * math.pi / cell_count * turns.astype(jnp.float32)
    return (jnp.cos(angles), jnp.sin(angles))


def matmul(left, right):
    return jnp.dot(left, right, precision=lax.Precision.HIGHEST, preferred_element_type=jnp.float32)


def contract(form, left, right):
    return jnp.einsum(form, left, right, precision=lax.Precision.HIGHEST)


def by_entries(blocks, cell_offsets, occ_coeff, vir_coeff, transfer_index):
    cell_count = lax.axis_size("cell")
    slab_rows = blocks.shape[1]
    basis_size = blocks.shape[2]
    occupied = occ_coeff.shape[2]
    cosines, sines = phase_tables(cell_offsets, cell_count)
    occ_real, occ_imag = (occ_coeff[0], occ_coeff[1])
    flattened = blocks.reshape(1, -1)
    arrived = lax.all_to_all(flattened, "cell", split_axis=1, concat_axis=0, tiled=True)
    grid_real = matmul(cosines, arrived)
    grid_imag = matmul(sines, arrived)
    back_real, back_imag = (
        lax.all_to_all(grid_real, "cell", split_axis=0, concat_axis=1, tiled=True),
        lax.all_to_all(grid_imag, "cell", split_axis=0, concat_axis=1, tiled=True),
    )
    spec_real = back_real.reshape(slab_rows, basis_size, basis_size)
    spec_imag = back_imag.reshape(slab_rows, basis_size, basis_size)
    half_real = contract("mi,pmn->pin", occ_real, spec_real) + contract(
        "mi,pmn->pin", occ_imag, spec_imag
    )
    half_imag = contract("mi,pmn->pin", occ_real, spec_imag) - contract(
        "mi,pmn->pin", occ_imag, spec_real
    )
    rows_real = half_real.reshape(slab_rows * occupied, basis_size)
    rows_imag = half_imag.reshape(slab_rows * occupied, basis_size)
    column_piece = lax.all_gather(vir_coeff, "aux", axis=3, tiled=True)
    coef_real = column_piece[0, 0]
    coef_imag = column_piece[0, 1]
    part_real = matmul(rows_real, coef_real) - matmul(rows_imag, coef_imag)
    part_imag = matmul(rows_real, coef_imag) + matmul(rows_imag, coef_real)
    banded = jnp.stack([part_real, part_imag])
    pair_rows = banded.reshape(2, slab_rows, 1, -1)
    regrouped = lax.all_to_all(pair_rows, "cell", split_axis=3, concat_axis=2, tiled=True)
    source = jnp.argsort(transfer_index)
    return jnp.take(regrouped, source, axis=2)


def split(value):
    high = value.astype(BF16)
    return high, (value - high.astype(F32)).astype(BF16)


def dot(left, right):
    return jnp.dot(left, right, preferred_element_type=F32)


def padded(count, step):
    return -(-count // step) * step


class Sizes:
    def __init__(self, blocks, occ_coeff, vir_coeff):
        self.slab = blocks.shape[1]
        self.basis = blocks.shape[2]
        self.occ = occ_coeff.shape[2]
        self.vir_half = vir_coeff.shape[3]
        self.main = self.basis // LANES * LANES
        self.rest = self.basis - self.main
        self.width = 2 * self.main + LANES
        self.bands = self.occ // KX
        self.rows = padded(self.bands, 8)
        self.chunk = self.vir_half // 2
        self.chunks = 4 * self.bands // KY
        self.tiles = self.chunks // 2 + 1
        self.pairs = self.chunk * self.chunks

    @staticmethod
    def fit(cells, aux, blocks, occ_coeff, vir_coeff):
        basis, occ, half = blocks.shape[2], occ_coeff.shape[2], vir_coeff.shape[3]
        return (
            cells == KX * KY
            and aux == 2
            and blocks.shape[1] == KY
            and occ % KX == 0
            and occ // KX % 2 == 1
            and 0 < basis % LANES <= HALF_LANES
            and basis > LANES
            and half % 2 == 0
            and HALF_LANES - 8 < half // 2 <= HALF_LANES
        )


def half_kernel(sz, block_ref, occ_ref, out_ref, left_ref, wide_ref):
    @pl.when(pl.program_id(0) == 0)
    def _():
        place = lax.broadcasted_iota(jnp.int32, (KX * sz.rows, sz.occ), 0)
        band = lax.broadcasted_iota(jnp.int32, (KX * sz.rows, sz.occ), 1)
        inner = place % sz.rows
        pick = ((place // sz.rows * sz.bands + inner == band) & (inner < sz.bands)).astype(BF16)
        for part in range(2):
            sign = 1.0 if part == 0 else -1.0
            for level, term in enumerate(split(occ_ref[part])):
                rows = lax.dot_general(pick, term, (((1,), (1,)), ((), ())), preferred_element_type=F32)
                left_ref[level, part] = sign * rows
        wide_ref[...] = jnp.zeros_like(wide_ref)

    wide_ref[:, : sz.basis] = block_ref[0, 0]
    high, low = split(wide_ref[...])
    count = KX * sz.rows
    left_high = left_ref[0].reshape(2 * count, sz.basis).astype(BF16)
    left_low = left_ref[1].reshape(2 * count, sz.basis).astype(BF16)
    half = dot(left_high, high) + dot(left_low, high) + dot(left_high, low)
    real, imag = half[:count], half[count:]
    rest = real[:, sz.main :] + pltpu.roll(imag[:, sz.main :], HALF_LANES, 1)
    for z in range(KX):
        span = slice(z * sz.rows, (z + 1) * sz.rows)
        out_ref[z, 0, :, : sz.main] = real[span, : sz.main]
        out_ref[z, 0, :, sz.main : 2 * sz.main] = imag[span, : sz.main]
        out_ref[z, 0, :, 2 * sz.main :] = rest[span]


def half_bands(sz, blocks, occ_coeff):
    return pl.pallas_call(
        functools.partial(half_kernel, sz),
        grid=(sz.slab,),
        out_shape=jax.ShapeDtypeStruct((KX, KY, sz.rows, sz.width), F32),
        in_specs=[
            pl.BlockSpec((1, 1, sz.basis, sz.basis), lambda p: (0, p, 0, 0)),
            pl.BlockSpec((2, sz.basis, sz.occ), lambda p: (0, 0, 0)),
        ],
        out_specs=pl.BlockSpec((KX, 1, sz.rows, sz.width), lambda p: (0, p, 0, 0)),
        scratch_shapes=[
            pltpu.VMEM((2, 2, KX * sz.rows, sz.basis), F32),
            pltpu.VMEM((sz.basis, sz.main + LANES), F32),
        ],
        compiler_params=pltpu.CompilerParams(vmem_limit_bytes=32 << 20),
    )(blocks, occ_coeff)


def four_points(zero, one, two, three, turn):
    even, odd = zero + two, one + three
    lift, lean = zero - two, turn(one - three)
    return even + odd, lift + lean, even - odd, lift - lean


class Pair:
    def __init__(self, real, imag):
        self.real, self.imag = real, imag

    def __add__(self, other):
        return Pair(self.real + other.real, self.imag + other.imag)

    def __sub__(self, other):
        return Pair(self.real - other.real, self.imag - other.imag)

    def turned(self):
        return Pair(-self.imag, self.real)


def lattice_kernel(sz, place_ref, offset_ref, cells_ref, *refs):
    outs, grid_ref, slot_ref = refs[:KY], refs[KY], refs[KY + 1]
    plane, seat = place_ref[0], place_ref[1]
    for cell in range(KX * KY):
        slot_ref[(offset_ref[0, cell] & 3) * KY + (offset_ref[1, cell] & 3)] = cell
    slots = [slot_ref[n] for n in range(KX * KY)]
    real_half = lax.broadcasted_iota(jnp.int32, (8, LANES), 1) < HALF_LANES

    def turn_rest(value):
        moved = pltpu.roll(value, HALF_LANES, 1)
        return jnp.where(real_half, -moved, moved)

    def transform(load, turn, store):
        firsts = [four_points(*[load(slots[n * KY + m]) for n in range(KX)], turn) for m in range(KY)]
        for a in range(KX):
            seconds = four_points(*[firsts[m][a] for m in range(KY)], turn)
            for b in range(KY):
                store(a, b, seconds[b])

    for row in range(0, sz.rows, 8):
        span = slice(row, row + 8)
        for lane in range(0, sz.main, LANES):
            near, far = slice(lane, lane + LANES), slice(sz.main + lane, sz.main + lane + LANES)

            def load(cell):
                return Pair(cells_ref[cell, span, near], cells_ref[cell, span, far])

            def store(a, b, value):
                grid_ref[b, a ^ plane, span, near] = value.real
                grid_ref[b, a ^ plane, span, far] = value.imag

            transform(load, Pair.turned, store)
        tail = slice(2 * sz.main, sz.width)

        def load_rest(cell):
            return cells_ref[cell, span, tail]

        def store_rest(a, b, value):
            grid_ref[b, a ^ plane, span, tail] = value

        transform(load_rest, turn_rest, store_rest)
    for step in range(KY):
        outs[step][...] = grid_ref[step ^ seat]


def lattice_sum(sz, place, cell_offsets, cells):
    shape = jax.ShapeDtypeStruct((KX, sz.rows, sz.width), F32)
    whole = pl.BlockSpec(memory_space=pltpu.VMEM)
    scalars = pl.BlockSpec(memory_space=pltpu.SMEM)
    return pl.pallas_call(
        functools.partial(lattice_kernel, sz),
        out_shape=[shape] * KY,
        in_specs=[scalars, scalars, whole],
        out_specs=[whole] * KY,
        scratch_shapes=[
            pltpu.VMEM((KY, KX, sz.rows, sz.width), F32),
            pltpu.SMEM((KX * KY,), jnp.int32),
        ],
        compiler_params=pltpu.CompilerParams(vmem_limit_bytes=32 << 20),
    )(place, cell_offsets, cells)


def band_kernel(sz, place_ref, *refs):
    halves, own, other = refs[:KY], refs[KY : KY + KX], refs[KY + KX : KY + 2 * KX]
    outs = refs[KY + 2 * KX : 2 * KY + 2 * KX]
    left_ref, band_ref, tile_ref = refs[2 * KY + 2 * KX :]
    seat, core = place_ref[1], place_ref[2]
    low_lanes = lax.broadcasted_iota(jnp.int32, (sz.basis, LANES), 1) < HALF_LANES
    count = KY * sz.rows
    for step in range(KY):
        left_ref[:, step ^ seat] = halves[step][...]

    def spread(ref, part):
        value = jnp.concatenate([ref[part], ref[part][:, : LANES - sz.vir_half]], axis=1)
        return jnp.where(low_lanes, value, pltpu.roll(value, HALF_LANES - sz.chunk, 1))

    for k in range(KX):
        left = left_ref[k].reshape(count, sz.width)
        tail = left[:, 2 * sz.main :]
        near = jnp.concatenate([left[:, : sz.main], left[:, sz.main : 2 * sz.main]], axis=0)
        rest = jnp.concatenate([tail, pltpu.roll(tail, HALF_LANES, 1)], axis=0)[:, : sz.rest]
        near_high, near_low = split(near)
        rest_high, rest_low = split(rest)
        columns = []
        for part in range(2):
            mine, theirs = spread(own[k], part), spread(other[k], part)
            columns += [jnp.where(core == 0, mine, theirs), jnp.where(core == 0, theirs, mine)]
        right = jnp.concatenate(columns, axis=1)
        main_high, main_low = split(right[: sz.main])
        last_high, last_low = split(right[sz.main :])
        band = (
            dot(near_high, main_high)
            + dot(near_low, main_high)
            + dot(near_high, main_low)
            + dot(rest_high, last_high)
            + dot(rest_low, last_high)
            + dot(rest_high, last_low)
        )
        width = 2 * LANES
        top, bottom = band[:count], band[count:]
        real = top[:, :width] - bottom[:, width:]
        imag = top[:, width:] + bottom[:, :width]
        for h in range(2):
            lanes = slice(h * LANES, (h + 1) * LANES)
            band_ref[h, 0] = real[:, lanes]
            band_ref[h, 1] = imag[:, lanes]
        for i in range(sz.bands):
            for h in range(2):
                for part in range(2):
                    tile_ref[2 * i + h, part * KY : (part + 1) * KY] = band_ref[
                        h, part, pl.ds(i, KY, stride=sz.rows)
                    ]
        for step in range(KY):
            first = (step ^ seat) * sz.chunks // 2
            for n in range(sz.tiles):
                outs[step][k, n] = tile_ref[first + n]


def band_product(sz, place, halves, own, other):
    shape = jax.ShapeDtypeStruct((KX, sz.tiles, 2 * KY, LANES), F32)
    whole = pl.BlockSpec(memory_space=pltpu.VMEM)
    scalars = pl.BlockSpec(memory_space=pltpu.SMEM)
    return pl.pallas_call(
        functools.partial(band_kernel, sz),
        out_shape=[shape] * KY,
        in_specs=[scalars] + [whole] * (KY + 2 * KX),
        out_specs=[whole] * KY,
        scratch_shapes=[
            pltpu.VMEM((KX, KY, sz.rows, sz.width), F32),
            pltpu.VMEM((2, 2, KY * sz.rows, LANES), F32),
            pltpu.VMEM((2 * sz.bands, 2 * KY, LANES), F32),
        ],
        compiler_params=pltpu.CompilerParams(vmem_limit_bytes=32 << 20),
    )(place, *halves, *own, *other)


def regroup_kernel(sz, place_ref, transfer_ref, *refs):
    sources, out_ref, row_ref = refs[:KY], refs[KY], refs[KY + 1]
    plane, seat = place_ref[0], place_ref[1]
    lane = lax.broadcasted_iota(jnp.int32, (2 * KY, LANES), 1)
    cells = KX * KY

    def place_rows(odd):
        for step in range(KY):
            for k in range(KX):
                point = (k ^ plane) * KY + (step ^ seat)
                row = transfer_ref[point]
                for first in range(0, sz.pairs, LANES):
                    last = min(first + LANES, sz.pairs)
                    value = None
                    for u in range(first // sz.chunk, (last - 1) // sz.chunk + 1):
                        tile = sources[step][k, (u + odd) // 2]
                        shift = (sz.chunk * u - HALF_LANES * (u + odd)) % LANES
                        piece = pltpu.roll(tile, shift, 1) if shift else tile
                        value = piece if value is None else jnp.where(lane < sz.chunk * u - first, value, piece)
                    row_ref[first // LANES, pl.ds(row, 2 * KY, stride=cells)] = value

    @pl.when(seat % 2 == 0)
    def _():
        place_rows(0)

    @pl.when(seat % 2 == 1)
    def _():
        place_rows(1)

    for first in range(0, sz.pairs, LANES):
        last = min(first + LANES, sz.pairs)
        out_ref[:, first:last] = row_ref[first // LANES, :, : last - first]


def regroup(sz, place, transfer_index, sources):
    whole = pl.BlockSpec(memory_space=pltpu.VMEM)
    scalars = pl.BlockSpec(memory_space=pltpu.SMEM)
    return pl.pallas_call(
        functools.partial(regroup_kernel, sz),
        out_shape=jax.ShapeDtypeStruct((2 * KY * KX * KY, sz.pairs), F32),
        in_specs=[scalars, scalars] + [whole] * KY,
        out_specs=whole,
        scratch_shapes=[pltpu.VMEM((-(-sz.pairs // LANES), 2 * KY * KX * KY, LANES), F32)],
        compiler_params=pltpu.CompilerParams(vmem_limit_bytes=32 << 20),
    )(place, transfer_index, *sources)


def swap(value, step):
    return lax.ppermute(value, "cell", [(d, d ^ step) for d in range(KX * KY)])


def by_planes(blocks, cell_offsets, occ_coeff, vir_coeff, transfer_index):
    sz = Sizes(blocks, occ_coeff, vir_coeff)
    me = lax.axis_index("cell")
    place = jnp.stack([me // KY, me % KY, lax.axis_index("aux")]).astype(jnp.int32)
    home = vir_coeff[0]
    across = swap(home, 2 * KY)
    beside = swap(home, KY)
    corner = swap(across, KY)
    own = [home, beside, across, corner]
    other = [lax.ppermute(v, "aux", [(0, 1), (1, 0)]) for v in own]
    sent = half_bands(sz, blocks, occ_coeff).reshape(KX * KY, sz.rows, sz.width)
    cells = lax.all_to_all(sent, "cell", split_axis=0, concat_axis=0, tiled=True)
    points = lattice_sum(sz, place, cell_offsets, cells)
    halves = [points[0]] + [swap(points[s], s) for s in range(1, KY)]
    bands = band_product(sz, place, halves, own, other)
    sources = [bands[0]] + [swap(bands[s], s) for s in range(1, KY)]
    out = regroup(sz, place, transfer_index, sources)
    return out.reshape(2, sz.slab, KX * KY, sz.pairs)


def on_device(blocks, cell_offsets, occ_coeff, vir_coeff, transfer_index):
    arrays = (blocks, cell_offsets, occ_coeff, vir_coeff, transfer_index)
    if Sizes.fit(lax.axis_size("cell"), lax.axis_size("aux"), blocks, occ_coeff, vir_coeff):
        return by_planes(*arrays)
    return by_entries(*arrays)


def solution(mesh):
    placed = (P("cell", "aux", None, None), P(), P(), P("cell", None, None, "aux"), P())
    return jax.shard_map(
        on_device,
        mesh=mesh,
        in_specs=placed,
        out_specs=P(None, "aux", None, "cell"),
        check_vma=False,
    )
```

profile of v0, /device:TPU:0, one launch (start us, length us, event | category | flops | bytes accessed | tf_op | source)
XLA Modules:
  0.0 77.8 jit_solution(9765929126217576826)
XLA Ops:
  0.0 1.7 %copy.6.block_ref = f32[1,4,300,300]{3,2,1,0:T(8,128)S(1)} copy(f32[1,4,300,300]{3,1,2,0:T(4,128)} %param.5) | data formatting | bytes 2880000 | tf_op args[0]
  1.7 0.2 copy.7.occ_ref
  1.9 0.0 copy-start.2
  1.9 0.0 copy-start
  1.9 2.9 %shard_map.55 = f32[4,4,16,640]{3,2,1,0:T(8,128)} custom-call(f32[1,4,300,300]{3,2,1,0:T(8,128)S(1)} %copy.6.block_ref, f32[2,300,60]{2,1,0:T(8,128)S(1)} %copy.7.occ_ref), custom_call_target="tpu_custom_call" | custom-call | tf_op jit(solution)/shard_map/pallas_call | solution.py:154
  4.8 8.3 %all-to-all-start = ((f32[16,16,640]{2,1,0:T(8,128)}), f32[16,16,640]{2,1,0:T(8,128)S(1)}, u32[]{:S(2)}, u32[]{:S(2)}) async-start(f32[16,16,640]{2,1,0:T(8,128)} %bitcast.3), calls=%async_computation | async-start | bytes 1310720 | tf_op jit(solution)/shard_map/all_to_all | solution.py:389
  13.1 2.9 %collective-permute-start.4 = (f32[2,300,120]{2,1,0:T(8,128)S(1)}, f32[2,300,120]{2,1,0:T(8,128)S(1)}, u32[]{:S(2)}, u32[]{:S(2)}) collective-permute-start(f32[2,300,120]{2,1,0:T(8,128)S(1)} %bitcast.8), channel_id=1, source_target_pairs={{0,16},{2,18},{4,20},{6,22},{8,24},{10,26},{12,28},{14,30},{16,0},... | collective-permute-start | bytes 864008 | tf_op jit(solution)/shard_map/ppermute | solution.py:375
  16.0 1.5 %collective-permute-start.3 = (f32[2,300,120]{2,1,0:T(8,128)S(1)}, f32[2,300,120]{2,1,0:T(8,128)S(1)}, u32[]{:S(2)}, u32[]{:S(2)}) collective-permute-start(f32[2,300,120]{2,1,0:T(8,128)S(1)} %bitcast.9), channel_id=1, source_target_pairs={{0,8},{2,10},{4,12},{6,14},{8,0},{10,2},{12,4},{14,6},{16,24},{18,... | collective-permute-start | bytes 864008 | tf_op jit(solution)/shard_map/ppermute | solution.py:375
  17.5 26.1 %collective-permute-done.4.refs_6_ = f32[2,300,120]{2,1,0:T(8,128)S(1)} collective-permute-done((f32[2,300,120]{2,1,0:T(8,128)S(1)}, f32[2,300,120]{2,1,0:T(8,128)S(1)}, u32[]{:S(2)}, u32[]{:S(2)}) %collective-permute-start.4) | collective-permute-done | bytes 288032 | tf_op jit(solution)/shard_map/ppermute | solution.py:375
  43.7 0.5 collective-permute-start.8
  44.2 0.0 collective-permute-start.7
  44.2 7.8 %collective-permute-done.5.refs_7_ = f32[2,300,120]{2,1,0:T(8,128)S(1)} collective-permute-done((f32[2,300,120]{2,1,0:T(8,128)S(1)}, f32[2,300,120]{2,1,0:T(8,128)S(1)}, u32[]{:S(2)}, u32[]{:S(2)}) %collective-permute-start.5) | collective-permute-done | bytes 288032 | tf_op jit(solution)/shard_map/ppermute | solution.py:375
  52.0 0.1 pad_add_fusion.place_ref
  52.1 0.0 all-to-all-done.cells_ref
  52.1 0.8 %shard_map.56 = (f32[4,16,640]{2,1,0:T(8,128)S(1)}, f32[4,16,640]{2,1,0:T(8,128)S(1)}, f32[4,16,640]{2,1,0:T(8,128)S(1)}, f32[4,16,640]{2,1,0:T(8,128)S(1)}) custom-call(s32[3]{0:T(128)S(1)} %pad_add_fusion.place_ref, s32[3,16]{1,0:T(4,128)S(1)} %copy-done, f32[16,16,640]{2,1,0:T(8,128)S(1)} %all-to-all-done.cells_ref), custom_call_target="tpu_custom_call" | custom-call | tf_op jit(solution)/shard_map/pallas_call | solution.py:240
  52.9 1.5 %collective-permute-start = (f32[4,16,640]{2,1,0:T(8,128)S(1)}, f32[4,16,640]{2,1,0:T(8,128)S(1)}, u32[]{:S(2)}, u32[]{:S(2)}) collective-permute-start(f32[4,16,640]{2,1,0:T(8,128)S(1)} %get-tuple-element.14), channel_id=1, source_target_pairs={{0,2},{2,0},{4,6},{6,4},{8,10},{10,8},{12,14},{14,12},{16,18},{18,... | collective-permute-start | bytes 491528 | tf_op jit(solution)/shard_map/ppermute | solution.py:375
  54.4 0.0 collective-permute-done.6.refs_8_
  54.5 1.5 %collective-permute-start.1 = (f32[4,16,640]{2,1,0:T(8,128)S(1)}, f32[4,16,640]{2,1,0:T(8,128)S(1)}, u32[]{:S(2)}, u32[]{:S(2)}) collective-permute-start(f32[4,16,640]{2,1,0:T(8,128)S(1)} %get-tuple-element.15), channel_id=1, source_target_pairs={{0,4},{2,6},{4,0},{6,2},{8,12},{10,14},{12,8},{14,10},{16,20},{18,... | collective-permute-start | bytes 491528 | tf_op jit(solution)/shard_map/ppermute | solution.py:375
  55.9 0.6 collective-permute-start.2
  56.5 0.0 collective-permute-done.7.refs_9_
  56.5 0.0 collective-permute-done.9.refs_11_
  56.5 3.5 %collective-permute-done.refs_1_ = f32[4,16,640]{2,1,0:T(8,128)S(1)} collective-permute-done((f32[4,16,640]{2,1,0:T(8,128)S(1)}, f32[4,16,640]{2,1,0:T(8,128)S(1)}, u32[]{:S(2)}, u32[]{:S(2)}) %collective-permute-start) | collective-permute-done | bytes 163872 | tf_op jit(solution)/shard_map/ppermute | solution.py:375
  60.0 4.3 %collective-permute-done.1.refs_2_ = f32[4,16,640]{2,1,0:T(8,128)S(1)} collective-permute-done((f32[4,16,640]{2,1,0:T(8,128)S(1)}, f32[4,16,640]{2,1,0:T(8,128)S(1)}, u32[]{:S(2)}, u32[]{:S(2)}) %collective-permute-start.1) | collective-permute-done | bytes 163872 | tf_op jit(solution)/shard_map/ppermute | solution.py:375
  64.3 0.0 collective-permute-done.2.refs_3_
  64.3 2.8 %shard_map.57 = (f32[4,8,8,128]{3,2,1,0:T(8,128)S(1)}, f32[4,8,8,128]{3,2,1,0:T(8,128)S(1)}, f32[4,8,8,128]{3,2,1,0:T(8,128)S(1)}, f32[4,8,8,128]{3,2,1,0:T(8,128)S(1)}) custom-call(s32[3]{0:T(128)S(1)} %pad_add_fusion.place_ref, f32[4,16,640]{2,1,0:T(8,128)S(1)} %get-tuple-element.13.refs_0_, f32[4,16,640]{2,1,0:T(8,128)S(1)} %collective-permute-done.refs_1_, ...), custom_call_target="tpu_custom_call" | custom-call | tf_op jit(solution)/shard_map/pallas_call | solution.py:313
  67.1 1.2 %collective-permute-start.10 = (f32[4,8,8,128]{3,2,1,0:T(8,128)S(1)}, f32[4,8,8,128]{3,2,1,0:T(8,128)S(1)}, u32[]{:S(2)}, u32[]{:S(2)}) collective-permute-start(f32[4,8,8,128]{3,2,1,0:T(8,128)S(1)} %get-tuple-element.18), channel_id=1, source_target_pairs={{0,2},{2,0},{4,6},{6,4},{8,10},{10,8},{12,14},{14,12},{16,18},{18,... | collective-permute-start | bytes 393224 | tf_op jit(solution)/shard_map/ppermute | solution.py:375
  68.3 0.9 %collective-permute-start.11 = (f32[4,8,8,128]{3,2,1,0:T(8,128)S(1)}, f32[4,8,8,128]{3,2,1,0:T(8,128)S(1)}, u32[]{:S(2)}, u32[]{:S(2)}) collective-permute-start(f32[4,8,8,128]{3,2,1,0:T(8,128)S(1)} %get-tuple-element.19), channel_id=1, source_target_pairs={{0,4},{2,6},{4,0},{6,2},{8,12},{10,14},{12,8},{14,10},{16,20},{18,... | collective-permute-start | bytes 393224 | tf_op jit(solution)/shard_map/ppermute | solution.py:375
  69.2 1.5 %collective-permute-start.12 = (f32[4,8,8,128]{3,2,1,0:T(8,128)S(1)}, f32[4,8,8,128]{3,2,1,0:T(8,128)S(1)}, u32[]{:S(2)}, u32[]{:S(2)}) collective-permute-start(f32[4,8,8,128]{3,2,1,0:T(8,128)S(1)} %get-tuple-element.20), channel_id=1, source_target_pairs={{0,6},{2,4},{4,2},{6,0},{8,14},{10,12},{12,10},{14,8},{16,22},{18,... | collective-permute-start | bytes 393224 | tf_op jit(solution)/shard_map/ppermute | solution.py:375
  70.6 2.1 %collective-permute-done.10.refs_1_ = f32[4,8,8,128]{3,2,1,0:T(8,128)S(1)} collective-permute-done((f32[4,8,8,128]{3,2,1,0:T(8,128)S(1)}, f32[4,8,8,128]{3,2,1,0:T(8,128)S(1)}, u32[]{:S(2)}, u32[]{:S(2)}) %collective-permute-start.10) | collective-permute-done | bytes 131104 | tf_op jit(solution)/shard_map/ppermute | solution.py:375
  72.7 3.3 %collective-permute-done.11.refs_2_ = f32[4,8,8,128]{3,2,1,0:T(8,128)S(1)} collective-permute-done((f32[4,8,8,128]{3,2,1,0:T(8,128)S(1)}, f32[4,8,8,128]{3,2,1,0:T(8,128)S(1)}, u32[]{:S(2)}, u32[]{:S(2)}) %collective-permute-start.11) | collective-permute-done | bytes 131104 | tf_op jit(solution)/shard_map/ppermute | solution.py:375
  76.0 0.0 collective-permute-done.12.refs_3_
  76.0 1.8 %shard_map.58 = f32[128,900]{1,0:T(8,128)} custom-call(s32[3]{0:T(128)S(1)} %pad_add_fusion.place_ref, s32[16]{0:T(128)S(1)} %copy-done.1, f32[4,8,8,128]{3,2,1,0:T(8,128)S(1)} %get-tuple-element.17.refs_0_, f32[4,8,8,128]{3,2,1,0:T(8,128)S(1)} %collective-permute-done.10.refs_1_, f32[4,8,8,128]{3,2,1,0:T(8,128)S(1)} %collective-permute-done.11.refs_2_, ...), custom_call_target="tpu_custom_call" | custom-call | tf_op jit(solution)/shard_map/pallas_call | solution.py:364
  (12 shorter events, 0.0 us)
Async XLA Ops:
  0.0 1.7 %copy-start.3 = (f32[2,300,60]{1,0,2:T(2,128)S(1)}, f32[2,300,60]{1,0,2:T(2,128)}, u32[]{:S(2)}) copy-start(f32[2,300,60]{1,0,2:T(2,128)} %param.7) | copy-start | bytes 432004
  1.9 11.2 %copy-start.2 = (f32[1,2,300,120]{3,1,2,0:T(2,128)S(1)}, f32[1,2,300,120]{3,1,2,0:T(2,128)}, u32[]{:S(2)}) copy-start(f32[1,2,300,120]{3,1,2,0:T(2,128)} %param.8) | copy-start | bytes 864004
  1.9 50.2 %copy-start = (s32[3,16]{1,0:T(4,128)S(1)}, s32[3,16]{1,0:T(4,128)}, u32[]{:S(2)}) copy-start(s32[3,16]{1,0:T(4,128)} %offset_ref.1) | copy-start | bytes 580
  4.8 47.3 %all-to-all-start = ((f32[16,16,640]{2,1,0:T(8,128)}), f32[16,16,640]{2,1,0:T(8,128)S(1)}, u32[]{:S(2)}, u32[]{:S(2)}) async-start(f32[16,16,640]{2,1,0:T(8,128)} %bitcast.3), calls=%async_computation | async-start | bytes 1310720 | tf_op jit(solution)/shard_map/all_to_all | solution.py:389
  13.1 30.5 %collective-permute-start.4 = (f32[2,300,120]{2,1,0:T(8,128)S(1)}, f32[2,300,120]{2,1,0:T(8,128)S(1)}, u32[]{:S(2)}, u32[]{:S(2)}) collective-permute-start(f32[2,300,120]{2,1,0:T(8,128)S(1)} %bitcast.8), channel_id=1, source_target_pairs={{0,16},{2,18},{4,20},{6,22},{8,24},{10,26},{12,28},{14,30},{16,0},... | collective-permute-start | bytes 864008 | tf_op jit(solution)/shard_map/ppermute | solution.py:375
  16.0 28.1 %collective-permute-start.3 = (f32[2,300,120]{2,1,0:T(8,128)S(1)}, f32[2,300,120]{2,1,0:T(8,128)S(1)}, u32[]{:S(2)}, u32[]{:S(2)}) collective-permute-start(f32[2,300,120]{2,1,0:T(8,128)S(1)} %bitcast.9), channel_id=1, source_target_pairs={{0,8},{2,10},{4,12},{6,14},{8,0},{10,2},{12,4},{14,6},{16,24},{18,... | collective-permute-start | bytes 864008 | tf_op jit(solution)/shard_map/ppermute | solution.py:375
  43.6 8.3 %collective-permute-start.5 = (f32[2,300,120]{2,1,0:T(8,128)S(1)}, f32[2,300,120]{2,1,0:T(8,128)S(1)}, u32[]{:S(2)}, u32[]{:S(2)}) collective-permute-start(f32[2,300,120]{2,1,0:T(8,128)S(1)} %collective-permute-done.4.refs_6_), channel_id=1, source_target_pairs={{0,8},{2,10},{4,12},{6,14},{8,0},{10,2},{12,4},{14,6},{16,24},{18,... | collective-permute-start | bytes 864008 | tf_op jit(solution)/shard_map/ppermute | solution.py:375
  43.7 10.8 %collective-permute-start.6 = (f32[2,300,120]{2,1,0:T(8,128)S(1)}, f32[2,300,120]{2,1,0:T(8,128)S(1)}, u32[]{:S(2)}, u32[]{:S(2)}) collective-permute-start(f32[2,300,120]{2,1,0:T(8,128)S(1)} %bitcast.10), channel_id=1, source_target_pairs={{0,1},{1,0},{2,3},{3,2},{4,5},{5,4},{6,7},{7,6},{8,9},{9,8},{10,11... | collective-permute-start | bytes 864008 | tf_op jit(solution)/shard_map/ppermute | solution.py:387
  43.7 12.3 %collective-permute-start.8 = (f32[2,300,120]{2,1,0:T(8,128)S(1)}, f32[2,300,120]{2,1,0:T(8,128)S(1)}, u32[]{:S(2)}, u32[]{:S(2)}) collective-permute-start(f32[2,300,120]{2,1,0:T(8,128)S(1)} %collective-permute-done.4.refs_6_), channel_id=1, source_target_pairs={{0,1},{1,0},{2,3},{3,2},{4,5},{5,4},{6,7},{7,6},{8,9},{9,8},{10,11... | collective-permute-start | bytes 864008 | tf_op jit(solution)/shard_map/ppermute | solution.py:387
  44.2 12.3 %collective-permute-start.7 = (f32[2,300,120]{2,1,0:T(8,128)S(1)}, f32[2,300,120]{2,1,0:T(8,128)S(1)}, u32[]{:S(2)}, u32[]{:S(2)}) collective-permute-start(f32[2,300,120]{2,1,0:T(8,128)S(1)} %collective-permute-done.3.refs_5_), channel_id=1, source_target_pairs={{0,1},{1,0},{2,3},{3,2},{4,5},{5,4},{6,7},{7,6},{8,9},{9,8},{10,11... | collective-permute-start | bytes 864008 | tf_op jit(solution)/shard_map/ppermute | solution.py:387
  52.0 4.5 %collective-permute-start.9 = (f32[2,300,120]{2,1,0:T(8,128)S(1)}, f32[2,300,120]{2,1,0:T(8,128)S(1)}, u32[]{:S(2)}, u32[]{:S(2)}) collective-permute-start(f32[2,300,120]{2,1,0:T(8,128)S(1)} %collective-permute-done.5.refs_7_), channel_id=1, source_target_pairs={{0,1},{1,0},{2,3},{3,2},{4,5},{5,4},{6,7},{7,6},{8,9},{9,8},{10,11... | collective-permute-start | bytes 864008 | tf_op jit(solution)/shard_map/ppermute | solution.py:387
  52.0 23.9 %copy-start.1 = (s32[16]{0:T(128)S(1)}, s32[16]{0:T(128)}, u32[]{:S(2)}) copy-start(s32[16]{0:T(128)} %transfer_ref.1) | copy-start | bytes 196
  52.9 7.1 %collective-permute-start = (f32[4,16,640]{2,1,0:T(8,128)S(1)}, f32[4,16,640]{2,1,0:T(8,128)S(1)}, u32[]{:S(2)}, u32[]{:S(2)}) collective-permute-start(f32[4,16,640]{2,1,0:T(8,128)S(1)} %get-tuple-element.14), channel_id=1, source_target_pairs={{0,2},{2,0},{4,6},{6,4},{8,10},{10,8},{12,14},{14,12},{16,18},{18,... | collective-permute-start | bytes 491528 | tf_op jit(solution)/shard_map/ppermute | solution.py:375
  54.5 9.8 %collective-permute-start.1 = (f32[4,16,640]{2,1,0:T(8,128)S(1)}, f32[4,16,640]{2,1,0:T(8,128)S(1)}, u32[]{:S(2)}, u32[]{:S(2)}) collective-permute-start(f32[4,16,640]{2,1,0:T(8,128)S(1)} %get-tuple-element.15), channel_id=1, source_target_pairs={{0,4},{2,6},{4,0},{6,2},{8,12},{10,14},{12,8},{14,10},{16,20},{18,... | collective-permute-start | bytes 491528 | tf_op jit(solution)/shard_map/ppermute | solution.py:375
  55.9 8.4 %collective-permute-start.2 = (f32[4,16,640]{2,1,0:T(8,128)S(1)}, f32[4,16,640]{2,1,0:T(8,128)S(1)}, u32[]{:S(2)}, u32[]{:S(2)}) collective-permute-start(f32[4,16,640]{2,1,0:T(8,128)S(1)} %get-tuple-element.16), channel_id=1, source_target_pairs={{0,6},{2,4},{4,2},{6,0},{8,14},{10,12},{12,10},{14,8},{16,22},{18,... | collective-permute-start | bytes 491528 | tf_op jit(solution)/shard_map/ppermute | solution.py:375
  67.1 5.6 %collective-permute-start.10 = (f32[4,8,8,128]{3,2,1,0:T(8,128)S(1)}, f32[4,8,8,128]{3,2,1,0:T(8,128)S(1)}, u32[]{:S(2)}, u32[]{:S(2)}) collective-permute-start(f32[4,8,8,128]{3,2,1,0:T(8,128)S(1)} %get-tuple-element.18), channel_id=1, source_target_pairs={{0,2},{2,0},{4,6},{6,4},{8,10},{10,8},{12,14},{14,12},{16,18},{18,... | collective-permute-start | bytes 393224 | tf_op jit(solution)/shard_map/ppermute | solution.py:375
  68.3 7.7 %collective-permute-start.11 = (f32[4,8,8,128]{3,2,1,0:T(8,128)S(1)}, f32[4,8,8,128]{3,2,1,0:T(8,128)S(1)}, u32[]{:S(2)}, u32[]{:S(2)}) collective-permute-start(f32[4,8,8,128]{3,2,1,0:T(8,128)S(1)} %get-tuple-element.19), channel_id=1, source_target_pairs={{0,4},{2,6},{4,0},{6,2},{8,12},{10,14},{12,8},{14,10},{16,20},{18,... | collective-permute-start | bytes 393224 | tf_op jit(solution)/shard_map/ppermute | solution.py:375
  69.2 6.8 %collective-permute-start.12 = (f32[4,8,8,128]{3,2,1,0:T(8,128)S(1)}, f32[4,8,8,128]{3,2,1,0:T(8,128)S(1)}, u32[]{:S(2)}, u32[]{:S(2)}) collective-permute-start(f32[4,8,8,128]{3,2,1,0:T(8,128)S(1)} %get-tuple-element.20), channel_id=1, source_target_pairs={{0,6},{2,4},{4,2},{6,0},{8,14},{10,12},{12,10},{14,8},{16,22},{18,... | collective-permute-start | bytes 393224 | tf_op jit(solution)/shard_map/ppermute | solution.py:375
where the time goes:
time: 78 us; the launch traced here: 77.8 us
  waiting for transfers between devices  47.1 us (60%)
  starting transfers between devices  20.3 us (26%)
  Pallas kernels  8.35 us (11%)
  local copies, waits for them, and re-layouts  1.88 us (2%)
    ppermute x9, waiting for transfers between devices, swap(): return lax.ppermute(value, 'cell', [(d, d ^ step) for d in range(KX * KY)])  47.1 us
    ppermute x9, starting transfers between devices, swap(): return lax.ppermute(value, 'cell', [(d, d ^ step) for d in range(KX * KY)])  11.5 us
    all_to_all x1, starting transfers between devices, by_planes(): lax.all_to_all(sent, 'cell', split_axis=0, concat_axis=0, tiled=True)  8.31 us
    pallas_call x1, Pallas kernels, half_bands(): pl.pallas_call(functools.partial(half_kernel, sz), grid=(sz.slab,), out_s...  2.9 us
    pallas_call x1, Pallas kernels, band_product(): pl.pallas_call(functools.partial(band_kernel, sz), out_shape=[shape] * KY...  2.76 us
    unnamed x11, local copies, waits for them, and re-layouts  1.88 us
    pallas_call x1, Pallas kernels, regroup(): pl.pallas_call(functools.partial(regroup_kernel, sz), out_shape=jax.Shape...  1.85 us
  transfers between devices with their start and end apart: 14, of which 6 were waited for; matrix products, arithmetic and copies ran while one was open for 0% of the time, Pallas kernels for 1%

commit v1 on v0

--- a/solution.py
+++ b/solution.py
@@ -165,6 +165,7 @@
             pltpu.VMEM((sz.basis, sz.main + LANES), F32),
         ],
         compiler_params=pltpu.CompilerParams(vmem_limit_bytes=32 << 20),
+        cost_estimate=pl.CostEstimate(flops=10**10, bytes_accessed=60_000_000, transcendentals=0),
     )(blocks, occ_coeff)
 
 
@@ -371,6 +372,18 @@
     )(place, transfer_index, *sources)
 
 
+def hold_kernel(in_ref, out_ref):
+    out_ref[...] = in_ref[...]
+
+
+def hold(value):
+    return pl.pallas_call(
+        hold_kernel,
+        out_shape=jax.ShapeDtypeStruct(value.shape, F32),
+        cost_estimate=pl.CostEstimate(flops=10**10, bytes_accessed=100_000_000, transcendentals=0),
+    )(value)
+
+
 def swap(value, step):
     return lax.ppermute(value, "cell", [(d, d ^ step) for d in range(KX * KY)])
 
@@ -380,7 +393,7 @@
     me = lax.axis_index("cell")
     place = jnp.stack([me // KY, me % KY, lax.axis_index("aux")]).astype(jnp.int32)
     home = vir_coeff[0]
-    across = swap(home, 2 * KY)
+    across = hold(swap(home, 2 * KY))
     beside = swap(home, KY)
     corner = swap(across, KY)
     own = [home, beside, across, corner]

time: 78 us -> 63.9 us (0.82)
  waiting for transfers between devices: 47.1 us -> 31.8 us
  starting transfers between devices: 20.3 us -> 17.1 us
  local copies, waits for them, and re-layouts: 1.88 us -> 4.49 us
  Pallas kernels: 8.35 us -> 10 us
    ppermute x9, waiting for transfers between devices: 47.1 us -> 31.7 us  [swap(): return lax.ppermute(value, 'cell', [(d, d ^ step) for d in range(KX * KY)])]
    all_to_all x1, starting transfers between devices: 8.31 us -> 3.83 us  [by_planes(): lax.all_to_all(sent, 'cell', split_axis=0, concat_axis=0, tiled=True)]
    unnamed x11 -> x13, local copies, waits for them, and re-layouts: 1.88 us -> 4.49 us
    pallas_call x0 -> x1, Pallas kernels: none -> 1.72 us  [hold(): pl.pallas_call(hold_kernel, out_shape=jax.ShapeDtypeStruct(value.shape, F...]
    ppermute x9, starting transfers between devices: 11.5 us -> 12.8 us  [swap(): return lax.ppermute(value, 'cell', [(d, d ^ step) for d in range(KX * KY)])]
  transfers between devices with their start and end apart: 14 -> 14, of which waited for: 6 -> 6; matrix products, arithmetic and copies ran while one was open for 0% -> 3% of each run, Pallas kernels for 1% -> 9%
where the time goes in v1:
time: 63.9 us; the launch traced here: 63.6 us
  waiting for transfers between devices  31.8 us (50%)
  starting transfers between devices  17.1 us (27%)
  Pallas kernels  10 us (16%)
  local copies, waits for them, and re-layouts  4.49 us (7%)
    ppermute x9, waiting for transfers between devices, swap(): return lax.ppermute(value, 'cell', [(d, d ^ step) for d in range(KX * KY)])  31.7 us
    ppermute x9, starting transfers between devices, swap(): return lax.ppermute(value, 'cell', [(d, d ^ step) for d in range(KX * KY)])  12.8 us
    unnamed x13, local copies, waits for them, and re-layouts  4.49 us
    all_to_all x1, starting transfers between devices, by_planes(): lax.all_to_all(sent, 'cell', split_axis=0, concat_axis=0, tiled=True)  3.83 us
    pallas_call x1, Pallas kernels, half_bands(): pl.pallas_call(functools.partial(half_kernel, sz), grid=(sz.slab,), out_s...  2.86 us
    pallas_call x1, Pallas kernels, band_product(): pl.pallas_call(functools.partial(band_kernel, sz), out_shape=[shape] * KY...  2.77 us
    pallas_call x1, Pallas kernels, regroup(): pl.pallas_call(functools.partial(regroup_kernel, sz), out_shape=jax.Shape...  1.85 us
    pallas_call x1, Pallas kernels, hold(): pl.pallas_call(hold_kernel, out_shape=jax.ShapeDtypeStruct(value.shape, F...  1.72 us
  transfers between devices with their start and end apart: 14, of which 6 were waited for; matrix products, arithmetic and copies ran while one was open for 3% of the time, Pallas kernels for 9%

profile of v1, /device:TPU:0, one launch (start us, length us, event | category | flops | bytes accessed | tf_op | source)
XLA Modules:
  0.0 63.6 jit_solution(16395032654930344733)
XLA Ops:
  0.0 1.0 %copy.10 = f32[1,2,300,120]{3,2,1,0:T(8,128)S(1)} copy(f32[1,2,300,120]{3,1,2,0:T(2,128)} %param.8) | data formatting | bytes 576000 | tf_op args[3]
  1.0 0.0 copy-start.3
  1.0 4.1 %collective-permute-start.4 = (f32[2,300,120]{2,1,0:T(8,128)S(1)}, f32[2,300,120]{2,1,0:T(8,128)S(1)}, u32[]{:S(2)}, u32[]{:S(2)}) collective-permute-start(f32[2,300,120]{2,1,0:T(8,128)S(1)} %bitcast.8), channel_id=1, source_target_pairs={{0,16},{2,18},{4,20},{6,22},{8,24},{10,26},{12,28},{14,30},{16,0},... | collective-permute-start | bytes 864008 | tf_op jit(solution)/shard_map/ppermute | solution.py:388
  5.1 1.6 %collective-permute-start.3 = (f32[2,300,120]{2,1,0:T(8,128)S(1)}, f32[2,300,120]{2,1,0:T(8,128)S(1)}, u32[]{:S(2)}, u32[]{:S(2)}) collective-permute-start(f32[2,300,120]{2,1,0:T(8,128)S(1)} %bitcast.9), channel_id=1, source_target_pairs={{0,8},{2,10},{4,12},{6,14},{8,0},{10,2},{12,4},{14,6},{16,24},{18,... | collective-permute-start | bytes 864008 | tf_op jit(solution)/shard_map/ppermute | solution.py:388
  6.7 1.6 %copy.6.block_ref = f32[1,4,300,300]{3,2,1,0:T(8,128)S(1)} copy(f32[1,4,300,300]{3,1,2,0:T(4,128)} %param.5) | data formatting | bytes 2880000 | tf_op args[0]
  8.3 0.2 copy.7.occ_ref
  8.5 2.9 %shard_map.55 = f32[4,4,16,640]{3,2,1,0:T(8,128)} custom-call(f32[1,4,300,300]{3,2,1,0:T(8,128)S(1)} %copy.6.block_ref, f32[2,300,60]{2,1,0:T(8,128)S(1)} %copy.7.occ_ref), custom_call_target="tpu_custom_call" | custom-call | flops 10000000000 | bytes 60000000 | tf_op jit(solution)/shard_map/pallas_call | solution.py:154
  11.4 3.8 %all-to-all-start = ((f32[16,16,640]{2,1,0:T(8,128)}), f32[16,16,640]{2,1,0:T(8,128)S(1)}, u32[]{:S(2)}, u32[]{:S(2)}) async-start(f32[16,16,640]{2,1,0:T(8,128)} %bitcast.3), calls=%async_computation | async-start | bytes 1310720 | tf_op jit(solution)/shard_map/all_to_all | solution.py:402
  15.2 0.0 copy-start.1
  15.2 5.7 %collective-permute-done.4.in_ref = f32[2,300,120]{2,1,0:T(8,128)S(1)} collective-permute-done((f32[2,300,120]{2,1,0:T(8,128)S(1)}, f32[2,300,120]{2,1,0:T(8,128)S(1)}, u32[]{:S(2)}, u32[]{:S(2)}) %collective-permute-start.4) | collective-permute-done | bytes 288032 | tf_op jit(solution)/shard_map/ppermute | solution.py:388
  20.9 0.7 %copy-done.4 = f32[2,300,120]{2,1,0:T(8,128)} copy-done((f32[2,300,120]{2,1,0:T(8,128)}, f32[2,300,120]{2,1,0:T(8,128)S(1)}, u32[]{:S(2)}) %copy-start.4) | copy-done | bytes 288024
  21.6 1.7 %shard_map.57.refs_6_ = f32[2,300,120]{2,1,0:T(8,128)} custom-call(f32[2,300,120]{2,1,0:T(8,128)} %copy-done.4), custom_call_target="tpu_custom_call" | custom-call | flops 10000000000 | bytes 100000000 | tf_op jit(solution)/shard_map/pallas_call | solution.py:380
  23.4 0.5 collective-permute-start.8
  23.9 0.0 collective-permute-done.3.refs_5_
  23.9 0.0 collective-permute-start.7
  23.9 12.7 %collective-permute-done.5.refs_7_ = f32[2,300,120]{2,1,0:T(8,128)S(1)} collective-permute-done((f32[2,300,120]{2,1,0:T(8,128)}, f32[2,300,120]{2,1,0:T(8,128)S(1)}, u32[]{:S(2)}, u32[]{:S(2)}) %collective-permute-start.5) | collective-permute-done | bytes 288032 | tf_op jit(solution)/shard_map/ppermute | solution.py:388
  36.6 0.0 collective-permute-start.9
  36.6 0.1 pad_add_fusion.place_ref
  36.7 0.9 %shard_map.56 = (f32[4,16,640]{2,1,0:T(8,128)S(1)}, f32[4,16,640]{2,1,0:T(8,128)S(1)}, f32[4,16,640]{2,1,0:T(8,128)S(1)}, f32[4,16,640]{2,1,0:T(8,128)S(1)}) custom-call(s32[3]{0:T(128)S(1)} %pad_add_fusion.place_ref, s32[3,16]{1,0:T(4,128)S(1)} %copy-done.1, f32[16,16,640]{2,1,0:T(8,128)S(1)} %all-to-all-done.cells_ref), custom_call_target="tpu_custom_call" | custom-call | tf_op jit(solution)/shard_map/pallas_call | solution.py:241
  37.6 1.6 %collective-permute-start = (f32[4,16,640]{2,1,0:T(8,128)S(1)}, f32[4,16,640]{2,1,0:T(8,128)S(1)}, u32[]{:S(2)}, u32[]{:S(2)}) collective-permute-start(f32[4,16,640]{2,1,0:T(8,128)S(1)} %get-tuple-element.14), channel_id=1, source_target_pairs={{0,2},{2,0},{4,6},{6,4},{8,10},{10,8},{12,14},{14,12},{16,18},{18,... | collective-permute-start | bytes 491528 | tf_op jit(solution)/shard_map/ppermute | solution.py:388
  39.2 1.5 %collective-permute-start.1 = (f32[4,16,640]{2,1,0:T(8,128)S(1)}, f32[4,16,640]{2,1,0:T(8,128)S(1)}, u32[]{:S(2)}, u32[]{:S(2)}) collective-permute-start(f32[4,16,640]{2,1,0:T(8,128)S(1)} %get-tuple-element.15), channel_id=1, source_target_pairs={{0,4},{2,6},{4,0},{6,2},{8,12},{10,14},{12,8},{14,10},{16,20},{18,... | collective-permute-start | bytes 491528 | tf_op jit(solution)/shard_map/ppermute | solution.py:388
  40.7 0.4 collective-permute-start.2
  41.2 3.5 %collective-permute-done.refs_1_ = f32[4,16,640]{2,1,0:T(8,128)S(1)} collective-permute-done((f32[4,16,640]{2,1,0:T(8,128)S(1)}, f32[4,16,640]{2,1,0:T(8,128)S(1)}, u32[]{:S(2)}, u32[]{:S(2)}) %collective-permute-start) | collective-permute-done | bytes 163872 | tf_op jit(solution)/shard_map/ppermute | solution.py:388
  44.6 4.4 %collective-permute-done.1.refs_2_ = f32[4,16,640]{2,1,0:T(8,128)S(1)} collective-permute-done((f32[4,16,640]{2,1,0:T(8,128)S(1)}, f32[4,16,640]{2,1,0:T(8,128)S(1)}, u32[]{:S(2)}, u32[]{:S(2)}) %collective-permute-start.1) | collective-permute-done | bytes 163872 | tf_op jit(solution)/shard_map/ppermute | solution.py:388
  49.0 1.0 %copy-done = f32[2,300,120]{2,1,0:T(8,128)S(1)} copy-done((f32[2,300,120]{2,1,0:T(8,128)S(1)}, f32[2,300,120]{2,1,0:T(8,128)}, u32[]{:S(2)}) %copy-start) | copy-done | bytes 288024
  50.0 2.8 %shard_map.58 = (f32[4,8,8,128]{3,2,1,0:T(8,128)S(1)}, f32[4,8,8,128]{3,2,1,0:T(8,128)S(1)}, f32[4,8,8,128]{3,2,1,0:T(8,128)S(1)}, f32[4,8,8,128]{3,2,1,0:T(8,128)S(1)}) custom-call(s32[3]{0:T(128)S(1)} %pad_add_fusion.place_ref, f32[4,16,640]{2,1,0:T(8,128)S(1)} %get-tuple-element.13.refs_0_, f32[4,16,640]{2,1,0:T(8,128)S(1)} %collective-permute-done.refs_1_, ...), custom_call_target="tpu_custom_call" | custom-call | tf_op jit(solution)/shard_map/pallas_call | solution.py:314
  52.8 1.3 %collective-permute-start.10 = (f32[4,8,8,128]{3,2,1,0:T(8,128)S(1)}, f32[4,8,8,128]{3,2,1,0:T(8,128)S(1)}, u32[]{:S(2)}, u32[]{:S(2)}) collective-permute-start(f32[4,8,8,128]{3,2,1,0:T(8,128)S(1)} %get-tuple-element.18), channel_id=1, source_target_pairs={{0,2},{2,0},{4,6},{6,4},{8,10},{10,8},{12,14},{14,12},{16,18},{18,... | collective-permute-start | bytes 393224 | tf_op jit(solution)/shard_map/ppermute | solution.py:388
  54.1 0.8 %collective-permute-start.11 = (f32[4,8,8,128]{3,2,1,0:T(8,128)S(1)}, f32[4,8,8,128]{3,2,1,0:T(8,128)S(1)}, u32[]{:S(2)}, u32[]{:S(2)}) collective-permute-start(f32[4,8,8,128]{3,2,1,0:T(8,128)S(1)} %get-tuple-element.19), channel_id=1, source_target_pairs={{0,4},{2,6},{4,0},{6,2},{8,12},{10,14},{12,8},{14,10},{16,20},{18,... | collective-permute-start | bytes 393224 | tf_op jit(solution)/shard_map/ppermute | solution.py:388
  54.9 1.4 %collective-permute-start.12 = (f32[4,8,8,128]{3,2,1,0:T(8,128)S(1)}, f32[4,8,8,128]{3,2,1,0:T(8,128)S(1)}, u32[]{:S(2)}, u32[]{:S(2)}) collective-permute-start(f32[4,8,8,128]{3,2,1,0:T(8,128)S(1)} %get-tuple-element.20), channel_id=1, source_target_pairs={{0,6},{2,4},{4,2},{6,0},{8,14},{10,12},{12,10},{14,8},{16,22},{18,... | collective-permute-start | bytes 393224 | tf_op jit(solution)/shard_map/ppermute | solution.py:388
  56.3 2.0 %collective-permute-done.10.refs_1_ = f32[4,8,8,128]{3,2,1,0:T(8,128)S(1)} collective-permute-done((f32[4,8,8,128]{3,2,1,0:T(8,128)S(1)}, f32[4,8,8,128]{3,2,1,0:T(8,128)S(1)}, u32[]{:S(2)}, u32[]{:S(2)}) %collective-permute-start.10) | collective-permute-done | bytes 131104 | tf_op jit(solution)/shard_map/ppermute | solution.py:388
  58.4 3.4 %collective-permute-done.11.refs_2_ = f32[4,8,8,128]{3,2,1,0:T(8,128)S(1)} collective-permute-done((f32[4,8,8,128]{3,2,1,0:T(8,128)S(1)}, f32[4,8,8,128]{3,2,1,0:T(8,128)S(1)}, u32[]{:S(2)}, u32[]{:S(2)}) %collective-permute-start.11) | collective-permute-done | bytes 131104 | tf_op jit(solution)/shard_map/ppermute | solution.py:388
  61.7 1.8 %shard_map.59 = f32[128,900]{1,0:T(8,128)} custom-call(s32[3]{0:T(128)S(1)} %pad_add_fusion.place_ref, s32[16]{0:T(128)S(1)} %copy-done.2, f32[4,8,8,128]{3,2,1,0:T(8,128)S(1)} %get-tuple-element.17.refs_0_, f32[4,8,8,128]{3,2,1,0:T(8,128)S(1)} %collective-permute-done.10.refs_1_, f32[4,8,8,128]{3,2,1,0:T(8,128)S(1)} %collective-permute-done.11.refs_2_, ...), custom_call_target="tpu_custom_call" | custom-call | tf_op jit(solution)/shard_map/pallas_call | solution.py:365
  (15 shorter events, 0.0 us)
Async XLA Ops:
  1.0 7.3 %copy-start.3 = (f32[2,300,60]{1,0,2:T(2,128)S(1)}, f32[2,300,60]{1,0,2:T(2,128)}, u32[]{:S(2)}) copy-start(f32[2,300,60]{1,0,2:T(2,128)} %param.7) | copy-start | bytes 432004
  1.0 19.9 %collective-permute-start.4 = (f32[2,300,120]{2,1,0:T(8,128)S(1)}, f32[2,300,120]{2,1,0:T(8,128)S(1)}, u32[]{:S(2)}, u32[]{:S(2)}) collective-permute-start(f32[2,300,120]{2,1,0:T(8,128)S(1)} %bitcast.8), channel_id=1, source_target_pairs={{0,16},{2,18},{4,20},{6,22},{8,24},{10,26},{12,28},{14,30},{16,0},... | collective-permute-start | bytes 864008 | tf_op jit(solution)/shard_map/ppermute | solution.py:388
  5.1 18.8 %collective-permute-start.3 = (f32[2,300,120]{2,1,0:T(8,128)S(1)}, f32[2,300,120]{2,1,0:T(8,128)S(1)}, u32[]{:S(2)}, u32[]{:S(2)}) collective-permute-start(f32[2,300,120]{2,1,0:T(8,128)S(1)} %bitcast.9), channel_id=1, source_target_pairs={{0,8},{2,10},{4,12},{6,14},{8,0},{10,2},{12,4},{14,6},{16,24},{18,... | collective-permute-start | bytes 864008 | tf_op jit(solution)/shard_map/ppermute | solution.py:388
  11.4 25.4 %all-to-all-start = ((f32[16,16,640]{2,1,0:T(8,128)}), f32[16,16,640]{2,1,0:T(8,128)S(1)}, u32[]{:S(2)}, u32[]{:S(2)}) async-start(f32[16,16,640]{2,1,0:T(8,128)} %bitcast.3), calls=%async_computation | async-start | bytes 1310720 | tf_op jit(solution)/shard_map/all_to_all | solution.py:402
  15.2 21.5 %copy-start.1 = (s32[3,16]{1,0:T(4,128)S(1)}, s32[3,16]{1,0:T(4,128)}, u32[]{:S(2)}) copy-start(s32[3,16]{1,0:T(4,128)} %offset_ref.1) | copy-start | bytes 580
  20.9 0.7 %copy-start.4 = (f32[2,300,120]{2,1,0:T(8,128)}, f32[2,300,120]{2,1,0:T(8,128)S(1)}, u32[]{:S(2)}) copy-start(f32[2,300,120]{2,1,0:T(8,128)S(1)} %collective-permute-done.4.in_ref) | copy-start | bytes 864004
  23.4 13.3 %collective-permute-start.5 = (f32[2,300,120]{2,1,0:T(8,128)}, f32[2,300,120]{2,1,0:T(8,128)S(1)}, u32[]{:S(2)}, u32[]{:S(2)}) collective-permute-start(f32[2,300,120]{2,1,0:T(8,128)} %shard_map.57.refs_6_), channel_id=1, source_target_pairs={{0,8},{2,10},{4,12},{6,14},{8,0},{10,2},{12,4},{14,6},{16,24},{18,... | collective-permute-start | bytes 864008 | tf_op jit(solution)/shard_map/ppermute | solution.py:388
  23.4 15.8 %collective-permute-start.6 = (f32[2,300,120]{2,1,0:T(8,128)S(1)}, f32[2,300,120]{2,1,0:T(8,128)S(1)}, u32[]{:S(2)}, u32[]{:S(2)}) collective-permute-start(f32[2,300,120]{2,1,0:T(8,128)S(1)} %bitcast.10), channel_id=1, source_target_pairs={{0,1},{1,0},{2,3},{3,2},{4,5},{5,4},{6,7},{7,6},{8,9},{9,8},{10,11... | collective-permute-start | bytes 864008 | tf_op jit(solution)/shard_map/ppermute | solution.py:400
  23.4 17.3 %collective-permute-start.8 = (f32[2,300,120]{2,1,0:T(8,128)}, f32[2,300,120]{2,1,0:T(8,128)S(1)}, u32[]{:S(2)}, u32[]{:S(2)}) collective-permute-start(f32[2,300,120]{2,1,0:T(8,128)} %shard_map.57.refs_6_), channel_id=1, source_target_pairs={{0,1},{1,0},{2,3},{3,2},{4,5},{5,4},{6,7},{7,6},{8,9},{9,8},{10,11... | collective-permute-start | bytes 864008 | tf_op jit(solution)/shard_map/ppermute | solution.py:400
  23.9 17.3 %collective-permute-start.7 = (f32[2,300,120]{2,1,0:T(8,128)S(1)}, f32[2,300,120]{2,1,0:T(8,128)S(1)}, u32[]{:S(2)}, u32[]{:S(2)}) collective-permute-start(f32[2,300,120]{2,1,0:T(8,128)S(1)} %collective-permute-done.3.refs_5_), channel_id=1, source_target_pairs={{0,1},{1,0},{2,3},{3,2},{4,5},{5,4},{6,7},{7,6},{8,9},{9,8},{10,11... | collective-permute-start | bytes 864008 | tf_op jit(solution)/shard_map/ppermute | solution.py:400
  36.6 4.5 %collective-permute-start.9 = (f32[2,300,120]{2,1,0:T(8,128)S(1)}, f32[2,300,120]{2,1,0:T(8,128)S(1)}, u32[]{:S(2)}, u32[]{:S(2)}) collective-permute-start(f32[2,300,120]{2,1,0:T(8,128)S(1)} %collective-permute-done.5.refs_7_), channel_id=1, source_target_pairs={{0,1},{1,0},{2,3},{3,2},{4,5},{5,4},{6,7},{7,6},{8,9},{9,8},{10,11... | collective-permute-start | bytes 864008 | tf_op jit(solution)/shard_map/ppermute | solution.py:400
  36.7 25.0 %copy-start.2 = (s32[16]{0:T(128)S(1)}, s32[16]{0:T(128)}, u32[]{:S(2)}) copy-start(s32[16]{0:T(128)} %transfer_ref.1) | copy-start | bytes 196
  37.6 7.1 %collective-permute-start = (f32[4,16,640]{2,1,0:T(8,128)S(1)}, f32[4,16,640]{2,1,0:T(8,128)S(1)}, u32[]{:S(2)}, u32[]{:S(2)}) collective-permute-start(f32[4,16,640]{2,1,0:T(8,128)S(1)} %get-tuple-element.14), channel_id=1, source_target_pairs={{0,2},{2,0},{4,6},{6,4},{8,10},{10,8},{12,14},{14,12},{16,18},{18,... | collective-permute-start | bytes 491528 | tf_op jit(solution)/shard_map/ppermute | solution.py:388
  39.2 9.8 %collective-permute-start.1 = (f32[4,16,640]{2,1,0:T(8,128)S(1)}, f32[4,16,640]{2,1,0:T(8,128)S(1)}, u32[]{:S(2)}, u32[]{:S(2)}) collective-permute-start(f32[4,16,640]{2,1,0:T(8,128)S(1)} %get-tuple-element.15), channel_id=1, source_target_pairs={{0,4},{2,6},{4,0},{6,2},{8,12},{10,14},{12,8},{14,10},{16,20},{18,... | collective-permute-start | bytes 491528 | tf_op jit(solution)/shard_map/ppermute | solution.py:388
  40.7 8.3 %collective-permute-start.2 = (f32[4,16,640]{2,1,0:T(8,128)S(1)}, f32[4,16,640]{2,1,0:T(8,128)S(1)}, u32[]{:S(2)}, u32[]{:S(2)}) collective-permute-start(f32[4,16,640]{2,1,0:T(8,128)S(1)} %get-tuple-element.16), channel_id=1, source_target_pairs={{0,6},{2,4},{4,2},{6,0},{8,14},{10,12},{12,10},{14,8},{16,22},{18,... | collective-permute-start | bytes 491528 | tf_op jit(solution)/shard_map/ppermute | solution.py:388
  49.0 1.0 %copy-start = (f32[2,300,120]{2,1,0:T(8,128)S(1)}, f32[2,300,120]{2,1,0:T(8,128)}, u32[]{:S(2)}) copy-start(f32[2,300,120]{2,1,0:T(8,128)} %shard_map.57.refs_6_) | copy-start | bytes 864004
  52.8 5.6 %collective-permute-start.10 = (f32[4,8,8,128]{3,2,1,0:T(8,128)S(1)}, f32[4,8,8,128]{3,2,1,0:T(8,128)S(1)}, u32[]{:S(2)}, u32[]{:S(2)}) collective-permute-start(f32[4,8,8,128]{3,2,1,0:T(8,128)S(1)} %get-tuple-element.18), channel_id=1, source_target_pairs={{0,2},{2,0},{4,6},{6,4},{8,10},{10,8},{12,14},{14,12},{16,18},{18,... | collective-permute-start | bytes 393224 | tf_op jit(solution)/shard_map/ppermute | solution.py:388
  54.1 7.7 %collective-permute-start.11 = (f32[4,8,8,128]{3,2,1,0:T(8,128)S(1)}, f32[4,8,8,128]{3,2,1,0:T(8,128)S(1)}, u32[]{:S(2)}, u32[]{:S(2)}) collective-permute-start(f32[4,8,8,128]{3,2,1,0:T(8,128)S(1)} %get-tuple-element.19), channel_id=1, source_target_pairs={{0,4},{2,6},{4,0},{6,2},{8,12},{10,14},{12,8},{14,10},{16,20},{18,... | collective-permute-start | bytes 393224 | tf_op jit(solution)/shard_map/ppermute | solution.py:388
  54.9 6.8 %collective-permute-start.12 = (f32[4,8,8,128]{3,2,1,0:T(8,128)S(1)}, f32[4,8,8,128]{3,2,1,0:T(8,128)S(1)}, u32[]{:S(2)}, u32[]{:S(2)}) collective-permute-start(f32[4,8,8,128]{3,2,1,0:T(8,128)S(1)} %get-tuple-element.20), channel_id=1, source_target_pairs={{0,6},{2,4},{4,2},{6,0},{8,14},{10,12},{12,10},{14,8},{16,22},{18,... | collective-permute-start | bytes 393224 | tf_op jit(solution)/shard_map/ppermute | solution.py:388

commit v2 on v1

--- a/solution.py
+++ b/solution.py
@@ -98,6 +98,7 @@
         self.main = self.basis // LANES * LANES
         self.rest = self.basis - self.main
         self.width = 2 * self.main + LANES
+        self.depth = self.main + HALF_LANES
         self.bands = self.occ // KX
         self.rows = padded(self.bands, 8)
         self.chunk = self.vir_half // 2
@@ -121,52 +122,50 @@
         )
 
 
-def half_kernel(sz, block_ref, occ_ref, out_ref, left_ref, wide_ref):
-    @pl.when(pl.program_id(0) == 0)
-    def _():
-        place = lax.broadcasted_iota(jnp.int32, (KX * sz.rows, sz.occ), 0)
-        band = lax.broadcasted_iota(jnp.int32, (KX * sz.rows, sz.occ), 1)
-        inner = place % sz.rows
-        pick = ((place // sz.rows * sz.bands + inner == band) & (inner < sz.bands)).astype(BF16)
-        for part in range(2):
-            sign = 1.0 if part == 0 else -1.0
-            for level, term in enumerate(split(occ_ref[part])):
-                rows = lax.dot_general(pick, term, (((1,), (1,)), ((), ())), preferred_element_type=F32)
-                left_ref[level, part] = sign * rows
-        wide_ref[...] = jnp.zeros_like(wide_ref)
-
-    wide_ref[:, : sz.basis] = block_ref[0, 0]
-    high, low = split(wide_ref[...])
+def half_kernel(sz, block_hbm, occ_hbm, out_ref, block_ref, occ_ref, block_sem, occ_sem):
     count = KX * sz.rows
-    left_high = left_ref[0].reshape(2 * count, sz.basis).astype(BF16)
-    left_low = left_ref[1].reshape(2 * count, sz.basis).astype(BF16)
-    half = dot(left_high, high) + dot(left_low, high) + dot(left_high, low)
-    real, imag = half[:count], half[count:]
-    rest = real[:, sz.main :] + pltpu.roll(imag[:, sz.main :], HALF_LANES, 1)
-    for z in range(KX):
-        span = slice(z * sz.rows, (z + 1) * sz.rows)
-        out_ref[z, 0, :, : sz.main] = real[span, : sz.main]
-        out_ref[z, 0, :, sz.main : 2 * sz.main] = imag[span, : sz.main]
-        out_ref[z, 0, :, 2 * sz.main :] = rest[span]
+    occ_copy = pltpu.make_async_copy(occ_hbm, occ_ref, occ_sem)
+    block_copy = pltpu.make_async_copy(block_hbm, block_ref, block_sem)
+    occ_copy.start()
+    block_copy.start()
+    place = lax.broadcasted_iota(jnp.int32, (count, sz.occ), 0)
+    band = lax.broadcasted_iota(jnp.int32, (count, sz.occ), 1)
+    inner = place % sz.rows
+    pick = ((place // sz.rows * sz.bands + inner == band) & (inner < sz.bands)).astype(BF16)
+    occ_copy.wait()
+    terms = [split(occ_ref[:, part]) for part in range(2)]
+    left_high = jnp.concatenate([dot(pick, terms[0][0]), -dot(pick, terms[1][0])], axis=0).astype(BF16)
+    left_low = jnp.concatenate([dot(pick, terms[0][1]), -dot(pick, terms[1][1])], axis=0).astype(BF16)
+    fill = jnp.zeros((sz.basis, LANES - sz.rest), F32)
+    block_copy.wait()
+    for p in range(sz.slab):
+        high, low = split(jnp.concatenate([block_ref[:, p], fill], axis=1))
+        half = dot(left_high, high) + dot(left_low, high) + dot(left_high, low)
+        real, imag = half[:count], half[count:]
+        rest = real[:, sz.main :] + pltpu.roll(imag[:, sz.main :], HALF_LANES, 1)
+        for z in range(KX):
+            span = slice(z * sz.rows, (z + 1) * sz.rows)
+            out_ref[z, p, :, : sz.main] = real[span, : sz.main]
+            out_ref[z, p, :, sz.main : 2 * sz.main] = imag[span, : sz.main]
+            out_ref[z, p, :, 2 * sz.main :] = rest[span]
 
 
 def half_bands(sz, blocks, occ_coeff):
+    anywhere = pl.BlockSpec(memory_space=pl.ANY)
     return pl.pallas_call(
         functools.partial(half_kernel, sz),
-        grid=(sz.slab,),
         out_shape=jax.ShapeDtypeStruct((KX, KY, sz.rows, sz.width), F32),
-        in_specs=[
-            pl.BlockSpec((1, 1, sz.basis, sz.basis), lambda p: (0, p, 0, 0)),
-            pl.BlockSpec((2, sz.basis, sz.occ), lambda p: (0, 0, 0)),
+        in_specs=[anywhere, anywhere],
+        out_specs=pl.BlockSpec(memory_space=pltpu.VMEM),
+        scratch_shapes=[
+            pltpu.VMEM((sz.basis, sz.slab, sz.basis), F32),
+            pltpu.VMEM((sz.occ, 2, sz.basis), F32),
+            pltpu.SemaphoreType.DMA,
+            pltpu.SemaphoreType.DMA,
         ],
-        out_specs=pl.BlockSpec((KX, 1, sz.rows, sz.width), lambda p: (0, p, 0, 0)),
-        scratch_shapes=[
-            pltpu.VMEM((2, 2, KX * sz.rows, sz.basis), F32),
-            pltpu.VMEM((sz.basis, sz.main + LANES), F32),
-        ],
-        compiler_params=pltpu.CompilerParams(vmem_limit_bytes=32 << 20),
+        compiler_params=pltpu.CompilerParams(vmem_limit_bytes=60 << 20),
         cost_estimate=pl.CostEstimate(flops=10**10, bytes_accessed=60_000_000, transcendentals=0),
-    )(blocks, occ_coeff)
+    )(blocks[0].transpose(1, 0, 2), occ_coeff.transpose(2, 0, 1))
 
 
 def four_points(zero, one, two, three, turn):
@@ -252,40 +251,28 @@
 
 
 def band_kernel(sz, place_ref, *refs):
-    halves, own, other = refs[:KY], refs[KY : KY + KX], refs[KY + KX : KY + 2 * KX]
-    outs = refs[KY + 2 * KX : 2 * KY + 2 * KX]
-    left_ref, band_ref, tile_ref = refs[2 * KY + 2 * KX :]
-    seat, core = place_ref[1], place_ref[2]
-    low_lanes = lax.broadcasted_iota(jnp.int32, (sz.basis, LANES), 1) < HALF_LANES
+    halves, rights, outs = refs[:KY], refs[KY : KY + KX], refs[KY + KX : 2 * KY + KX]
+    left_ref, band_ref, tile_ref = refs[2 * KY + KX :]
+    seat = place_ref[1]
     count = KY * sz.rows
     for step in range(KY):
         left_ref[:, step ^ seat] = halves[step][...]
-
-    def spread(ref, part):
-        value = jnp.concatenate([ref[part], ref[part][:, : LANES - sz.vir_half]], axis=1)
-        return jnp.where(low_lanes, value, pltpu.roll(value, HALF_LANES - sz.chunk, 1))
 
     for k in range(KX):
         left = left_ref[k].reshape(count, sz.width)
         tail = left[:, 2 * sz.main :]
         near = jnp.concatenate([left[:, : sz.main], left[:, sz.main : 2 * sz.main]], axis=0)
-        rest = jnp.concatenate([tail, pltpu.roll(tail, HALF_LANES, 1)], axis=0)[:, : sz.rest]
+        rest = jnp.concatenate([tail, pltpu.roll(tail, HALF_LANES, 1)], axis=0)[:, :HALF_LANES]
         near_high, near_low = split(near)
         rest_high, rest_low = split(rest)
-        columns = []
-        for part in range(2):
-            mine, theirs = spread(own[k], part), spread(other[k], part)
-            columns += [jnp.where(core == 0, mine, theirs), jnp.where(core == 0, theirs, mine)]
-        right = jnp.concatenate(columns, axis=1)
-        main_high, main_low = split(right[: sz.main])
-        last_high, last_low = split(right[sz.main :])
+        high, low = rights[k][0], rights[k][1]
         band = (
-            dot(near_high, main_high)
-            + dot(near_low, main_high)
-            + dot(near_high, main_low)
-            + dot(rest_high, last_high)
-            + dot(rest_low, last_high)
-            + dot(rest_high, last_low)
+            dot(near_high, high[: sz.main])
+            + dot(near_low, high[: sz.main])
+            + dot(near_high, low[: sz.main])
+            + dot(rest_high, high[sz.main :])
+            + dot(rest_low, high[sz.main :])
+            + dot(rest_high, low[sz.main :])
         )
         width = 2 * LANES
         top, bottom = band[:count], band[count:]
@@ -307,14 +294,14 @@
                 outs[step][k, n] = tile_ref[first + n]
 
 
-def band_product(sz, place, halves, own, other):
+def band_product(sz, place, halves, rights):
     shape = jax.ShapeDtypeStruct((KX, sz.tiles, 2 * KY, LANES), F32)
     whole = pl.BlockSpec(memory_space=pltpu.VMEM)
     scalars = pl.BlockSpec(memory_space=pltpu.SMEM)
     return pl.pallas_call(
         functools.partial(band_kernel, sz),
         out_shape=[shape] * KY,
-        in_specs=[scalars] + [whole] * (KY + 2 * KX),
+        in_specs=[scalars] + [whole] * (KY + KX),
         out_specs=[whole] * KY,
         scratch_shapes=[
             pltpu.VMEM((KX, KY, sz.rows, sz.width), F32),
@@ -322,7 +309,7 @@
             pltpu.VMEM((2 * sz.bands, 2 * KY, LANES), F32),
         ],
         compiler_params=pltpu.CompilerParams(vmem_limit_bytes=32 << 20),
-    )(place, *halves, *own, *other)
+    )(place, *halves, *rights)
 
 
 def regroup_kernel(sz, place_ref, transfer_ref, *refs):
@@ -372,37 +359,84 @@
     )(place, transfer_index, *sources)
 
 
+def columns_kernel(sz, place_ref, own_ref, other_ref, out_ref):
+    core = place_ref[2]
+    low_lanes = lax.broadcasted_iota(jnp.int32, (sz.basis, LANES), 1) < HALF_LANES
+    fill = jnp.zeros((sz.basis, LANES - sz.vir_half), F32)
+    under = jnp.zeros((sz.depth - sz.basis, LANES), F32)
+    for part in range(2):
+        sides = []
+        for ref in (own_ref, other_ref):
+            value = jnp.concatenate([ref[:, part], fill], axis=1)
+            value = jnp.where(low_lanes, value, pltpu.roll(value, HALF_LANES - sz.chunk, 1))
+            sides.append(jnp.concatenate([value, under], axis=0))
+        mine, theirs = sides
+        for h, value in enumerate([jnp.where(core == 0, mine, theirs), jnp.where(core == 0, theirs, mine)]):
+            lanes = slice((2 * part + h) * LANES, (2 * part + h + 1) * LANES)
+            for level, term in enumerate(split(value)):
+                out_ref[level, :, lanes] = term
+
+
+def columns(sz, place, own, other, flops):
+    whole = pl.BlockSpec(memory_space=pltpu.VMEM)
+    scalars = pl.BlockSpec(memory_space=pltpu.SMEM)
+    return pl.pallas_call(
+        functools.partial(columns_kernel, sz),
+        out_shape=jax.ShapeDtypeStruct((2, sz.depth, 4 * LANES), BF16),
+        in_specs=[scalars, whole, whole],
+        out_specs=whole,
+        compiler_params=pltpu.CompilerParams(vmem_limit_bytes=32 << 20),
+        cost_estimate=pl.CostEstimate(flops=flops, bytes_accessed=flops // 100, transcendentals=0),
+    )(place, own, other)
+
+
 def hold_kernel(in_ref, out_ref):
-    out_ref[...] = in_ref[...]
+    del in_ref, out_ref
 
 
 def hold(value):
     return pl.pallas_call(
         hold_kernel,
-        out_shape=jax.ShapeDtypeStruct(value.shape, F32),
-        cost_estimate=pl.CostEstimate(flops=10**10, bytes_accessed=100_000_000, transcendentals=0),
+        out_shape=jax.ShapeDtypeStruct(value.shape, value.dtype),
+        in_specs=[pl.BlockSpec(memory_space=pl.ANY)],
+        out_specs=pl.BlockSpec(memory_space=pl.ANY),
+        input_output_aliases={0: 0},
+        cost_estimate=pl.CostEstimate(flops=10**10, bytes_accessed=10**8, transcendentals=0),
     )(value)
 
 
 def swap(value, step):
     return lax.ppermute(value, "cell", [(d, d ^ step) for d in range(KX * KY)])
+
+
+def swap_cores(value):
+    return lax.ppermute(value, "aux", [(0, 1), (1, 0)])
 
 
 def by_planes(blocks, cell_offsets, occ_coeff, vir_coeff, transfer_index):
     sz = Sizes(blocks, occ_coeff, vir_coeff)
     me = lax.axis_index("cell")
     place = jnp.stack([me // KY, me % KY, lax.axis_index("aux")]).astype(jnp.int32)
-    home = vir_coeff[0]
+    home = vir_coeff[0].transpose(1, 0, 2)
     across = hold(swap(home, 2 * KY))
-    beside = swap(home, KY)
-    corner = swap(across, KY)
-    own = [home, beside, across, corner]
-    other = [lax.ppermute(v, "aux", [(0, 1), (1, 0)]) for v in own]
+    beside = hold(swap(home, KY))
     sent = half_bands(sz, blocks, occ_coeff).reshape(KX * KY, sz.rows, sz.width)
     cells = lax.all_to_all(sent, "cell", split_axis=0, concat_axis=0, tiled=True)
-    points = lattice_sum(sz, place, cell_offsets, cells)
+    corner = swap(across, KY)
+    ours, beside = lax.optimization_barrier((home, beside))
+    long, short = 10**10, 10**6
+    rights = [
+        columns(sz, place, ours, swap_cores(ours), long),
+        columns(sz, place, beside, swap_cores(beside), long),
+        columns(sz, place, across, swap_cores(across), long),
+    ]
+    cells, *rights = lax.optimization_barrier((cells, *rights))
+    points = list(lattice_sum(sz, place, cell_offsets, cells))
+    corner, points[0] = lax.optimization_barrier((corner, points[0]))
+    rights.append(columns(sz, place, corner, swap_cores(corner), short))
     halves = [points[0]] + [swap(points[s], s) for s in range(1, KY)]
-    bands = band_product(sz, place, halves, own, other)
+    halves[1] = hold(halves[1])
+    bands = band_product(sz, place, halves, rights)
     sources = [bands[0]] + [swap(bands[s], s) for s in range(1, KY)]
     out = regroup(sz, place, transfer_index, sources)
     return out.reshape(2, sz.slab, KX * KY, sz.pairs)

time: 63.9 us -> 59.6 us (0.933)
  waiting for transfers between devices: 31.8 us -> 25.6 us
  Pallas kernels: 10 us -> 13 us
  local copies, waits for them, and re-layouts: 4.49 us -> 3.04 us
    ppermute x9, waiting for transfers between devices: 31.7 us -> 19.8 us  [swap(): return lax.ppermute(value, 'cell', [(d, d ^ step) for d in range(KX * KY)])]
    all_to_all x1, waiting for transfers between devices: 0.01 us -> 5.84 us  [by_planes(): lax.all_to_all(sent, 'cell', split_axis=0, concat_axis=0, tiled=True)]
    pallas_call x2 -> x8, Pallas kernels: 4.58 us -> 7.76 us  [the longest x4 4.06 us: columns(): pl.pallas_call(functools.partial(columns_kernel, sz), out_shape=jax.Shape...]
    unnamed x13 -> x20, local copies, waits for them, and re-layouts: 4.49 us -> 3.04 us
    pallas_call x1, Pallas kernels: 2.77 us -> 1.83 us  [band_product(): pl.pallas_call(functools.partial(band_kernel, sz), out_shape=[shape] * KY...]
    pallas_call x1, Pallas kernels: 0.85 us -> 1.57 us  [lattice_sum(): pl.pallas_call(functools.partial(lattice_kernel, sz), out_shape=[shape] *...]
  transfers between devices with their start and end apart: 14 -> 14, of which waited for: 6 -> 8; matrix products, arithmetic and copies ran while one was open for 3% -> 0% of each run, Pallas kernels for 9% -> 16%
where the time goes in v2:
time: 59.6 us; the launch traced here: 59.3 us
  waiting for transfers between devices  25.6 us (43%)
  starting transfers between devices  17.5 us (29%)
  Pallas kernels  13 us (22%)
  local copies, waits for them, and re-layouts  3.04 us (5%)
    ppermute x9, waiting for transfers between devices, swap(): return lax.ppermute(value, 'cell', [(d, d ^ step) for d in range(KX * KY)])  19.8 us
    ppermute x9, starting transfers between devices, swap(): return lax.ppermute(value, 'cell', [(d, d ^ step) for d in range(KX * KY)])  13.4 us
    all_to_all x1, waiting for transfers between devices, by_planes(): lax.all_to_all(sent, 'cell', split_axis=0, concat_axis=0, tiled=True)  5.84 us
    pallas_call x4, Pallas kernels, columns(): pl.pallas_call(functools.partial(columns_kernel, sz), out_shape=jax.Shape...  4.06 us
    all_to_all x1, starting transfers between devices, by_planes(): lax.all_to_all(sent, 'cell', split_axis=0, concat_axis=0, tiled=True)  3.84 us
    pallas_call x1, Pallas kernels, half_bands(): pl.pallas_call(functools.partial(half_kernel, sz), out_shape=jax.ShapeDty...  3.69 us
    unnamed x20, local copies, waits for them, and re-layouts  3.04 us
    pallas_call x1, Pallas kernels, regroup(): pl.pallas_call(functools.partial(regroup_kernel, sz), out_shape=jax.Shape...  1.85 us
  transfers between devices with their start and end apart: 14, of which 8 were waited for; matrix products, arithmetic and copies ran while one was open for 0% of the time, Pallas kernels for 16%

profile of v2, /device:TPU:0, one launch (start us, length us, event | category | flops | bytes accessed | tf_op | source)
XLA Modules:
  0.0 59.3 jit_solution(13248382236145654593)
XLA Ops:
  0.0 3.0 %collective-permute-start.2 = (f32[300,2,120]{2,1,0:T(2,128)}, f32[300,2,120]{2,1,0:T(2,128)S(1)}, u32[]{:S(2)}, u32[]{:S(2)}) collective-permute-start(f32[300,2,120]{2,1,0:T(2,128)} %bitcast.12), channel_id=1, source_target_pairs={{0,8},{2,10},{4,12},{6,14},{8,0},{10,2},{12,4},{14,6},{16,24},{18,... | collective-permute-start | bytes 864008 | tf_op jit(solution)/shard_map/ppermute | solution.py:409
  3.0 2.6 %collective-permute-start = (f32[300,2,120]{2,1,0:T(2,128)}, f32[300,2,120]{2,1,0:T(2,128)S(1)}, u32[]{:S(2)}, u32[]{:S(2)}) collective-permute-start(f32[300,2,120]{2,1,0:T(2,128)} %bitcast.13), channel_id=1, source_target_pairs={{0,16},{2,18},{4,20},{6,22},{8,24},{10,26},{12,28},{14,30},{16,0},... | collective-permute-start | bytes 864008 | tf_op jit(solution)/shard_map/ppermute | solution.py:409
  5.6 3.7 %shard_map.56 = f32[4,4,16,640]{3,2,1,0:T(8,128)} custom-call(f32[300,4,300]{2,1,0:T(4,128)} %bitcast.17, f32[60,2,300]{2,1,0:T(2,128)} %bitcast.18), custom_call_target="tpu_custom_call" | custom-call | flops 10000000000 | bytes 60000000 | tf_op jit(solution)/shard_map/pallas_call | solution.py:155
  9.3 3.8 %all-to-all-start = ((f32[16,16,640]{2,1,0:T(8,128)}), f32[16,16,640]{2,1,0:T(8,128)S(1)}, u32[]{:S(2)}, u32[]{:S(2)}) async-start(f32[16,16,640]{2,1,0:T(8,128)} %bitcast.16), calls=%async_computation | async-start | bytes 1310720 | tf_op jit(solution)/shard_map/all_to_all | solution.py:424
  13.2 0.1 pad_add_fusion.place_ref
  13.3 4.5 %collective-permute-done.2.in_ref = f32[300,2,120]{2,1,0:T(2,128)S(1)} collective-permute-done((f32[300,2,120]{2,1,0:T(2,128)}, f32[300,2,120]{2,1,0:T(2,128)S(1)}, u32[]{:S(2)}, u32[]{:S(2)}) %collective-permute-start.2) | collective-permute-done | bytes 288032 | tf_op jit(solution)/shard_map/ppermute | solution.py:409
  17.8 0.7 %copy-done.8 = f32[300,2,120]{2,1,0:T(2,128)} copy-done((f32[300,2,120]{2,1,0:T(2,128)}, f32[300,2,120]{2,1,0:T(2,128)S(1)}, u32[]{:S(2)}) %copy-start.8) | copy-done | bytes 288024
  18.5 3.8 %collective-permute-done.in_ref = f32[300,2,120]{2,1,0:T(2,128)S(1)} collective-permute-done((f32[300,2,120]{2,1,0:T(2,128)}, f32[300,2,120]{2,1,0:T(2,128)S(1)}, u32[]{:S(2)}, u32[]{:S(2)}) %collective-permute-start) | collective-permute-done | bytes 288032 | tf_op jit(solution)/shard_map/ppermute | solution.py:409
  22.3 0.7 %copy-done.6 = f32[300,2,120]{2,1,0:T(2,128)} copy-done((f32[300,2,120]{2,1,0:T(2,128)}, f32[300,2,120]{2,1,0:T(2,128)S(1)}, u32[]{:S(2)}) %copy-start.6) | copy-done | bytes 288024
  23.0 0.7 %collective-permute-start.1 = (f32[300,2,120]{2,1,0:T(2,128)}, f32[300,2,120]{2,1,0:T(2,128)S(1)}, u32[]{:S(2)}, u32[]{:S(2)}) collective-permute-start(f32[300,2,120]{2,1,0:T(2,128)} %shard_map.55.own_ref), channel_id=1, source_target_pairs={{0,8},{2,10},{4,12},{6,14},{8,0},{10,2},{12,4},{14,6},{16,24},{18,... | collective-permute-start | bytes 864008 | tf_op jit(solution)/shard_map/ppermute | solution.py:409
  23.7 0.2 collective-permute-start.3
  24.0 1.0 %shard_map.59.refs_5_ = bf16[2,320,512]{2,1,0:T(8,128)(2,1)S(1)} custom-call(s32[3]{0:T(128)S(1)} %pad_add_fusion.place_ref, f32[300,2,120]{2,1,0:T(2,128)S(1)} %copy-done.9, f32[300,2,120]{2,1,0:T(2,128)S(1)} %collective-permute-done.4.other_ref), custom_call_target="tpu_custom_call" | custom-call | flops 10000000000 | bytes 100000000 | tf_op jit(solution)/shard_map/pallas_call | solution.py:383
  25.0 1.0 %shard_map.60.refs_6_ = bf16[2,320,512]{2,1,0:T(8,128)(2,1)S(1)} custom-call(s32[3]{0:T(128)S(1)} %pad_add_fusion.place_ref, f32[300,2,120]{2,1,0:T(2,128)S(1)} %copy-done.7, f32[300,2,120]{2,1,0:T(2,128)S(1)} %collective-permute-done.5.other_ref), custom_call_target="tpu_custom_call" | custom-call | flops 10000000000 | bytes 100000000 | tf_op jit(solution)/shard_map/pallas_call | solution.py:383
  26.1 1.0 %shard_map.58.refs_4_ = bf16[2,320,512]{2,1,0:T(8,128)(2,1)S(1)} custom-call(s32[3]{0:T(128)S(1)} %pad_add_fusion.place_ref, f32[300,2,120]{2,1,0:T(2,128)S(1)} %bitcast.15, f32[300,2,120]{2,1,0:T(2,128)S(1)} %collective-permute-done.3.other_ref), custom_call_target="tpu_custom_call" | custom-call | flops 10000000000 | bytes 100000000 | tf_op jit(solution)/shard_map/pallas_call | solution.py:383
  27.1 5.8 %all-to-all-done.cells_ref = f32[16,16,640]{2,1,0:T(8,128)S(1)} async-done(((f32[16,16,640]{2,1,0:T(8,128)}), f32[16,16,640]{2,1,0:T(8,128)S(1)}, u32[]{:S(2)}, u32[]{:S(2)}) %all-to-all-start) | async-done | bytes 655392 | tf_op jit(solution)/shard_map/all_to_all | solution.py:424
  32.9 1.6 %shard_map.61 = (f32[4,16,640]{2,1,0:T(8,128)S(1)}, f32[4,16,640]{2,1,0:T(8,128)S(1)}, f32[4,16,640]{2,1,0:T(8,128)}, f32[4,16,640]{2,1,0:T(8,128)}) custom-call(s32[3]{0:T(128)S(1)} %pad_add_fusion.place_ref, s32[3,16]{1,0:T(4,128)S(1)} %copy-done.2, f32[16,16,640]{2,1,0:T(8,128)S(1)} %all-to-all-done.cells_ref), custom_call_target="tpu_custom_call" | custom-call | tf_op jit(solution)/shard_map/pallas_call | solution.py:240
  34.5 0.5 collective-permute-start.6
  35.0 0.4 collective-permute-done.1.own_ref
  35.4 2.0 %collective-permute-start.7 = (f32[4,16,640]{2,1,0:T(8,128)}, f32[4,16,640]{2,1,0:T(8,128)S(1)}, u32[]{:S(2)}, u32[]{:S(2)}) collective-permute-start(f32[4,16,640]{2,1,0:T(8,128)} %get-tuple-element.27), channel_id=1, source_target_pairs={{0,4},{2,6},{4,0},{6,2},{8,12},{10,14},{12,8},{14,10},{16,20},{18,... | collective-permute-start | bytes 491528 | tf_op jit(solution)/shard_map/ppermute | solution.py:409
  37.4 0.9 %collective-permute-start.8 = (f32[4,16,640]{2,1,0:T(8,128)}, f32[4,16,640]{2,1,0:T(8,128)S(1)}, u32[]{:S(2)}, u32[]{:S(2)}) collective-permute-start(f32[4,16,640]{2,1,0:T(8,128)} %get-tuple-element.28), channel_id=1, source_target_pairs={{0,6},{2,4},{4,2},{6,0},{8,14},{10,12},{12,10},{14,8},{16,22},{18,... | collective-permute-start | bytes 491528 | tf_op jit(solution)/shard_map/ppermute | solution.py:409
  38.4 3.0 %collective-permute-done.6.in_ref = f32[4,16,640]{2,1,0:T(8,128)S(1)} collective-permute-done((f32[4,16,640]{2,1,0:T(8,128)S(1)}, f32[4,16,640]{2,1,0:T(8,128)S(1)}, u32[]{:S(2)}, u32[]{:S(2)}) %collective-permute-start.6) | collective-permute-done | bytes 163872 | tf_op jit(solution)/shard_map/ppermute | solution.py:409
  41.4 0.7 %copy-done = f32[4,16,640]{2,1,0:T(8,128)} copy-done((f32[4,16,640]{2,1,0:T(8,128)}, f32[4,16,640]{2,1,0:T(8,128)S(1)}, u32[]{:S(2)}) %copy-start) | copy-done | bytes 163864
  42.1 1.0 %shard_map.63.refs_7_ = bf16[2,320,512]{2,1,0:T(8,128)(2,1)S(1)} custom-call(s32[3]{0:T(128)S(1)} %pad_add_fusion.place_ref, f32[300,2,120]{2,1,0:T(2,128)S(1)} %collective-permute-done.1.own_ref, f32[300,2,120]{2,1,0:T(2,128)S(1)} %collective-permute-done.9.other_ref), custom_call_target="tpu_custom_call" | custom-call | flops 1000000 | bytes 10000 | tf_op jit(solution)/shard_map/pallas_call | solution.py:383
  43.1 2.3 %collective-permute-done.7.refs_2_ = f32[4,16,640]{2,1,0:T(8,128)S(1)} collective-permute-done((f32[4,16,640]{2,1,0:T(8,128)}, f32[4,16,640]{2,1,0:T(8,128)S(1)}, u32[]{:S(2)}, u32[]{:S(2)}) %collective-permute-start.7) | collective-permute-done | bytes 163872 | tf_op jit(solution)/shard_map/ppermute | solution.py:409
  45.4 0.9 %copy-done.1 = f32[4,16,640]{2,1,0:T(8,128)S(1)} copy-done((f32[4,16,640]{2,1,0:T(8,128)S(1)}, f32[4,16,640]{2,1,0:T(8,128)}, u32[]{:S(2)}) %copy-start.1) | copy-done | bytes 163864
  46.3 1.8 %shard_map.64 = (f32[4,8,8,128]{3,2,1,0:T(8,128)S(1)}, f32[4,8,8,128]{3,2,1,0:T(8,128)S(1)}, f32[4,8,8,128]{3,2,1,0:T(8,128)S(1)}, f32[4,8,8,128]{3,2,1,0:T(8,128)S(1)}) custom-call(s32[3]{0:T(128)S(1)} %pad_add_fusion.place_ref, f32[4,16,640]{2,1,0:T(8,128)S(1)} %get-tuple-element.25.refs_0_, f32[4,16,640]{2,1,0:T(8,128)S(1)} %copy-done.1, ...), custom_call_target="tpu_custom_call" | custom-call | tf_op jit(solution)/shard_map/pallas_call | solution.py:301
  48.2 1.5 %collective-permute-start.10 = (f32[4,8,8,128]{3,2,1,0:T(8,128)S(1)}, f32[4,8,8,128]{3,2,1,0:T(8,128)S(1)}, u32[]{:S(2)}, u32[]{:S(2)}) collective-permute-start(f32[4,8,8,128]{3,2,1,0:T(8,128)S(1)} %get-tuple-element.34), channel_id=1, source_target_pairs={{0,2},{2,0},{4,6},{6,4},{8,10},{10,8},{12,14},{14,12},{16,18},{18,... | collective-permute-start | bytes 393224 | tf_op jit(solution)/shard_map/ppermute | solution.py:409
  49.7 1.7 %collective-permute-start.11 = (f32[4,8,8,128]{3,2,1,0:T(8,128)S(1)}, f32[4,8,8,128]{3,2,1,0:T(8,128)S(1)}, u32[]{:S(2)}, u32[]{:S(2)}) collective-permute-start(f32[4,8,8,128]{3,2,1,0:T(8,128)S(1)} %get-tuple-element.35), channel_id=1, source_target_pairs={{0,4},{2,6},{4,0},{6,2},{8,12},{10,14},{12,8},{14,10},{16,20},{18,... | collective-permute-start | bytes 393224 | tf_op jit(solution)/shard_map/ppermute | solution.py:409
  51.5 0.3 collective-permute-start.12
  51.7 2.2 %collective-permute-done.10.refs_1_ = f32[4,8,8,128]{3,2,1,0:T(8,128)S(1)} collective-permute-done((f32[4,8,8,128]{3,2,1,0:T(8,128)S(1)}, f32[4,8,8,128]{3,2,1,0:T(8,128)S(1)}, u32[]{:S(2)}, u32[]{:S(2)}) %collective-permute-start.10) | collective-permute-done | bytes 131104 | tf_op jit(solution)/shard_map/ppermute | solution.py:409
  53.9 3.6 %collective-permute-done.11.refs_2_ = f32[4,8,8,128]{3,2,1,0:T(8,128)S(1)} collective-permute-done((f32[4,8,8,128]{3,2,1,0:T(8,128)S(1)}, f32[4,8,8,128]{3,2,1,0:T(8,128)S(1)}, u32[]{:S(2)}, u32[]{:S(2)}) %collective-permute-start.11) | collective-permute-done | bytes 131104 | tf_op jit(solution)/shard_map/ppermute | solution.py:409
  57.5 1.8 %shard_map.65 = f32[128,900]{1,0:T(8,128)} custom-call(s32[3]{0:T(128)S(1)} %pad_add_fusion.place_ref, s32[16]{0:T(128)S(1)} %copy-done.3, f32[4,8,8,128]{3,2,1,0:T(8,128)S(1)} %get-tuple-element.33.refs_0_, f32[4,8,8,128]{3,2,1,0:T(8,128)S(1)} %collective-permute-done.10.refs_1_, f32[4,8,8,128]{3,2,1,0:T(8,128)S(1)} %collective-permute-done.11.refs_2_, ...), custom_call_target="tpu_custom_call" | custom-call | tf_op jit(solution)/shard_map/pallas_call | solution.py:352
  (28 shorter events, 0.1 us)
Async XLA Ops:
  0.0 17.8 %collective-permute-start.2 = (f32[300,2,120]{2,1,0:T(2,128)}, f32[300,2,120]{2,1,0:T(2,128)S(1)}, u32[]{:S(2)}, u32[]{:S(2)}) collective-permute-start(f32[300,2,120]{2,1,0:T(2,128)} %bitcast.12), channel_id=1, source_target_pairs={{0,8},{2,10},{4,12},{6,14},{8,0},{10,2},{12,4},{14,6},{16,24},{18,... | collective-permute-start | bytes 864008 | tf_op jit(solution)/shard_map/ppermute | solution.py:409
  3.0 19.3 %collective-permute-start = (f32[300,2,120]{2,1,0:T(2,128)}, f32[300,2,120]{2,1,0:T(2,128)S(1)}, u32[]{:S(2)}, u32[]{:S(2)}) collective-permute-start(f32[300,2,120]{2,1,0:T(2,128)} %bitcast.13), channel_id=1, source_target_pairs={{0,16},{2,18},{4,20},{6,22},{8,24},{10,26},{12,28},{14,30},{16,0},... | collective-permute-start | bytes 864008 | tf_op jit(solution)/shard_map/ppermute | solution.py:409
  9.3 23.6 %all-to-all-start = ((f32[16,16,640]{2,1,0:T(8,128)}), f32[16,16,640]{2,1,0:T(8,128)S(1)}, u32[]{:S(2)}, u32[]{:S(2)}) async-start(f32[16,16,640]{2,1,0:T(8,128)} %bitcast.16), calls=%async_computation | async-start | bytes 1310720 | tf_op jit(solution)/shard_map/all_to_all | solution.py:424
  17.8 0.7 %copy-start.8 = (f32[300,2,120]{2,1,0:T(2,128)}, f32[300,2,120]{2,1,0:T(2,128)S(1)}, u32[]{:S(2)}) copy-start(f32[300,2,120]{2,1,0:T(2,128)S(1)} %collective-permute-done.2.in_ref) | copy-start | bytes 864004
  18.5 5.2 %copy-start.4 = (f32[1,2,300,120]{3,1,2,0:T(2,128)S(1)}, f32[1,2,300,120]{3,1,2,0:T(2,128)}, u32[]{:S(2)}) copy-start(f32[1,2,300,120]{3,1,2,0:T(2,128)} %param.8) | copy-start | bytes 864004
  18.5 5.5 %copy-start.9 = (f32[300,2,120]{2,1,0:T(2,128)S(1)}, f32[300,2,120]{2,1,0:T(2,128)}, u32[]{:S(2)}) copy-start(f32[300,2,120]{2,1,0:T(2,128)} %shard_map.57.own_ref) | copy-start | bytes 864004
  18.5 5.4 %collective-permute-start.4 = (f32[300,2,120]{2,1,0:T(2,128)}, f32[300,2,120]{2,1,0:T(2,128)S(1)}, u32[]{:S(2)}, u32[]{:S(2)}) collective-permute-start(f32[300,2,120]{2,1,0:T(2,128)} %shard_map.57.own_ref), channel_id=1, source_target_pairs={{0,1},{1,0},{2,3},{3,2},{4,5},{5,4},{6,7},{7,6},{8,9},{9,8},{10,11... | collective-permute-start | bytes 864008 | tf_op jit(solution)/shard_map/ppermute | solution.py:413
  22.3 0.7 %copy-start.6 = (f32[300,2,120]{2,1,0:T(2,128)}, f32[300,2,120]{2,1,0:T(2,128)S(1)}, u32[]{:S(2)}) copy-start(f32[300,2,120]{2,1,0:T(2,128)S(1)} %collective-permute-done.in_ref) | copy-start | bytes 864004
  23.0 2.0 %copy-start.7 = (f32[300,2,120]{2,1,0:T(2,128)S(1)}, f32[300,2,120]{2,1,0:T(2,128)}, u32[]{:S(2)}) copy-start(f32[300,2,120]{2,1,0:T(2,128)} %shard_map.55.own_ref) | copy-start | bytes 864004
  23.0 2.0 %collective-permute-start.5 = (f32[300,2,120]{2,1,0:T(2,128)}, f32[300,2,120]{2,1,0:T(2,128)S(1)}, u32[]{:S(2)}, u32[]{:S(2)}) collective-permute-start(f32[300,2,120]{2,1,0:T(2,128)} %shard_map.55.own_ref), channel_id=1, source_target_pairs={{0,1},{1,0},{2,3},{3,2},{4,5},{5,4},{6,7},{7,6},{8,9},{9,8},{10,11... | collective-permute-start | bytes 864008 | tf_op jit(solution)/shard_map/ppermute | solution.py:413
  23.0 12.4 %collective-permute-start.1 = (f32[300,2,120]{2,1,0:T(2,128)}, f32[300,2,120]{2,1,0:T(2,128)S(1)}, u32[]{:S(2)}, u32[]{:S(2)}) collective-permute-start(f32[300,2,120]{2,1,0:T(2,128)} %shard_map.55.own_ref), channel_id=1, source_target_pairs={{0,8},{2,10},{4,12},{6,14},{8,0},{10,2},{12,4},{14,6},{16,24},{18,... | collective-permute-start | bytes 864008 | tf_op jit(solution)/shard_map/ppermute | solution.py:409
  23.7 2.3 %collective-permute-start.3 = (f32[300,2,120]{2,1,0:T(2,128)S(1)}, f32[300,2,120]{2,1,0:T(2,128)S(1)}, u32[]{:S(2)}, u32[]{:S(2)}) collective-permute-start(f32[300,2,120]{2,1,0:T(2,128)S(1)} %bitcast.14), channel_id=1, source_target_pairs={{0,1},{1,0},{2,3},{3,2},{4,5},{5,4},{6,7},{7,6},{8,9},{9,8},{10,11... | collective-permute-start | bytes 864008 | tf_op jit(solution)/shard_map/ppermute | solution.py:413
  25.0 1.1 %copy-start.5 = (f32[1,2,300,120]{3,1,2,0:T(2,128)S(1)}, f32[1,2,300,120]{3,1,2,0:T(2,128)}, u32[]{:S(2)}) copy-start(f32[1,2,300,120]{3,1,2,0:T(2,128)} %param.8) | copy-start | bytes 864004
  26.0 6.9 %copy-start.2 = (s32[3,16]{1,0:T(4,128)S(1)}, s32[3,16]{1,0:T(4,128)}, u32[]{:S(2)}) copy-start(s32[3,16]{1,0:T(4,128)} %offset_ref.1) | copy-start | bytes 580
  34.5 6.9 %collective-permute-start.6 = (f32[4,16,640]{2,1,0:T(8,128)S(1)}, f32[4,16,640]{2,1,0:T(8,128)S(1)}, u32[]{:S(2)}, u32[]{:S(2)}) collective-permute-start(f32[4,16,640]{2,1,0:T(8,128)S(1)} %get-tuple-element.26), channel_id=1, source_target_pairs={{0,2},{2,0},{4,6},{6,4},{8,10},{10,8},{12,14},{14,12},{16,18},{18,... | collective-permute-start | bytes 491528 | tf_op jit(solution)/shard_map/ppermute | solution.py:409
  35.4 10.0 %collective-permute-start.7 = (f32[4,16,640]{2,1,0:T(8,128)}, f32[4,16,640]{2,1,0:T(8,128)S(1)}, u32[]{:S(2)}, u32[]{:S(2)}) collective-permute-start(f32[4,16,640]{2,1,0:T(8,128)} %get-tuple-element.27), channel_id=1, source_target_pairs={{0,4},{2,6},{4,0},{6,2},{8,12},{10,14},{12,8},{14,10},{16,20},{18,... | collective-permute-start | bytes 491528 | tf_op jit(solution)/shard_map/ppermute | solution.py:409
  37.4 7.9 %collective-permute-start.8 = (f32[4,16,640]{2,1,0:T(8,128)}, f32[4,16,640]{2,1,0:T(8,128)S(1)}, u32[]{:S(2)}, u32[]{:S(2)}) collective-permute-start(f32[4,16,640]{2,1,0:T(8,128)} %get-tuple-element.28), channel_id=1, source_target_pairs={{0,6},{2,4},{4,2},{6,0},{8,14},{10,12},{12,10},{14,8},{16,22},{18,... | collective-permute-start | bytes 491528 | tf_op jit(solution)/shard_map/ppermute | solution.py:409
  38.4 3.7 %collective-permute-start.9 = (f32[300,2,120]{2,1,0:T(2,128)S(1)}, f32[300,2,120]{2,1,0:T(2,128)S(1)}, u32[]{:S(2)}, u32[]{:S(2)}) collective-permute-start(f32[300,2,120]{2,1,0:T(2,128)S(1)} %collective-permute-done.1.own_ref), channel_id=1, source_target_pairs={{0,1},{1,0},{2,3},{3,2},{4,5},{5,4},{6,7},{7,6},{8,9},{9,8},{10,11... | collective-permute-start | bytes 864008 | tf_op jit(solution)/shard_map/ppermute | solution.py:413
  41.4 0.7 %copy-start = (f32[4,16,640]{2,1,0:T(8,128)}, f32[4,16,640]{2,1,0:T(8,128)S(1)}, u32[]{:S(2)}) copy-start(f32[4,16,640]{2,1,0:T(8,128)S(1)} %collective-permute-done.6.in_ref) | copy-start | bytes 491524
  42.1 15.4 %copy-start.3 = (s32[16]{0:T(128)S(1)}, s32[16]{0:T(128)}, u32[]{:S(2)}) copy-start(s32[16]{0:T(128)} %transfer_ref.1) | copy-start | bytes 196
  45.4 0.9 %copy-start.1 = (f32[4,16,640]{2,1,0:T(8,128)S(1)}, f32[4,16,640]{2,1,0:T(8,128)}, u32[]{:S(2)}) copy-start(f32[4,16,640]{2,1,0:T(8,128)} %shard_map.62.refs_1_) | copy-start | bytes 491524
  48.2 5.8 %collective-permute-start.10 = (f32[4,8,8,128]{3,2,1,0:T(8,128)S(1)}, f32[4,8,8,128]{3,2,1,0:T(8,128)S(1)}, u32[]{:S(2)}, u32[]{:S(2)}) collective-permute-start(f32[4,8,8,128]{3,2,1,0:T(8,128)S(1)} %get-tuple-element.34), channel_id=1, source_target_pairs={{0,2},{2,0},{4,6},{6,4},{8,10},{10,8},{12,14},{14,12},{16,18},{18,... | collective-permute-start | bytes 393224 | tf_op jit(solution)/shard_map/ppermute | solution.py:409
  49.7 7.8 %collective-permute-start.11 = (f32[4,8,8,128]{3,2,1,0:T(8,128)S(1)}, f32[4,8,8,128]{3,2,1,0:T(8,128)S(1)}, u32[]{:S(2)}, u32[]{:S(2)}) collective-permute-start(f32[4,8,8,128]{3,2,1,0:T(8,128)S(1)} %get-tuple-element.35), channel_id=1, source_target_pairs={{0,4},{2,6},{4,0},{6,2},{8,12},{10,14},{12,8},{14,10},{16,20},{18,... | collective-permute-start | bytes 393224 | tf_op jit(solution)/shard_map/ppermute | solution.py:409
  51.5 6.0 %collective-permute-start.12 = (f32[4,8,8,128]{3,2,1,0:T(8,128)S(1)}, f32[4,8,8,128]{3,2,1,0:T(8,128)S(1)}, u32[]{:S(2)}, u32[]{:S(2)}) collective-permute-start(f32[4,8,8,128]{3,2,1,0:T(8,128)S(1)} %get-tuple-element.36), channel_id=1, source_target_pairs={{0,6},{2,4},{4,2},{6,0},{8,14},{10,12},{12,10},{14,8},{16,22},{18,... | collective-permute-start | bytes 393224 | tf_op jit(solution)/shard_map/ppermute | solution.py:409

commit v3 on v2

--- a/solution.py
+++ b/solution.py
@@ -12,6 +12,10 @@
 KY = 4
 LANES = 128
 HALF_LANES = 64
+SEGMENT = 32
+PIECE = 4
+SUBLANES = 8
+SEGMENTS = LANES // SEGMENT
 BF16 = jnp.bfloat16
 F32 = jnp.float32
 
@@ -85,10 +89,6 @@
     return jnp.dot(left, right, preferred_element_type=F32)
 
 
-def padded(count, step):
-    return -(-count // step) * step
-
-
 class Sizes:
     def __init__(self, blocks, occ_coeff, vir_coeff):
         self.slab = blocks.shape[1]
@@ -97,10 +97,12 @@
         self.vir_half = vir_coeff.shape[3]
         self.main = self.basis // LANES * LANES
         self.rest = self.basis - self.main
-        self.width = 2 * self.main + LANES
-        self.depth = self.main + HALF_LANES
+        self.columns = self.main // LANES
+        self.gap = HALF_LANES - self.rest
+        self.depth = 2 * self.main + 3 * HALF_LANES
         self.bands = self.occ // KX
-        self.rows = padded(self.bands, 8)
+        self.rows = 2 * SUBLANES
+        self.tail = 4 * self.columns
         self.chunk = self.vir_half // 2
         self.chunks = 4 * self.bands // KY
         self.tiles = self.chunks // 2 + 1
@@ -115,14 +117,23 @@
             and blocks.shape[1] == KY
             and occ % KX == 0
             and occ // KX % 2 == 1
-            and 0 < basis % LANES <= HALF_LANES
             and basis > LANES
+            and HALF_LANES // 2 <= basis % LANES <= HALF_LANES // 2 + SEGMENT // 2
+            and SUBLANES <= occ // KX < 2 * SUBLANES
+            and occ // KX - SUBLANES <= basis // LANES * (LANES // SEGMENT)
             and half % 2 == 0
             and HALF_LANES - 8 < half // 2 <= HALF_LANES
         )
 
 
-def half_kernel(sz, block_hbm, occ_hbm, out_ref, block_ref, occ_ref, block_sem, occ_sem):
+def staggered(tile, row, first, stride):
+    out = pltpu.roll(tile, first % LANES, 1)
+    for r in range(1, SEGMENTS):
+        out = jnp.where(row % SEGMENTS == r, pltpu.roll(tile, (first + r * stride) % LANES, 1), out)
+    return out
+
+
+def half_kernel(sz, block_hbm, occ_hbm, out_hbm, block_ref, occ_ref, out_ref, block_sem, occ_sem, out_sem):
     count = KX * sz.rows
     occ_copy = pltpu.make_async_copy(occ_hbm, occ_ref, occ_sem)
     block_copy = pltpu.make_async_copy(block_hbm, block_ref, block_sem)
@@ -136,32 +147,52 @@
     terms = [split(occ_ref[:, part]) for part in range(2)]
     left_high = jnp.concatenate([dot(pick, terms[0][0]), -dot(pick, terms[1][0])], axis=0).astype(BF16)
     left_low = jnp.concatenate([dot(pick, terms[0][1]), -dot(pick, terms[1][1])], axis=0).astype(BF16)
+    left = jnp.concatenate([left_high, left_low], axis=0)
     fill = jnp.zeros((sz.basis, LANES - sz.rest), F32)
+    row = lax.broadcasted_iota(jnp.int32, (SUBLANES, LANES), 0)
+    lane = lax.broadcasted_iota(jnp.int32, (SUBLANES, LANES), 1)
     block_copy.wait()
     for p in range(sz.slab):
         high, low = split(jnp.concatenate([block_ref[:, p], fill], axis=1))
-        half = dot(left_high, high) + dot(left_low, high) + dot(left_high, low)
+        half = dot(left, high)
+        half = half[: 2 * count] + half[2 * count :] + dot(left_high, low)
         real, imag = half[:count], half[count:]
-        rest = real[:, sz.main :] + pltpu.roll(imag[:, sz.main :], HALF_LANES, 1)
         for z in range(KX):
-            span = slice(z * sz.rows, (z + 1) * sz.rows)
-            out_ref[z, p, :, : sz.main] = real[span, : sz.main]
-            out_ref[z, p, :, sz.main : 2 * sz.main] = imag[span, : sz.main]
-            out_ref[z, p, :, 2 * sz.main :] = rest[span]
+            near = slice(z * sz.rows, z * sz.rows + SUBLANES)
+            far = slice(z * sz.rows + SUBLANES, (z + 1) * sz.rows)
+            tails = []
+            for part, value in enumerate((real, imag)):
+                head, last = value[near, sz.main :], value[far, sz.main :]
+                tails.append(head + pltpu.roll(jnp.where(lane < sz.gap, last, 0.0), sz.rest, 1))
+                spare = jnp.where(lane < sz.gap, 0.0, last)
+                spare = staggered(spare, row, LANES - sz.gap, SEGMENT)
+                for c in range(sz.columns):
+                    lanes = slice(c * LANES, (c + 1) * LANES)
+                    rows = slice(c * SEGMENTS, (c + 1) * SEGMENTS)
+                    kept = jnp.sum(spare[rows], axis=0, keepdims=True)
+                    tile = part * sz.columns + c
+                    out_ref[z, p, tile] = value[near, lanes]
+                    out_ref[z, p, 2 * sz.columns + tile] = jnp.where(row == SUBLANES - 1, kept, value[far, lanes])
+            out_ref[z, p, sz.tail] = tails[0] + pltpu.roll(tails[1], HALF_LANES, 1)
+        pltpu.make_async_copy(out_ref.at[:, p], out_hbm.at[:, p], out_sem.at[p]).start()
+    for p in range(sz.slab):
+        pltpu.make_async_copy(out_ref.at[:, p], out_hbm.at[:, p], out_sem.at[p]).wait()
 
 
 def half_bands(sz, blocks, occ_coeff):
     anywhere = pl.BlockSpec(memory_space=pl.ANY)
     return pl.pallas_call(
         functools.partial(half_kernel, sz),
-        out_shape=jax.ShapeDtypeStruct((KX, KY, sz.rows, sz.width), F32),
+        out_shape=jax.ShapeDtypeStruct((KX, KY, sz.tail + 1, SUBLANES, LANES), F32),
         in_specs=[anywhere, anywhere],
-        out_specs=pl.BlockSpec(memory_space=pltpu.VMEM),
+        out_specs=anywhere,
         scratch_shapes=[
             pltpu.VMEM((sz.basis, sz.slab, sz.basis), F32),
             pltpu.VMEM((sz.occ, 2, sz.basis), F32),
+            pltpu.VMEM((KX, KY, sz.tail + 1, SUBLANES, LANES), F32),
             pltpu.SemaphoreType.DMA,
             pltpu.SemaphoreType.DMA,
+            pltpu.SemaphoreType.DMA((sz.slab,)),
         ],
         compiler_params=pltpu.CompilerParams(vmem_limit_bytes=60 << 20),
         cost_estimate=pl.CostEstimate(flops=10**10, bytes_accessed=60_000_000, transcendentals=0),
@@ -194,7 +225,7 @@
     for cell in range(KX * KY):
         slot_ref[(offset_ref[0, cell] & 3) * KY + (offset_ref[1, cell] & 3)] = cell
     slots = [slot_ref[n] for n in range(KX * KY)]
-    real_half = lax.broadcasted_iota(jnp.int32, (8, LANES), 1) < HALF_LANES
+    real_half = lax.broadcasted_iota(jnp.int32, (SUBLANES, LANES), 1) < HALF_LANES
 
     def turn_rest(value):
         moved = pltpu.roll(value, HALF_LANES, 1)
@@ -207,34 +238,33 @@
             for b in range(KY):
                 store(a, b, seconds[b])
 
-    for row in range(0, sz.rows, 8):
-        span = slice(row, row + 8)
-        for lane in range(0, sz.main, LANES):
-            near, far = slice(lane, lane + LANES), slice(sz.main + lane, sz.main + lane + LANES)
+    for h in range(2):
+        for c in range(sz.columns):
+            near = 2 * sz.columns * h + c
+            far = near + sz.columns
 
             def load(cell):
-                return Pair(cells_ref[cell, span, near], cells_ref[cell, span, far])
+                return Pair(cells_ref[cell, near], cells_ref[cell, far])
 
             def store(a, b, value):
-                grid_ref[b, a ^ plane, span, near] = value.real
-                grid_ref[b, a ^ plane, span, far] = value.imag
+                grid_ref[b, a ^ plane, near] = value.real
+                grid_ref[b, a ^ plane, far] = value.imag
 
             transform(load, Pair.turned, store)
-        tail = slice(2 * sz.main, sz.width)
-
-        def load_rest(cell):
-            return cells_ref[cell, span, tail]
-
-        def store_rest(a, b, value):
-            grid_ref[b, a ^ plane, span, tail] = value
-
-        transform(load_rest, turn_rest, store_rest)
+
+    def load_rest(cell):
+        return cells_ref[cell, sz.tail]
+
+    def store_rest(a, b, value):
+        grid_ref[b, a ^ plane, sz.tail] = value
+
+    transform(load_rest, turn_rest, store_rest)
     for step in range(KY):
         outs[step][...] = grid_ref[step ^ seat]
 
 
 def lattice_sum(sz, place, cell_offsets, cells):
-    shape = jax.ShapeDtypeStruct((KX, sz.rows, sz.width), F32)
+    shape = jax.ShapeDtypeStruct((KX, sz.tail + 1, SUBLANES, LANES), F32)
     whole = pl.BlockSpec(memory_space=pltpu.VMEM)
     scalars = pl.BlockSpec(memory_space=pltpu.SMEM)
     return pl.pallas_call(
@@ -243,7 +273,7 @@
         in_specs=[scalars, scalars, whole],
         out_specs=[whole] * KY,
         scratch_shapes=[
-            pltpu.VMEM((KY, KX, sz.rows, sz.width), F32),
+            pltpu.VMEM((KY, KX, sz.tail + 1, SUBLANES, LANES), F32),
             pltpu.SMEM((KX * KY,), jnp.int32),
         ],
         compiler_params=pltpu.CompilerParams(vmem_limit_bytes=32 << 20),
@@ -255,25 +285,40 @@
     left_ref, band_ref, tile_ref = refs[2 * KY + KX :]
     seat = place_ref[1]
     count = KY * sz.rows
+    row = lax.broadcasted_iota(jnp.int32, (SUBLANES, LANES), 0)
+    lane = lax.broadcasted_iota(jnp.int32, (SUBLANES, LANES), 1)
+    low_lanes = lax.broadcasted_iota(jnp.int32, (2 * count, LANES), 1) < HALF_LANES
     for step in range(KY):
         left_ref[:, step ^ seat] = halves[step][...]
 
     for k in range(KX):
-        left = left_ref[k].reshape(count, sz.width)
-        tail = left[:, 2 * sz.main :]
-        near = jnp.concatenate([left[:, : sz.main], left[:, sz.main : 2 * sz.main]], axis=0)
-        rest = jnp.concatenate([tail, pltpu.roll(tail, HALF_LANES, 1)], axis=0)[:, :HALF_LANES]
-        near_high, near_low = split(near)
-        rest_high, rest_low = split(rest)
-        high, low = rights[k][0], rights[k][1]
-        band = (
-            dot(near_high, high[: sz.main])
-            + dot(near_low, high[: sz.main])
-            + dot(near_high, low[: sz.main])
-            + dot(rest_high, high[sz.main :])
-            + dot(rest_low, high[sz.main :])
-            + dot(rest_high, low[sz.main :])
-        )
+        left = left_ref[k]
+        near, rest = [], []
+        for part in range(2):
+            tiles = []
+            for c in range(sz.columns):
+                first = part * sz.columns + c
+                halves_of = [left[:, first], left[:, 2 * sz.columns + first]]
+                tiles.append(jnp.stack(halves_of, axis=1).reshape(count, LANES))
+            near.append(jnp.concatenate(tiles, axis=1))
+            for p in range(KY):
+                tail = left[p, sz.tail]
+                head = pltpu.roll(tail, HALF_LANES, 1) if part else tail
+                kept = [left[p, 2 * sz.columns + part * sz.columns + c] for c in range(sz.columns)]
+                spare = jnp.concatenate(
+                    [jnp.broadcast_to(tile[SUBLANES - 1 :], (SEGMENTS, LANES)) for tile in kept], axis=0
+                )[:SUBLANES]
+                spare = staggered(spare, row, sz.gap, LANES - SEGMENT)
+                rest += [head, jnp.where(lane < sz.gap, pltpu.roll(head, LANES - sz.rest, 1), spare)]
+        near_high, near_low = split(jnp.concatenate(near, axis=0))
+        rest_high = jnp.concatenate(rest, axis=0)
+        rest_low = rest_high - rest_high.astype(BF16).astype(F32)
+        both = jnp.where(low_lanes, rest_high, pltpu.roll(rest_low, HALF_LANES, 1)).astype(BF16)
+        rest_three = jnp.concatenate([both, rest_high.astype(BF16)[:, :HALF_LANES]], axis=1)
+        right = rights[k]
+        band = dot(jnp.concatenate([near_high, near_low], axis=0), right[: sz.main])
+        band = band[: 2 * count] + band[2 * count :]
+        band += dot(near_high, right[sz.main : 2 * sz.main]) + dot(rest_three, right[2 * sz.main :])
         width = 2 * LANES
         top, bottom = band[:count], band[count:]
         real = top[:, :width] - bottom[:, width:]
@@ -304,7 +349,7 @@
         in_specs=[scalars] + [whole] * (KY + KX),
         out_specs=[whole] * KY,
         scratch_shapes=[
-            pltpu.VMEM((KX, KY, sz.rows, sz.width), F32),
+            pltpu.VMEM((KX, KY, sz.tail + 1, SUBLANES, LANES), F32),
             pltpu.VMEM((2, 2, KY * sz.rows, LANES), F32),
             pltpu.VMEM((2 * sz.bands, 2 * KY, LANES), F32),
         ],
@@ -313,25 +358,37 @@
 
 
 def regroup_kernel(sz, place_ref, transfer_ref, *refs):
-    sources, out_ref, row_ref = refs[:KY], refs[KY], refs[KY + 1]
+    sources, out_hbm = refs[:KY], refs[KY]
+    row_ref, out_ref, sems = refs[KY + 1 :]
     plane, seat = place_ref[0], place_ref[1]
     lane = lax.broadcasted_iota(jnp.int32, (2 * KY, LANES), 1)
     cells = KX * KY
+    starts = list(range(0, sz.pairs, LANES))
+    pieces = [starts[i : i + PIECE] for i in range(0, len(starts), PIECE)]
+    targets = [
+        transfer_ref[(k ^ plane) * KY + (step ^ seat)] for step in range(KY) for k in range(KX)
+    ]
+
+    def piece_copy(index):
+        first = pieces[index][0]
+        span = pl.ds(first, min(pieces[index][-1] + LANES, sz.pairs) - first)
+        return pltpu.make_async_copy(out_ref.at[:, span], out_hbm.at[:, span], sems.at[index])
 
     def place_rows(odd):
-        for step in range(KY):
-            for k in range(KX):
-                point = (k ^ plane) * KY + (step ^ seat)
-                row = transfer_ref[point]
-                for first in range(0, sz.pairs, LANES):
-                    last = min(first + LANES, sz.pairs)
+        for index, piece in enumerate(pieces):
+            for first in piece:
+                last = min(first + LANES, sz.pairs)
+                for source, row in enumerate(targets):
+                    step, k = divmod(source, KX)
                     value = None
                     for u in range(first // sz.chunk, (last - 1) // sz.chunk + 1):
                         tile = sources[step][k, (u + odd) // 2]
                         shift = (sz.chunk * u - HALF_LANES * (u + odd)) % LANES
-                        piece = pltpu.roll(tile, shift, 1) if shift else tile
-                        value = piece if value is None else jnp.where(lane < sz.chunk * u - first, value, piece)
+                        moved = pltpu.roll(tile, shift, 1) if shift else tile
+                        value = moved if value is None else jnp.where(lane < sz.chunk * u - first, value, moved)
                     row_ref[first // LANES, pl.ds(row, 2 * KY, stride=cells)] = value
+                out_ref[:, first:last] = row_ref[first // LANES, :, : last - first]
+            piece_copy(index).start()
 
     @pl.when(seat % 2 == 0)
     def _():
@@ -341,40 +398,62 @@
     def _():
         place_rows(1)
 
-    for first in range(0, sz.pairs, LANES):
-        last = min(first + LANES, sz.pairs)
-        out_ref[:, first:last] = row_ref[first // LANES, :, : last - first]
+    for index in range(len(pieces)):
+        piece_copy(index).wait()
 
 
 def regroup(sz, place, transfer_index, sources):
     whole = pl.BlockSpec(memory_space=pltpu.VMEM)
     scalars = pl.BlockSpec(memory_space=pltpu.SMEM)
+    rows = 2 * KY * KX * KY
+    tiles = -(-sz.pairs // LANES)
     return pl.pallas_call(
         functools.partial(regroup_kernel, sz),
-        out_shape=jax.ShapeDtypeStruct((2 * KY * KX * KY, sz.pairs), F32),
+        out_shape=jax.ShapeDtypeStruct((rows, sz.pairs), F32),
         in_specs=[scalars, scalars] + [whole] * KY,
-        out_specs=whole,
-        scratch_shapes=[pltpu.VMEM((-(-sz.pairs // LANES), 2 * KY * KX * KY, LANES), F32)],
+        out_specs=pl.BlockSpec(memory_space=pl.ANY),
+        scratch_shapes=[
+            pltpu.VMEM((tiles, rows, LANES), F32),
+            pltpu.VMEM((rows, sz.pairs), F32),
+            pltpu.SemaphoreType.DMA((-(-tiles // PIECE),)),
+        ],
         compiler_params=pltpu.CompilerParams(vmem_limit_bytes=32 << 20),
     )(place, transfer_index, *sources)
 
 
+def spread_kernel(sz, in_ref, out_ref):
+    low_lanes = lax.broadcasted_iota(jnp.int32, (sz.basis, LANES), 1) < HALF_LANES
+    fill = jnp.zeros((sz.basis, LANES - sz.vir_half), F32)
+    for part in range(2):
+        value = jnp.concatenate([in_ref[:, part], fill], axis=1)
+        out_ref[part] = jnp.where(low_lanes, value, pltpu.roll(value, HALF_LANES - sz.chunk, 1))
+
+
+def spread(sz, value, flops):
+    whole = pl.BlockSpec(memory_space=pltpu.VMEM)
+    return pl.pallas_call(
+        functools.partial(spread_kernel, sz),
+        out_shape=jax.ShapeDtypeStruct((2, sz.basis, LANES), F32),
+        in_specs=[whole],
+        out_specs=whole,
+        compiler_params=pltpu.CompilerParams(vmem_limit_bytes=32 << 20),
+        cost_estimate=pl.CostEstimate(flops=flops, bytes_accessed=flops // 100, transcendentals=0),
+    )(value)
+
+
 def columns_kernel(sz, place_ref, own_ref, other_ref, out_ref):
     core = place_ref[2]
-    low_lanes = lax.broadcasted_iota(jnp.int32, (sz.basis, LANES), 1) < HALF_LANES
-    fill = jnp.zeros((sz.basis, LANES - sz.vir_half), F32)
-    under = jnp.zeros((sz.depth - sz.basis, LANES), F32)
+    under = jnp.zeros((sz.gap, LANES), F32)
     for part in range(2):
-        sides = []
-        for ref in (own_ref, other_ref):
-            value = jnp.concatenate([ref[:, part], fill], axis=1)
-            value = jnp.where(low_lanes, value, pltpu.roll(value, HALF_LANES - sz.chunk, 1))
-            sides.append(jnp.concatenate([value, under], axis=0))
-        mine, theirs = sides
+        mine, theirs = [jnp.concatenate([ref[part], under], axis=0) for ref in (own_ref, other_ref)]
         for h, value in enumerate([jnp.where(core == 0, mine, theirs), jnp.where(core == 0, theirs, mine)]):
             lanes = slice((2 * part + h) * LANES, (2 * part + h + 1) * LANES)
-            for level, term in enumerate(split(value)):
-                out_ref[level, :, lanes] = term
+            high, low = split(value)
+            out_ref[: sz.main, lanes] = high[: sz.main]
+            out_ref[sz.main : 2 * sz.main, lanes] = low[: sz.main]
+            for place, term in enumerate((high, high, low)):
+                first = 2 * sz.main + place * HALF_LANES
+                out_ref[first : first + HALF_LANES, lanes] = term[sz.main :]
 
 
 def columns(sz, place, own, other, flops):
@@ -382,7 +461,7 @@
     scalars = pl.BlockSpec(memory_space=pltpu.SMEM)
     return pl.pallas_call(
         functools.partial(columns_kernel, sz),
-        out_shape=jax.ShapeDtypeStruct((2, sz.depth, 4 * LANES), BF16),
+        out_shape=jax.ShapeDtypeStruct((sz.depth, 4 * LANES), BF16),
         in_specs=[scalars, whole, whole],
         out_specs=whole,
         compiler_params=pltpu.CompilerParams(vmem_limit_bytes=32 << 20),
@@ -390,21 +469,6 @@
     )(place, own, other)
 
 
-def hold_kernel(in_ref, out_ref):
-    del in_ref, out_ref
-
-
-def hold(value):
-    return pl.pallas_call(
-        hold_kernel,
-        out_shape=jax.ShapeDtypeStruct(value.shape, value.dtype),
-        in_specs=[pl.BlockSpec(memory_space=pl.ANY)],
-        out_specs=pl.BlockSpec(memory_space=pl.ANY),
-        input_output_aliases={0: 0},
-        cost_estimate=pl.CostEstimate(flops=10**10, bytes_accessed=10**8, transcendentals=0),
-    )(value)
-
-
 def swap(value, step):
     return lax.ppermute(value, "cell", [(d, d ^ step) for d in range(KX * KY)])
 
@@ -417,25 +481,18 @@
     sz = Sizes(blocks, occ_coeff, vir_coeff)
     me = lax.axis_index("cell")
     place = jnp.stack([me // KY, me % KY, lax.axis_index("aux")]).astype(jnp.int32)
+    long, short = 10**10, 10**6
     home = vir_coeff[0].transpose(1, 0, 2)
-    across = hold(swap(home, 2 * KY))
-    beside = hold(swap(home, KY))
-    sent = half_bands(sz, blocks, occ_coeff).reshape(KX * KY, sz.rows, sz.width)
+    across = spread(sz, swap(home, 2 * KY), long)
+    beside = spread(sz, swap(home, KY), long)
+    corner = swap(across, KY)
+    ours = spread(sz, home, short)
+    rights = [columns(sz, place, v, swap_cores(v), short) for v in (ours, beside, across)]
+    sent = half_bands(sz, blocks, occ_coeff).reshape(KX * KY, sz.tail + 1, SUBLANES, LANES)
     cells = lax.all_to_all(sent, "cell", split_axis=0, concat_axis=0, tiled=True)
-    corner = swap(across, KY)
-    ours, beside = lax.optimization_barrier((home, beside))
-    long, short = 10**10, 10**6
-    rights = [
-        columns(sz, place, ours, swap_cores(ours), long),
-        columns(sz, place, beside, swap_cores(beside), long),
-        columns(sz, place, across, swap_cores(across), long),
-    ]
-    cells, *rights = lax.optimization_barrier((cells, *rights))
     points = list(lattice_sum(sz, place, cell_offsets, cells))
-    corner, points[0] = lax.optimization_barrier((corner, points[0]))
     rights.append(columns(sz, place, corner, swap_cores(corner), short))
     halves = [points[0]] + [swap(points[s], s) for s in range(1, KY)]
-    halves[1] = hold(halves[1])
     bands = band_product(sz, place, halves, rights)
     sources = [bands[0]] + [swap(bands[s], s) for s in range(1, KY)]
     out = regroup(sz, place, transfer_index, sources)

time: 59.6 us -> 58.8 us (0.987)
  waiting for transfers between devices: 25.6 us -> 27.9 us
  local copies, waits for them, and re-layouts: 3.04 us -> 1.01 us
  Pallas kernels: 13 us -> 11.2 us
  starting transfers between devices: 17.5 us -> 18.1 us
    ppermute x9, waiting for transfers between devices: 19.8 us -> 27.9 us  [swap(): return lax.ppermute(value, 'cell', [(d, d ^ step) for d in range(KX * KY)])]
    all_to_all x1, waiting for transfers between devices: 5.84 us -> 0.01 us  [by_planes(): lax.all_to_all(sent, 'cell', split_axis=0, concat_axis=0, tiled=True)]
    unnamed x20 -> x6, local copies, waits for them, and re-layouts: 3.04 us -> 1.01 us
    pallas_call x4, Pallas kernels: 4.06 us -> 2.79 us  [columns(): pl.pallas_call(functools.partial(columns_kernel, sz), out_shape=jax.Shape...]
    pallas_call x1, Pallas kernels: 1.57 us -> 0.82 us  [lattice_sum(): pl.pallas_call(functools.partial(lattice_kernel, sz), out_shape=[shape] *...]
    pallas_call x3, Pallas kernels: 0.01 us -> 0.72 us  [spread(): pl.pallas_call(functools.partial(spread_kernel, sz), out_shape=jax.ShapeD...]
  transfers between devices with their start and end apart: 14 -> 14, of which waited for: 8 -> 7; matrix products, arithmetic and copies ran while one was open for 0% -> 0% of each run, Pallas kernels for 16% -> 14%
where the time goes in v3:
time: 58.8 us; the launch traced here: 58.5 us
  waiting for transfers between devices  27.9 us (47%)
  starting transfers between devices  18.1 us (31%)
  Pallas kernels  11.2 us (19%)
  local copies, waits for them, and re-layouts  1.01 us (2%)
    ppermute x9, waiting for transfers between devices, swap(): return lax.ppermute(value, 'cell', [(d, d ^ step) for d in range(KX * KY)])  27.9 us
    ppermute x9, starting transfers between devices, swap(): return lax.ppermute(value, 'cell', [(d, d ^ step) for d in range(KX * KY)])  13.6 us
    all_to_all x1, starting transfers between devices, by_planes(): lax.all_to_all(sent, 'cell', split_axis=0, concat_axis=0, tiled=True)  3.84 us
    pallas_call x1, Pallas kernels, half_bands(): pl.pallas_call(functools.partial(half_kernel, sz), out_shape=jax.ShapeDty...  3.57 us
    pallas_call x4, Pallas kernels, columns(): pl.pallas_call(functools.partial(columns_kernel, sz), out_shape=jax.Shape...  2.79 us
    pallas_call x1, Pallas kernels, regroup(): pl.pallas_call(functools.partial(regroup_kernel, sz), out_shape=jax.Shape...  1.76 us
    pallas_call x1, Pallas kernels, band_product(): pl.pallas_call(functools.partial(band_kernel, sz), out_shape=[shape] * KY...  1.58 us
  transfers between devices with their start and end apart: 14, of which 7 were waited for; matrix products, arithmetic and copies ran while one was open for 0% of the time, Pallas kernels for 14%

profile of v3, /device:TPU:0, one launch (start us, length us, event | category | flops | bytes accessed | tf_op | source)
XLA Modules:
  0.0 58.5 jit_solution(5695878299536128451)
XLA Ops:
  0.0 4.0 %collective-permute-start.6 = (f32[300,2,120]{2,1,0:T(2,128)}, f32[300,2,120]{2,1,0:T(2,128)S(1)}, u32[]{:S(2)}, u32[]{:S(2)}) collective-permute-start(f32[300,2,120]{2,1,0:T(2,128)} %bitcast.12), channel_id=1, source_target_pairs={{0,16},{2,18},{4,20},{6,22},{8,24},{10,26},{12,28},{14,30},{16,0},... | collective-permute-start | bytes 864008 | tf_op jit(solution)/shard_map/ppermute | solution.py:473
  4.0 1.6 %collective-permute-start.4 = (f32[300,2,120]{2,1,0:T(2,128)}, f32[300,2,120]{2,1,0:T(2,128)S(1)}, u32[]{:S(2)}, u32[]{:S(2)}) collective-permute-start(f32[300,2,120]{2,1,0:T(2,128)} %bitcast.13), channel_id=1, source_target_pairs={{0,8},{2,10},{4,12},{6,14},{8,0},{10,2},{12,4},{14,6},{16,24},{18,... | collective-permute-start | bytes 864008 | tf_op jit(solution)/shard_map/ppermute | solution.py:473
  5.6 1.0 %copy-done = f32[1,2,300,120]{3,1,2,0:T(2,128)S(1)} copy-done((f32[1,2,300,120]{3,1,2,0:T(2,128)S(1)}, f32[1,2,300,120]{3,1,2,0:T(2,128)}, u32[]{:S(2)}) %copy-start) | copy-done | bytes 288024
  6.6 0.2 shard_map.57.own_ref
  6.9 3.6 %shard_map.55 = f32[4,4,9,8,128]{4,3,2,1,0:T(8,128)} custom-call(f32[300,4,300]{2,1,0:T(4,128)} %bitcast.16, f32[60,2,300]{2,1,0:T(2,128)} %bitcast.17), custom_call_target="tpu_custom_call" | custom-call | flops 10000000000 | bytes 60000000 | tf_op jit(solution)/shard_map/pallas_call | solution.py:184
  10.5 3.8 %all-to-all-start = ((f32[16,9,8,128]{3,2,1,0:T(8,128)}), f32[16,9,8,128]{3,2,1,0:T(8,128)S(1)}, u32[]{:S(2)}, u32[]{:S(2)}) async-start(f32[16,9,8,128]{3,2,1,0:T(8,128)} %bitcast.15), calls=%async_computation | async-start | bytes 1179648 | tf_op jit(solution)/shard_map/all_to_all | solution.py:492
  14.4 3.8 %collective-permute-done.6.in_ref = f32[300,2,120]{2,1,0:T(2,128)S(1)} collective-permute-done((f32[300,2,120]{2,1,0:T(2,128)}, f32[300,2,120]{2,1,0:T(2,128)S(1)}, u32[]{:S(2)}, u32[]{:S(2)}) %collective-permute-start.6) | collective-permute-done | bytes 288032 | tf_op jit(solution)/shard_map/ppermute | solution.py:473
  18.2 0.2 shard_map.61.own_ref
  18.5 0.9 %collective-permute-start.8 = (f32[2,300,128]{2,1,0:T(8,128)S(1)}, f32[2,300,128]{2,1,0:T(8,128)S(1)}, u32[]{:S(2)}, u32[]{:S(2)}) collective-permute-start(f32[2,300,128]{2,1,0:T(8,128)S(1)} %shard_map.61.own_ref), channel_id=1, source_target_pairs={{0,8},{2,10},{4,12},{6,14},{8,0},{10,2},{12,4},{14,6},{16,24},{18,... | collective-permute-start | bytes 921608 | tf_op jit(solution)/shard_map/ppermute | solution.py:473
  19.4 1.3 %collective-permute-done.4.in_ref = f32[300,2,120]{2,1,0:T(2,128)S(1)} collective-permute-done((f32[300,2,120]{2,1,0:T(2,128)}, f32[300,2,120]{2,1,0:T(2,128)S(1)}, u32[]{:S(2)}, u32[]{:S(2)}) %collective-permute-start.4) | collective-permute-done | bytes 288032 | tf_op jit(solution)/shard_map/ppermute | solution.py:473
  20.7 0.2 shard_map.59.own_ref
  21.0 0.1 collective-permute-start.5
  21.1 0.5 collective-permute-start.7
  21.5 13.0 %collective-permute-done.8.own_ref = f32[2,300,128]{2,1,0:T(8,128)S(1)} collective-permute-done((f32[2,300,128]{2,1,0:T(8,128)S(1)}, f32[2,300,128]{2,1,0:T(8,128)S(1)}, u32[]{:S(2)}, u32[]{:S(2)}) %collective-permute-start.8) | collective-permute-done | bytes 307232 | tf_op jit(solution)/shard_map/ppermute | solution.py:473
  34.5 0.1 pad_add_fusion.place_ref
  34.6 0.8 %shard_map.56 = (f32[4,9,8,128]{3,2,1,0:T(8,128)S(1)}, f32[4,9,8,128]{3,2,1,0:T(8,128)S(1)}, f32[4,9,8,128]{3,2,1,0:T(8,128)S(1)}, f32[4,9,8,128]{3,2,1,0:T(8,128)S(1)}) custom-call(s32[3]{0:T(128)S(1)} %pad_add_fusion.place_ref, s32[3,16]{1,0:T(4,128)S(1)} %copy-done.1, f32[16,9,8,128]{3,2,1,0:T(8,128)S(1)} %all-to-all-done.cells_ref), custom_call_target="tpu_custom_call" | custom-call | tf_op jit(solution)/shard_map/pallas_call | solution.py:270
  35.5 1.6 %collective-permute-start = (f32[4,9,8,128]{3,2,1,0:T(8,128)S(1)}, f32[4,9,8,128]{3,2,1,0:T(8,128)S(1)}, u32[]{:S(2)}, u32[]{:S(2)}) collective-permute-start(f32[4,9,8,128]{3,2,1,0:T(8,128)S(1)} %get-tuple-element.14), channel_id=1, source_target_pairs={{0,2},{2,0},{4,6},{6,4},{8,10},{10,8},{12,14},{14,12},{16,18},{18,... | collective-permute-start | bytes 442376 | tf_op jit(solution)/shard_map/ppermute | solution.py:473
  37.1 1.5 %collective-permute-start.1 = (f32[4,9,8,128]{3,2,1,0:T(8,128)S(1)}, f32[4,9,8,128]{3,2,1,0:T(8,128)S(1)}, u32[]{:S(2)}, u32[]{:S(2)}) collective-permute-start(f32[4,9,8,128]{3,2,1,0:T(8,128)S(1)} %get-tuple-element.15), channel_id=1, source_target_pairs={{0,4},{2,6},{4,0},{6,2},{8,12},{10,14},{12,8},{14,10},{16,20},{18,... | collective-permute-start | bytes 442376 | tf_op jit(solution)/shard_map/ppermute | solution.py:473
  38.6 0.4 collective-permute-start.2
  39.0 0.7 %shard_map.58.refs_4_ = bf16[704,512]{1,0:T(8,128)(2,1)S(1)} custom-call(s32[3]{0:T(128)S(1)} %pad_add_fusion.place_ref, f32[2,300,128]{2,1,0:T(8,128)S(1)} %shard_map.57.own_ref, f32[2,300,128]{2,1,0:T(8,128)S(1)} %collective-permute-done.3.other_ref), custom_call_target="tpu_custom_call" | custom-call | flops 1000000 | bytes 10000 | tf_op jit(solution)/shard_map/pallas_call | solution.py:462
  39.7 0.7 %shard_map.60.refs_5_ = bf16[704,512]{1,0:T(8,128)(2,1)S(1)} custom-call(s32[3]{0:T(128)S(1)} %pad_add_fusion.place_ref, f32[2,300,128]{2,1,0:T(8,128)S(1)} %shard_map.59.own_ref, f32[2,300,128]{2,1,0:T(8,128)S(1)} %collective-permute-done.5.other_ref), custom_call_target="tpu_custom_call" | custom-call | flops 1000000 | bytes 10000 | tf_op jit(solution)/shard_map/pallas_call | solution.py:462
  40.4 0.7 %shard_map.62.refs_6_ = bf16[704,512]{1,0:T(8,128)(2,1)S(1)} custom-call(s32[3]{0:T(128)S(1)} %pad_add_fusion.place_ref, f32[2,300,128]{2,1,0:T(8,128)S(1)} %shard_map.61.own_ref, f32[2,300,128]{2,1,0:T(8,128)S(1)} %collective-permute-done.7.other_ref), custom_call_target="tpu_custom_call" | custom-call | flops 1000000 | bytes 10000 | tf_op jit(solution)/shard_map/pallas_call | solution.py:462
  41.2 0.7 %shard_map.63.refs_7_ = bf16[704,512]{1,0:T(8,128)(2,1)S(1)} custom-call(s32[3]{0:T(128)S(1)} %pad_add_fusion.place_ref, f32[2,300,128]{2,1,0:T(8,128)S(1)} %collective-permute-done.8.own_ref, f32[2,300,128]{2,1,0:T(8,128)S(1)} %collective-permute-done.9.other_ref), custom_call_target="tpu_custom_call" | custom-call | flops 1000000 | bytes 10000 | tf_op jit(solution)/shard_map/pallas_call | solution.py:462
  41.9 0.3 collective-permute-done.refs_1_
  42.2 4.0 %collective-permute-done.1.refs_2_ = f32[4,9,8,128]{3,2,1,0:T(8,128)S(1)} collective-permute-done((f32[4,9,8,128]{3,2,1,0:T(8,128)S(1)}, f32[4,9,8,128]{3,2,1,0:T(8,128)S(1)}, u32[]{:S(2)}, u32[]{:S(2)}) %collective-permute-start.1) | collective-permute-done | bytes 147488 | tf_op jit(solution)/shard_map/ppermute | solution.py:473
  46.2 1.6 %shard_map.64 = (f32[4,8,8,128]{3,2,1,0:T(8,128)S(1)}, f32[4,8,8,128]{3,2,1,0:T(8,128)S(1)}, f32[4,8,8,128]{3,2,1,0:T(8,128)S(1)}, f32[4,8,8,128]{3,2,1,0:T(8,128)S(1)}) custom-call(s32[3]{0:T(128)S(1)} %pad_add_fusion.place_ref, f32[4,9,8,128]{3,2,1,0:T(8,128)S(1)} %get-tuple-element.13.refs_0_, f32[4,9,8,128]{3,2,1,0:T(8,128)S(1)} %collective-permute-done.refs_1_, ...), custom_call_target="tpu_custom_call" | custom-call | tf_op jit(solution)/shard_map/pallas_call | solution.py:346
  47.8 1.3 %collective-permute-start.10 = (f32[4,8,8,128]{3,2,1,0:T(8,128)S(1)}, f32[4,8,8,128]{3,2,1,0:T(8,128)S(1)}, u32[]{:S(2)}, u32[]{:S(2)}) collective-permute-start(f32[4,8,8,128]{3,2,1,0:T(8,128)S(1)} %get-tuple-element.18), channel_id=1, source_target_pairs={{0,2},{2,0},{4,6},{6,4},{8,10},{10,8},{12,14},{14,12},{16,18},{18,... | collective-permute-start | bytes 393224 | tf_op jit(solution)/shard_map/ppermute | solution.py:473
  49.1 0.8 %collective-permute-start.11 = (f32[4,8,8,128]{3,2,1,0:T(8,128)S(1)}, f32[4,8,8,128]{3,2,1,0:T(8,128)S(1)}, u32[]{:S(2)}, u32[]{:S(2)}) collective-permute-start(f32[4,8,8,128]{3,2,1,0:T(8,128)S(1)} %get-tuple-element.19), channel_id=1, source_target_pairs={{0,4},{2,6},{4,0},{6,2},{8,12},{10,14},{12,8},{14,10},{16,20},{18,... | collective-permute-start | bytes 393224 | tf_op jit(solution)/shard_map/ppermute | solution.py:473
  49.9 1.4 %collective-permute-start.12 = (f32[4,8,8,128]{3,2,1,0:T(8,128)S(1)}, f32[4,8,8,128]{3,2,1,0:T(8,128)S(1)}, u32[]{:S(2)}, u32[]{:S(2)}) collective-permute-start(f32[4,8,8,128]{3,2,1,0:T(8,128)S(1)} %get-tuple-element.20), channel_id=1, source_target_pairs={{0,6},{2,4},{4,2},{6,0},{8,14},{10,12},{12,10},{14,8},{16,22},{18,... | collective-permute-start | bytes 393224 | tf_op jit(solution)/shard_map/ppermute | solution.py:473
  51.3 2.0 %collective-permute-done.10.refs_1_ = f32[4,8,8,128]{3,2,1,0:T(8,128)S(1)} collective-permute-done((f32[4,8,8,128]{3,2,1,0:T(8,128)S(1)}, f32[4,8,8,128]{3,2,1,0:T(8,128)S(1)}, u32[]{:S(2)}, u32[]{:S(2)}) %collective-permute-start.10) | collective-permute-done | bytes 131104 | tf_op jit(solution)/shard_map/ppermute | solution.py:473
  53.4 3.4 %collective-permute-done.11.refs_2_ = f32[4,8,8,128]{3,2,1,0:T(8,128)S(1)} collective-permute-done((f32[4,8,8,128]{3,2,1,0:T(8,128)S(1)}, f32[4,8,8,128]{3,2,1,0:T(8,128)S(1)}, u32[]{:S(2)}, u32[]{:S(2)}) %collective-permute-start.11) | collective-permute-done | bytes 131104 | tf_op jit(solution)/shard_map/ppermute | solution.py:473
  56.8 1.8 %shard_map.65 = f32[128,900]{1,0:T(8,128)} custom-call(s32[3]{0:T(128)S(1)} %pad_add_fusion.place_ref, s32[16]{0:T(128)S(1)} %copy-done.2, f32[4,8,8,128]{3,2,1,0:T(8,128)S(1)} %get-tuple-element.17.refs_0_, f32[4,8,8,128]{3,2,1,0:T(8,128)S(1)} %collective-permute-done.10.refs_1_, f32[4,8,8,128]{3,2,1,0:T(8,128)S(1)} %collective-permute-done.11.refs_2_, ...), custom_call_target="tpu_custom_call" | custom-call | tf_op jit(solution)/shard_map/pallas_call | solution.py:410
  (14 shorter events, 0.1 us)
Async XLA Ops:
  0.0 18.2 %collective-permute-start.6 = (f32[300,2,120]{2,1,0:T(2,128)}, f32[300,2,120]{2,1,0:T(2,128)S(1)}, u32[]{:S(2)}, u32[]{:S(2)}) collective-permute-start(f32[300,2,120]{2,1,0:T(2,128)} %bitcast.12), channel_id=1, source_target_pairs={{0,16},{2,18},{4,20},{6,22},{8,24},{10,26},{12,28},{14,30},{16,0},... | collective-permute-start | bytes 864008 | tf_op jit(solution)/shard_map/ppermute | solution.py:473
  4.0 16.7 %collective-permute-start.4 = (f32[300,2,120]{2,1,0:T(2,128)}, f32[300,2,120]{2,1,0:T(2,128)S(1)}, u32[]{:S(2)}, u32[]{:S(2)}) collective-permute-start(f32[300,2,120]{2,1,0:T(2,128)} %bitcast.13), channel_id=1, source_target_pairs={{0,8},{2,10},{4,12},{6,14},{8,0},{10,2},{12,4},{14,6},{16,24},{18,... | collective-permute-start | bytes 864008 | tf_op jit(solution)/shard_map/ppermute | solution.py:473
  5.6 1.0 %copy-start = (f32[1,2,300,120]{3,1,2,0:T(2,128)S(1)}, f32[1,2,300,120]{3,1,2,0:T(2,128)}, u32[]{:S(2)}) copy-start(f32[1,2,300,120]{3,1,2,0:T(2,128)} %param.8) | copy-start | bytes 864004
  6.9 30.2 %collective-permute-start.3 = (f32[2,300,128]{2,1,0:T(8,128)S(1)}, f32[2,300,128]{2,1,0:T(8,128)S(1)}, u32[]{:S(2)}, u32[]{:S(2)}) collective-permute-start(f32[2,300,128]{2,1,0:T(8,128)S(1)} %shard_map.57.own_ref), channel_id=1, source_target_pairs={{0,1},{1,0},{2,3},{3,2},{4,5},{5,4},{6,7},{7,6},{8,9},{9,8},{10,11... | collective-permute-start | bytes 921608 | tf_op jit(solution)/shard_map/ppermute | solution.py:477
  10.5 24.1 %all-to-all-start = ((f32[16,9,8,128]{3,2,1,0:T(8,128)}), f32[16,9,8,128]{3,2,1,0:T(8,128)S(1)}, u32[]{:S(2)}, u32[]{:S(2)}) async-start(f32[16,9,8,128]{3,2,1,0:T(8,128)} %bitcast.15), calls=%async_computation | async-start | bytes 1179648 | tf_op jit(solution)/shard_map/all_to_all | solution.py:492
  18.4 16.2 %copy-start.1 = (s32[3,16]{1,0:T(4,128)S(1)}, s32[3,16]{1,0:T(4,128)}, u32[]{:S(2)}) copy-start(s32[3,16]{1,0:T(4,128)} %offset_ref.1) | copy-start | bytes 580
  18.5 16.1 %collective-permute-start.8 = (f32[2,300,128]{2,1,0:T(8,128)S(1)}, f32[2,300,128]{2,1,0:T(8,128)S(1)}, u32[]{:S(2)}, u32[]{:S(2)}) collective-permute-start(f32[2,300,128]{2,1,0:T(8,128)S(1)} %shard_map.61.own_ref), channel_id=1, source_target_pairs={{0,8},{2,10},{4,12},{6,14},{8,0},{10,2},{12,4},{14,6},{16,24},{18,... | collective-permute-start | bytes 921608 | tf_op jit(solution)/shard_map/ppermute | solution.py:473
  21.0 17.6 %collective-permute-start.5 = (f32[2,300,128]{2,1,0:T(8,128)S(1)}, f32[2,300,128]{2,1,0:T(8,128)S(1)}, u32[]{:S(2)}, u32[]{:S(2)}) collective-permute-start(f32[2,300,128]{2,1,0:T(8,128)S(1)} %shard_map.59.own_ref), channel_id=1, source_target_pairs={{0,1},{1,0},{2,3},{3,2},{4,5},{5,4},{6,7},{7,6},{8,9},{9,8},{10,11... | collective-permute-start | bytes 921608 | tf_op jit(solution)/shard_map/ppermute | solution.py:477
  21.1 19.4 %collective-permute-start.7 = (f32[2,300,128]{2,1,0:T(8,128)S(1)}, f32[2,300,128]{2,1,0:T(8,128)S(1)}, u32[]{:S(2)}, u32[]{:S(2)}) collective-permute-start(f32[2,300,128]{2,1,0:T(8,128)S(1)} %shard_map.61.own_ref), channel_id=1, source_target_pairs={{0,1},{1,0},{2,3},{3,2},{4,5},{5,4},{6,7},{7,6},{8,9},{9,8},{10,11... | collective-permute-start | bytes 921608 | tf_op jit(solution)/shard_map/ppermute | solution.py:477
  34.5 6.6 %collective-permute-start.9 = (f32[2,300,128]{2,1,0:T(8,128)S(1)}, f32[2,300,128]{2,1,0:T(8,128)S(1)}, u32[]{:S(2)}, u32[]{:S(2)}) collective-permute-start(f32[2,300,128]{2,1,0:T(8,128)S(1)} %collective-permute-done.8.own_ref), channel_id=1, source_target_pairs={{0,1},{1,0},{2,3},{3,2},{4,5},{5,4},{6,7},{7,6},{8,9},{9,8},{10,11... | collective-permute-start | bytes 921608 | tf_op jit(solution)/shard_map/ppermute | solution.py:477
  35.5 6.7 %collective-permute-start = (f32[4,9,8,128]{3,2,1,0:T(8,128)S(1)}, f32[4,9,8,128]{3,2,1,0:T(8,128)S(1)}, u32[]{:S(2)}, u32[]{:S(2)}) collective-permute-start(f32[4,9,8,128]{3,2,1,0:T(8,128)S(1)} %get-tuple-element.14), channel_id=1, source_target_pairs={{0,2},{2,0},{4,6},{6,4},{8,10},{10,8},{12,14},{14,12},{16,18},{18,... | collective-permute-start | bytes 442376 | tf_op jit(solution)/shard_map/ppermute | solution.py:473
  37.1 9.1 %collective-permute-start.1 = (f32[4,9,8,128]{3,2,1,0:T(8,128)S(1)}, f32[4,9,8,128]{3,2,1,0:T(8,128)S(1)}, u32[]{:S(2)}, u32[]{:S(2)}) collective-permute-start(f32[4,9,8,128]{3,2,1,0:T(8,128)S(1)} %get-tuple-element.15), channel_id=1, source_target_pairs={{0,4},{2,6},{4,0},{6,2},{8,12},{10,14},{12,8},{14,10},{16,20},{18,... | collective-permute-start | bytes 442376 | tf_op jit(solution)/shard_map/ppermute | solution.py:473
  38.6 7.6 %collective-permute-start.2 = (f32[4,9,8,128]{3,2,1,0:T(8,128)S(1)}, f32[4,9,8,128]{3,2,1,0:T(8,128)S(1)}, u32[]{:S(2)}, u32[]{:S(2)}) collective-permute-start(f32[4,9,8,128]{3,2,1,0:T(8,128)S(1)} %get-tuple-element.16), channel_id=1, source_target_pairs={{0,6},{2,4},{4,2},{6,0},{8,14},{10,12},{12,10},{14,8},{16,22},{18,... | collective-permute-start | bytes 442376 | tf_op jit(solution)/shard_map/ppermute | solution.py:473
  41.9 14.9 %copy-start.2 = (s32[16]{0:T(128)S(1)}, s32[16]{0:T(128)}, u32[]{:S(2)}) copy-start(s32[16]{0:T(128)} %transfer_ref.1) | copy-start | bytes 196
  47.8 5.6 %collective-permute-start.10 = (f32[4,8,8,128]{3,2,1,0:T(8,128)S(1)}, f32[4,8,8,128]{3,2,1,0:T(8,128)S(1)}, u32[]{:S(2)}, u32[]{:S(2)}) collective-permute-start(f32[4,8,8,128]{3,2,1,0:T(8,128)S(1)} %get-tuple-element.18), channel_id=1, source_target_pairs={{0,2},{2,0},{4,6},{6,4},{8,10},{10,8},{12,14},{14,12},{16,18},{18,... | collective-permute-start | bytes 393224 | tf_op jit(solution)/shard_map/ppermute | solution.py:473
  49.1 7.7 %collective-permute-start.11 = (f32[4,8,8,128]{3,2,1,0:T(8,128)S(1)}, f32[4,8,8,128]{3,2,1,0:T(8,128)S(1)}, u32[]{:S(2)}, u32[]{:S(2)}) collective-permute-start(f32[4,8,8,128]{3,2,1,0:T(8,128)S(1)} %get-tuple-element.19), channel_id=1, source_target_pairs={{0,4},{2,6},{4,0},{6,2},{8,12},{10,14},{12,8},{14,10},{16,20},{18,... | collective-permute-start | bytes 393224 | tf_op jit(solution)/shard_map/ppermute | solution.py:473
  49.9 6.8 %collective-permute-start.12 = (f32[4,8,8,128]{3,2,1,0:T(8,128)S(1)}, f32[4,8,8,128]{3,2,1,0:T(8,128)S(1)}, u32[]{:S(2)}, u32[]{:S(2)}) collective-permute-start(f32[4,8,8,128]{3,2,1,0:T(8,128)S(1)} %get-tuple-element.20), channel_id=1, source_target_pairs={{0,6},{2,4},{4,2},{6,0},{8,14},{10,12},{12,10},{14,8},{16,22},{18,... | collective-permute-start | bytes 393224 | tf_op jit(solution)/shard_map/ppermute | solution.py:473

commit v4 on v3

--- a/solution.py
+++ b/solution.py
@@ -78,6 +78,10 @@
     regrouped = lax.all_to_all(pair_rows, "cell", split_axis=3, concat_axis=2, tiled=True)
     source = jnp.argsort(transfer_index)
     return jnp.take(regrouped, source, axis=2)
+
+
+def cost(flops):
+    return pl.CostEstimate(flops=flops, bytes_accessed=flops // 100, transcendentals=0)
 
 
 def split(value):
@@ -195,7 +199,7 @@
             pltpu.SemaphoreType.DMA((sz.slab,)),
         ],
         compiler_params=pltpu.CompilerParams(vmem_limit_bytes=60 << 20),
-        cost_estimate=pl.CostEstimate(flops=10**10, bytes_accessed=60_000_000, transcendentals=0),
+        cost_estimate=cost(100000000000),
     )(blocks[0].transpose(1, 0, 2), occ_coeff.transpose(2, 0, 1))
 
 
@@ -277,6 +281,7 @@
             pltpu.SMEM((KX * KY,), jnp.int32),
         ],
         compiler_params=pltpu.CompilerParams(vmem_limit_bytes=32 << 20),
+        cost_estimate=cost(100000000000),
     )(place, cell_offsets, cells)
 
 
@@ -354,6 +359,7 @@
             pltpu.VMEM((2 * sz.bands, 2 * KY, LANES), F32),
         ],
         compiler_params=pltpu.CompilerParams(vmem_limit_bytes=32 << 20),
+        cost_estimate=cost(10000000000),
     )(place, *halves, *rights)
 
 
@@ -421,7 +427,8 @@
     )(place, transfer_index, *sources)
 
 
-def spread_kernel(sz, in_ref, out_ref):
+def spread_kernel(sz, in_ref, *refs):
+    out_ref = refs[-1]
     low_lanes = lax.broadcasted_iota(jnp.int32, (sz.basis, LANES), 1) < HALF_LANES
     fill = jnp.zeros((sz.basis, LANES - sz.vir_half), F32)
     for part in range(2):
@@ -429,16 +436,32 @@
         out_ref[part] = jnp.where(low_lanes, value, pltpu.roll(value, HALF_LANES - sz.chunk, 1))
 
 
-def spread(sz, value, flops):
+def spread(sz, value, flops, *after):
     whole = pl.BlockSpec(memory_space=pltpu.VMEM)
     return pl.pallas_call(
         functools.partial(spread_kernel, sz),
         out_shape=jax.ShapeDtypeStruct((2, sz.basis, LANES), F32),
-        in_specs=[whole],
+        in_specs=[whole] + [pl.BlockSpec(memory_space=pl.ANY)] * len(after),
         out_specs=whole,
         compiler_params=pltpu.CompilerParams(vmem_limit_bytes=32 << 20),
-        cost_estimate=pl.CostEstimate(flops=flops, bytes_accessed=flops // 100, transcendentals=0),
-    )(value)
+        cost_estimate=cost(flops),
+    )(value, *after)
+
+
+def copy_kernel(in_ref, *refs):
+    refs[-1][...] = in_ref[...]
+
+
+def copied(value, *after):
+    whole = pl.BlockSpec(memory_space=pltpu.VMEM)
+    return pl.pallas_call(
+        copy_kernel,
+        out_shape=jax.ShapeDtypeStruct(value.shape, F32),
+        in_specs=[whole] + [pl.BlockSpec(memory_space=pl.ANY)] * len(after),
+        out_specs=whole,
+        compiler_params=pltpu.CompilerParams(vmem_limit_bytes=32 << 20),
+        cost_estimate=cost(10**6),
+    )(value, *after)
 
 
 def columns_kernel(sz, place_ref, own_ref, other_ref, out_ref):
@@ -465,7 +488,7 @@
         in_specs=[scalars, whole, whole],
         out_specs=whole,
         compiler_params=pltpu.CompilerParams(vmem_limit_bytes=32 << 20),
-        cost_estimate=pl.CostEstimate(flops=flops, bytes_accessed=flops // 100, transcendentals=0),
+        cost_estimate=cost(flops),
     )(place, own, other)
 
 
@@ -481,18 +504,21 @@
     sz = Sizes(blocks, occ_coeff, vir_coeff)
     me = lax.axis_index("cell")
     place = jnp.stack([me // KY, me % KY, lax.axis_index("aux")]).astype(jnp.int32)
-    long, short = 10**10, 10**6
     home = vir_coeff[0].transpose(1, 0, 2)
-    across = spread(sz, swap(home, 2 * KY), long)
-    beside = spread(sz, swap(home, KY), long)
+    across = spread(sz, swap(home, 2 * KY), 10000000000)
+    beside = spread(sz, swap(home, KY), 100000000)
     corner = swap(across, KY)
-    ours = spread(sz, home, short)
-    rights = [columns(sz, place, v, swap_cores(v), short) for v in (ours, beside, across)]
     sent = half_bands(sz, blocks, occ_coeff).reshape(KX * KY, sz.tail + 1, SUBLANES, LANES)
     cells = lax.all_to_all(sent, "cell", split_axis=0, concat_axis=0, tiled=True)
     points = list(lattice_sum(sz, place, cell_offsets, cells))
-    rights.append(columns(sz, place, corner, swap_cores(corner), short))
     halves = [points[0]] + [swap(points[s], s) for s in range(1, KY)]
+    ours = spread(sz, home, 3000000000, beside)
+    if 1 == 1:
+        corner = copied(corner, points[0])
+    if 1 in (2, 3):
+        corner = copied(corner, halves[1 - 1])
+    rights = [columns(sz, place, v, swap_cores(v), 10000000000) for v in (ours, beside, across)]
+    rights.append(columns(sz, place, corner, swap_cores(corner), 1000000000))
     bands = band_product(sz, place, halves, rights)
     sources = [bands[0]] + [swap(bands[s], s) for s in range(1, KY)]
     out = regroup(sz, place, transfer_index, sources)

time: 58.8 us -> 53.2 us (0.905)
  the two profiles are of different devices: /device:TPU:0 before, /device:TPU:16 now
where the time goes in v4:
time: 53.2 us; the launch traced here: 53 us
  waiting for transfers between devices  24.9 us (47%)
  starting transfers between devices  16.6 us (31%)
  Pallas kernels  11.3 us (21%)
    ppermute x9, waiting for transfers between devices, swap(): return lax.ppermute(value, 'cell', [(d, d ^ step) for d in range(KX * KY)])  13.7 us
    all_to_all x1, waiting for transfers between devices, by_planes(): lax.all_to_all(sent, 'cell', split_axis=0, concat_axis=0, tiled=True)  9.75 us
    ppermute x9, starting transfers between devices, swap(): return lax.ppermute(value, 'cell', [(d, d ^ step) for d in range(KX * KY)])  9.42 us
    all_to_all x1, starting transfers between devices, by_planes(): lax.all_to_all(sent, 'cell', split_axis=0, concat_axis=0, tiled=True)  6.47 us
    pallas_call x1, Pallas kernels, half_bands(): pl.pallas_call(functools.partial(half_kernel, sz), out_shape=jax.ShapeDty...  3.57 us
    pallas_call x4, Pallas kernels, columns(): pl.pallas_call(functools.partial(columns_kernel, sz), out_shape=jax.Shape...  2.79 us
    pallas_call x1, Pallas kernels, regroup(): pl.pallas_call(functools.partial(regroup_kernel, sz), out_shape=jax.Shape...  1.76 us
    pallas_call x1, Pallas kernels, band_product(): pl.pallas_call(functools.partial(band_kernel, sz), out_shape=[shape] * KY...  1.58 us
  transfers between devices with their start and end apart: 14, of which 8 were waited for; matrix products, arithmetic and copies ran while one was open for 0% of the time, Pallas kernels for 15%

profile of v4, /device:TPU:16, one launch (start us, length us, event | category | flops | bytes accessed | tf_op | source)
XLA Modules:
  0.0 53.0 jit_solution(944419773766650526)
XLA Ops:
  0.0 1.9 %collective-permute-start.3 = (f32[300,2,120]{2,1,0:T(2,128)}, f32[300,2,120]{2,1,0:T(2,128)S(1)}, u32[]{:S(2)}, u32[]{:S(2)}) collective-permute-start(f32[300,2,120]{2,1,0:T(2,128)} %bitcast.13), channel_id=1, source_target_pairs={{0,8},{2,10},{4,12},{6,14},{8,0},{10,2},{12,4},{14,6},{16,24},{18,... | collective-permute-start | bytes 864008 | tf_op jit(solution)/shard_map/ppermute | solution.py:496
  1.9 3.6 %shard_map.55 = f32[4,4,9,8,128]{4,3,2,1,0:T(8,128)} custom-call(f32[300,4,300]{2,1,0:T(4,128)} %bitcast.16, f32[60,2,300]{2,1,0:T(2,128)} %bitcast.17), custom_call_target="tpu_custom_call" | custom-call | flops 99999997952 | bytes 1000000000 | tf_op jit(solution)/shard_map/pallas_call | solution.py:188
  5.5 6.5 %all-to-all-start = ((f32[16,9,8,128]{3,2,1,0:T(8,128)}), f32[16,9,8,128]{3,2,1,0:T(8,128)S(1)}, u32[]{:S(2)}, u32[]{:S(2)}) async-start(f32[16,9,8,128]{3,2,1,0:T(8,128)} %bitcast.15), calls=%async_computation | async-start | bytes 1179648 | tf_op jit(solution)/shard_map/all_to_all | solution.py:512
  12.0 0.1 pad_add_fusion.place_ref
  12.0 4.8 %collective-permute-done.3.in_ref = f32[300,2,120]{2,1,0:T(2,128)S(1)} collective-permute-done((f32[300,2,120]{2,1,0:T(2,128)}, f32[300,2,120]{2,1,0:T(2,128)S(1)}, u32[]{:S(2)}, u32[]{:S(2)}) %collective-permute-start.3) | collective-permute-done | bytes 288032 | tf_op jit(solution)/shard_map/ppermute | solution.py:496
  16.8 0.2 shard_map.57.refs_0_.own_ref
  17.1 0.1 collective-permute-start.5
  17.2 0.2 shard_map.58.own_ref
  17.4 0.6 %collective-permute-start.4 = (f32[2,300,128]{2,1,0:T(8,128)S(1)}, f32[2,300,128]{2,1,0:T(8,128)S(1)}, u32[]{:S(2)}, u32[]{:S(2)}) collective-permute-start(f32[2,300,128]{2,1,0:T(8,128)S(1)} %shard_map.58.own_ref), channel_id=1, source_target_pairs={{0,1},{1,0},{2,3},{3,2},{4,5},{5,4},{6,7},{7,6},{8,9},{9,8},{10,11... | collective-permute-start | bytes 921608 | tf_op jit(solution)/shard_map/ppermute | solution.py:500
  18.0 0.2 shard_map.61.own_ref
  18.2 0.4 collective-permute-start.8
  18.6 0.6 %collective-permute-done.4.other_ref = f32[2,300,128]{2,1,0:T(8,128)S(1)} collective-permute-done((f32[2,300,128]{2,1,0:T(8,128)S(1)}, f32[2,300,128]{2,1,0:T(8,128)S(1)}, u32[]{:S(2)}, u32[]{:S(2)}) %collective-permute-start.4) | collective-permute-done | bytes 307232 | tf_op jit(solution)/shard_map/ppermute | solution.py:500
  19.2 0.7 %shard_map.59.refs_4_ = bf16[704,512]{1,0:T(8,128)(2,1)S(1)} custom-call(s32[3]{0:T(128)S(1)} %pad_add_fusion.place_ref, f32[2,300,128]{2,1,0:T(8,128)S(1)} %shard_map.58.own_ref, f32[2,300,128]{2,1,0:T(8,128)S(1)} %collective-permute-done.4.other_ref), custom_call_target="tpu_custom_call" | custom-call | flops 10000000000 | bytes 100000000 | tf_op jit(solution)/shard_map/pallas_call | solution.py:485
  19.9 0.7 %shard_map.60.refs_5_ = bf16[704,512]{1,0:T(8,128)(2,1)S(1)} custom-call(s32[3]{0:T(128)S(1)} %pad_add_fusion.place_ref, f32[2,300,128]{2,1,0:T(8,128)S(1)} %shard_map.57.refs_0_.own_ref, f32[2,300,128]{2,1,0:T(8,128)S(1)} %collective-permute-done.5.other_ref), custom_call_target="tpu_custom_call" | custom-call | flops 10000000000 | bytes 100000000 | tf_op jit(solution)/shard_map/pallas_call | solution.py:485
  20.6 9.8 %all-to-all-done.cells_ref = f32[16,9,8,128]{3,2,1,0:T(8,128)S(1)} async-done(((f32[16,9,8,128]{3,2,1,0:T(8,128)}), f32[16,9,8,128]{3,2,1,0:T(8,128)S(1)}, u32[]{:S(2)}, u32[]{:S(2)}) %all-to-all-start) | async-done | bytes 589856 | tf_op jit(solution)/shard_map/all_to_all | solution.py:512
  30.4 0.8 %shard_map.56 = (f32[4,9,8,128]{3,2,1,0:T(8,128)S(1)}, f32[4,9,8,128]{3,2,1,0:T(8,128)S(1)}, f32[4,9,8,128]{3,2,1,0:T(8,128)S(1)}, f32[4,9,8,128]{3,2,1,0:T(8,128)S(1)}) custom-call(s32[3]{0:T(128)S(1)} %pad_add_fusion.place_ref, s32[3,16]{1,0:T(4,128)S(1)} %copy-done.2, f32[16,9,8,128]{3,2,1,0:T(8,128)S(1)} %all-to-all-done.cells_ref), custom_call_target="tpu_custom_call" | custom-call | flops 99999997952 | bytes 1000000000 | tf_op jit(solution)/shard_map/pallas_call | solution.py:274
  31.2 1.6 %collective-permute-start = (f32[4,9,8,128]{3,2,1,0:T(8,128)S(1)}, f32[4,9,8,128]{3,2,1,0:T(8,128)S(1)}, u32[]{:S(2)}, u32[]{:S(2)}) collective-permute-start(f32[4,9,8,128]{3,2,1,0:T(8,128)S(1)} %get-tuple-element.14), channel_id=1, source_target_pairs={{0,2},{2,0},{4,6},{6,4},{8,10},{10,8},{12,14},{14,12},{16,18},{18,... | collective-permute-start | bytes 442376 | tf_op jit(solution)/shard_map/ppermute | solution.py:496
  32.8 2.0 %collective-permute-start.2 = (f32[4,9,8,128]{3,2,1,0:T(8,128)S(1)}, f32[4,9,8,128]{3,2,1,0:T(8,128)S(1)}, u32[]{:S(2)}, u32[]{:S(2)}) collective-permute-start(f32[4,9,8,128]{3,2,1,0:T(8,128)S(1)} %get-tuple-element.16), channel_id=1, source_target_pairs={{0,6},{2,4},{4,2},{6,0},{8,14},{10,12},{12,10},{14,8},{16,22},{18,... | collective-permute-start | bytes 442376 | tf_op jit(solution)/shard_map/ppermute | solution.py:496
  34.8 0.1 collective-permute-start.9
  34.9 0.7 %shard_map.62.refs_6_ = bf16[704,512]{1,0:T(8,128)(2,1)S(1)} custom-call(s32[3]{0:T(128)S(1)} %pad_add_fusion.place_ref, f32[2,300,128]{2,1,0:T(8,128)S(1)} %shard_map.61.own_ref, f32[2,300,128]{2,1,0:T(8,128)S(1)} %collective-permute-done.7.other_ref), custom_call_target="tpu_custom_call" | custom-call | flops 10000000000 | bytes 100000000 | tf_op jit(solution)/shard_map/pallas_call | solution.py:485
  35.6 0.9 %collective-permute-done.9.other_ref = f32[2,300,128]{2,1,0:T(8,128)S(1)} collective-permute-done((f32[2,300,128]{2,1,0:T(8,128)S(1)}, f32[2,300,128]{2,1,0:T(8,128)S(1)}, u32[]{:S(2)}, u32[]{:S(2)}) %collective-permute-start.9) | collective-permute-done | bytes 307232 | tf_op jit(solution)/shard_map/ppermute | solution.py:500
  36.5 0.7 %shard_map.64.refs_7_ = bf16[704,512]{1,0:T(8,128)(2,1)S(1)} custom-call(s32[3]{0:T(128)S(1)} %pad_add_fusion.place_ref, f32[2,300,128]{2,1,0:T(8,128)S(1)} %shard_map.63.own_ref, f32[2,300,128]{2,1,0:T(8,128)S(1)} %collective-permute-done.9.other_ref), custom_call_target="tpu_custom_call" | custom-call | flops 1000000000 | bytes 10000000 | tf_op jit(solution)/shard_map/pallas_call | solution.py:485
  37.2 0.0 copy-start
  37.2 0.6 %collective-permute-done.refs_1_ = f32[4,9,8,128]{3,2,1,0:T(8,128)S(1)} collective-permute-done((f32[4,9,8,128]{3,2,1,0:T(8,128)S(1)}, f32[4,9,8,128]{3,2,1,0:T(8,128)S(1)}, u32[]{:S(2)}, u32[]{:S(2)}) %collective-permute-start) | collective-permute-done | bytes 147488 | tf_op jit(solution)/shard_map/ppermute | solution.py:496
  37.7 3.7 %collective-permute-done.1.refs_2_ = f32[4,9,8,128]{3,2,1,0:T(8,128)S(1)} collective-permute-done((f32[4,9,8,128]{3,2,1,0:T(8,128)S(1)}, f32[4,9,8,128]{3,2,1,0:T(8,128)S(1)}, u32[]{:S(2)}, u32[]{:S(2)}) %collective-permute-start.1) | collective-permute-done | bytes 147488 | tf_op jit(solution)/shard_map/ppermute | solution.py:496
  41.4 1.6 %shard_map.65 = (f32[4,8,8,128]{3,2,1,0:T(8,128)S(1)}, f32[4,8,8,128]{3,2,1,0:T(8,128)S(1)}, f32[4,8,8,128]{3,2,1,0:T(8,128)S(1)}, f32[4,8,8,128]{3,2,1,0:T(8,128)S(1)}) custom-call(s32[3]{0:T(128)S(1)} %pad_add_fusion.place_ref, f32[4,9,8,128]{3,2,1,0:T(8,128)S(1)} %get-tuple-element.13.refs_0_, f32[4,9,8,128]{3,2,1,0:T(8,128)S(1)} %collective-permute-done.refs_1_, ...), custom_call_target="tpu_custom_call" | custom-call | flops 10000000000 | bytes 100000000 | tf_op jit(solution)/shard_map/pallas_call | solution.py:351
  43.0 0.6 %collective-permute-start.10 = (f32[4,8,8,128]{3,2,1,0:T(8,128)S(1)}, f32[4,8,8,128]{3,2,1,0:T(8,128)S(1)}, u32[]{:S(2)}, u32[]{:S(2)}) collective-permute-start(f32[4,8,8,128]{3,2,1,0:T(8,128)S(1)} %get-tuple-element.18), channel_id=1, source_target_pairs={{0,2},{2,0},{4,6},{6,4},{8,10},{10,8},{12,14},{14,12},{16,18},{18,... | collective-permute-start | bytes 393224 | tf_op jit(solution)/shard_map/ppermute | solution.py:496
  43.6 1.2 %collective-permute-start.11 = (f32[4,8,8,128]{3,2,1,0:T(8,128)S(1)}, f32[4,8,8,128]{3,2,1,0:T(8,128)S(1)}, u32[]{:S(2)}, u32[]{:S(2)}) collective-permute-start(f32[4,8,8,128]{3,2,1,0:T(8,128)S(1)} %get-tuple-element.19), channel_id=1, source_target_pairs={{0,4},{2,6},{4,0},{6,2},{8,12},{10,14},{12,8},{14,10},{16,20},{18,... | collective-permute-start | bytes 393224 | tf_op jit(solution)/shard_map/ppermute | solution.py:496
  44.8 1.8 %collective-permute-start.12 = (f32[4,8,8,128]{3,2,1,0:T(8,128)S(1)}, f32[4,8,8,128]{3,2,1,0:T(8,128)S(1)}, u32[]{:S(2)}, u32[]{:S(2)}) collective-permute-start(f32[4,8,8,128]{3,2,1,0:T(8,128)S(1)} %get-tuple-element.20), channel_id=1, source_target_pairs={{0,6},{2,4},{4,2},{6,0},{8,14},{10,12},{12,10},{14,8},{16,22},{18,... | collective-permute-start | bytes 393224 | tf_op jit(solution)/shard_map/ppermute | solution.py:496
  46.6 2.3 %collective-permute-done.10.refs_1_ = f32[4,8,8,128]{3,2,1,0:T(8,128)S(1)} collective-permute-done((f32[4,8,8,128]{3,2,1,0:T(8,128)S(1)}, f32[4,8,8,128]{3,2,1,0:T(8,128)S(1)}, u32[]{:S(2)}, u32[]{:S(2)}) %collective-permute-start.10) | collective-permute-done | bytes 131104 | tf_op jit(solution)/shard_map/ppermute | solution.py:496
  48.9 2.3 %collective-permute-done.11.refs_2_ = f32[4,8,8,128]{3,2,1,0:T(8,128)S(1)} collective-permute-done((f32[4,8,8,128]{3,2,1,0:T(8,128)S(1)}, f32[4,8,8,128]{3,2,1,0:T(8,128)S(1)}, u32[]{:S(2)}, u32[]{:S(2)}) %collective-permute-start.11) | collective-permute-done | bytes 131104 | tf_op jit(solution)/shard_map/ppermute | solution.py:496
  51.2 1.8 %shard_map.66 = f32[128,900]{1,0:T(8,128)} custom-call(s32[3]{0:T(128)S(1)} %pad_add_fusion.place_ref, s32[16]{0:T(128)S(1)} %copy-done, f32[4,8,8,128]{3,2,1,0:T(8,128)S(1)} %get-tuple-element.17.refs_0_, f32[4,8,8,128]{3,2,1,0:T(8,128)S(1)} %collective-permute-done.10.refs_1_, f32[4,8,8,128]{3,2,1,0:T(8,128)S(1)} %collective-permute-done.11.refs_2_, ...), custom_call_target="tpu_custom_call" | custom-call | tf_op jit(solution)/shard_map/pallas_call | solution.py:416
  (15 shorter events, 0.1 us)
Async XLA Ops:
  0.0 18.0 %collective-permute-start.6 = (f32[300,2,120]{2,1,0:T(2,128)}, f32[300,2,120]{2,1,0:T(2,128)S(1)}, u32[]{:S(2)}, u32[]{:S(2)}) collective-permute-start(f32[300,2,120]{2,1,0:T(2,128)} %bitcast.12), channel_id=1, source_target_pairs={{0,16},{2,18},{4,20},{6,22},{8,24},{10,26},{12,28},{14,30},{16,0},... | collective-permute-start | bytes 864008 | tf_op jit(solution)/shard_map/ppermute | solution.py:496
  0.0 16.8 %collective-permute-start.3 = (f32[300,2,120]{2,1,0:T(2,128)}, f32[300,2,120]{2,1,0:T(2,128)S(1)}, u32[]{:S(2)}, u32[]{:S(2)}) collective-permute-start(f32[300,2,120]{2,1,0:T(2,128)} %bitcast.13), channel_id=1, source_target_pairs={{0,8},{2,10},{4,12},{6,14},{8,0},{10,2},{12,4},{14,6},{16,24},{18,... | collective-permute-start | bytes 864008 | tf_op jit(solution)/shard_map/ppermute | solution.py:496
  5.5 11.7 %copy-start.1 = (f32[1,2,300,120]{3,1,2,0:T(2,128)S(1)}, f32[1,2,300,120]{3,1,2,0:T(2,128)}, u32[]{:S(2)}) copy-start(f32[1,2,300,120]{3,1,2,0:T(2,128)} %param.8) | copy-start | bytes 864004
  5.5 24.9 %all-to-all-start = ((f32[16,9,8,128]{3,2,1,0:T(8,128)}), f32[16,9,8,128]{3,2,1,0:T(8,128)S(1)}, u32[]{:S(2)}, u32[]{:S(2)}) async-start(f32[16,9,8,128]{3,2,1,0:T(8,128)} %bitcast.15), calls=%async_computation | async-start | bytes 1179648 | tf_op jit(solution)/shard_map/all_to_all | solution.py:512
  17.1 2.8 %collective-permute-start.5 = (f32[2,300,128]{2,1,0:T(8,128)S(1)}, f32[2,300,128]{2,1,0:T(8,128)S(1)}, u32[]{:S(2)}, u32[]{:S(2)}) collective-permute-start(f32[2,300,128]{2,1,0:T(8,128)S(1)} %shard_map.57.refs_0_.own_ref), channel_id=1, source_target_pairs={{0,1},{1,0},{2,3},{3,2},{4,5},{5,4},{6,7},{7,6},{8,9},{9,8},{10,11... | collective-permute-start | bytes 921608 | tf_op jit(solution)/shard_map/ppermute | solution.py:500
  17.4 1.8 %collective-permute-start.4 = (f32[2,300,128]{2,1,0:T(8,128)S(1)}, f32[2,300,128]{2,1,0:T(8,128)S(1)}, u32[]{:S(2)}, u32[]{:S(2)}) collective-permute-start(f32[2,300,128]{2,1,0:T(8,128)S(1)} %shard_map.58.own_ref), channel_id=1, source_target_pairs={{0,1},{1,0},{2,3},{3,2},{4,5},{5,4},{6,7},{7,6},{8,9},{9,8},{10,11... | collective-permute-start | bytes 921608 | tf_op jit(solution)/shard_map/ppermute | solution.py:500
  18.2 16.6 %collective-permute-start.8 = (f32[2,300,128]{2,1,0:T(8,128)S(1)}, f32[2,300,128]{2,1,0:T(8,128)S(1)}, u32[]{:S(2)}, u32[]{:S(2)}) collective-permute-start(f32[2,300,128]{2,1,0:T(8,128)S(1)} %shard_map.61.own_ref), channel_id=1, source_target_pairs={{0,8},{2,10},{4,12},{6,14},{8,0},{10,2},{12,4},{14,6},{16,24},{18,... | collective-permute-start | bytes 921608 | tf_op jit(solution)/shard_map/ppermute | solution.py:496
  18.6 16.3 %collective-permute-start.7 = (f32[2,300,128]{2,1,0:T(8,128)S(1)}, f32[2,300,128]{2,1,0:T(8,128)S(1)}, u32[]{:S(2)}, u32[]{:S(2)}) collective-permute-start(f32[2,300,128]{2,1,0:T(8,128)S(1)} %shard_map.61.own_ref), channel_id=1, source_target_pairs={{0,1},{1,0},{2,3},{3,2},{4,5},{5,4},{6,7},{7,6},{8,9},{9,8},{10,11... | collective-permute-start | bytes 921608 | tf_op jit(solution)/shard_map/ppermute | solution.py:500
  19.9 10.5 %copy-start.2 = (s32[3,16]{1,0:T(4,128)S(1)}, s32[3,16]{1,0:T(4,128)}, u32[]{:S(2)}) copy-start(s32[3,16]{1,0:T(4,128)} %offset_ref.1) | copy-start | bytes 580
  31.2 6.5 %collective-permute-start = (f32[4,9,8,128]{3,2,1,0:T(8,128)S(1)}, f32[4,9,8,128]{3,2,1,0:T(8,128)S(1)}, u32[]{:S(2)}, u32[]{:S(2)}) collective-permute-start(f32[4,9,8,128]{3,2,1,0:T(8,128)S(1)} %get-tuple-element.14), channel_id=1, source_target_pairs={{0,2},{2,0},{4,6},{6,4},{8,10},{10,8},{12,14},{14,12},{16,18},{18,... | collective-permute-start | bytes 442376 | tf_op jit(solution)/shard_map/ppermute | solution.py:496
  32.8 8.6 %collective-permute-start.1 = (f32[4,9,8,128]{3,2,1,0:T(8,128)S(1)}, f32[4,9,8,128]{3,2,1,0:T(8,128)S(1)}, u32[]{:S(2)}, u32[]{:S(2)}) collective-permute-start(f32[4,9,8,128]{3,2,1,0:T(8,128)S(1)} %get-tuple-element.15), channel_id=1, source_target_pairs={{0,4},{2,6},{4,0},{6,2},{8,12},{10,14},{12,8},{14,10},{16,20},{18,... | collective-permute-start | bytes 442376 | tf_op jit(solution)/shard_map/ppermute | solution.py:496
  32.8 8.6 %collective-permute-start.2 = (f32[4,9,8,128]{3,2,1,0:T(8,128)S(1)}, f32[4,9,8,128]{3,2,1,0:T(8,128)S(1)}, u32[]{:S(2)}, u32[]{:S(2)}) collective-permute-start(f32[4,9,8,128]{3,2,1,0:T(8,128)S(1)} %get-tuple-element.16), channel_id=1, source_target_pairs={{0,6},{2,4},{4,2},{6,0},{8,14},{10,12},{12,10},{14,8},{16,22},{18,... | collective-permute-start | bytes 442376 | tf_op jit(solution)/shard_map/ppermute | solution.py:496
  34.8 1.7 %collective-permute-start.9 = (f32[2,300,128]{2,1,0:T(8,128)S(1)}, f32[2,300,128]{2,1,0:T(8,128)S(1)}, u32[]{:S(2)}, u32[]{:S(2)}) collective-permute-start(f32[2,300,128]{2,1,0:T(8,128)S(1)} %shard_map.63.own_ref), channel_id=1, source_target_pairs={{0,1},{1,0},{2,3},{3,2},{4,5},{5,4},{6,7},{7,6},{8,9},{9,8},{10,11... | collective-permute-start | bytes 921608 | tf_op jit(solution)/shard_map/ppermute | solution.py:500
  37.2 14.1 %copy-start = (s32[16]{0:T(128)S(1)}, s32[16]{0:T(128)}, u32[]{:S(2)}) copy-start(s32[16]{0:T(128)} %transfer_ref.1) | copy-start | bytes 196
  43.0 5.9 %collective-permute-start.10 = (f32[4,8,8,128]{3,2,1,0:T(8,128)S(1)}, f32[4,8,8,128]{3,2,1,0:T(8,128)S(1)}, u32[]{:S(2)}, u32[]{:S(2)}) collective-permute-start(f32[4,8,8,128]{3,2,1,0:T(8,128)S(1)} %get-tuple-element.18), channel_id=1, source_target_pairs={{0,2},{2,0},{4,6},{6,4},{8,10},{10,8},{12,14},{14,12},{16,18},{18,... | collective-permute-start | bytes 393224 | tf_op jit(solution)/shard_map/ppermute | solution.py:496
  43.6 7.6 %collective-permute-start.11 = (f32[4,8,8,128]{3,2,1,0:T(8,128)S(1)}, f32[4,8,8,128]{3,2,1,0:T(8,128)S(1)}, u32[]{:S(2)}, u32[]{:S(2)}) collective-permute-start(f32[4,8,8,128]{3,2,1,0:T(8,128)S(1)} %get-tuple-element.19), channel_id=1, source_target_pairs={{0,4},{2,6},{4,0},{6,2},{8,12},{10,14},{12,8},{14,10},{16,20},{18,... | collective-permute-start | bytes 393224 | tf_op jit(solution)/shard_map/ppermute | solution.py:496
  44.8 6.4 %collective-permute-start.12 = (f32[4,8,8,128]{3,2,1,0:T(8,128)S(1)}, f32[4,8,8,128]{3,2,1,0:T(8,128)S(1)}, u32[]{:S(2)}, u32[]{:S(2)}) collective-permute-start(f32[4,8,8,128]{3,2,1,0:T(8,128)S(1)} %get-tuple-element.20), channel_id=1, source_target_pairs={{0,6},{2,4},{4,2},{6,0},{8,14},{10,12},{12,10},{14,8},{16,22},{18,... | collective-permute-start | bytes 393224 | tf_op jit(solution)/shard_map/ppermute | solution.py:496

commit v5 on v4

--- a/solution.py
+++ b/solution.py
@@ -107,10 +107,9 @@
         self.bands = self.occ // KX
         self.rows = 2 * SUBLANES
         self.tail = 4 * self.columns
-        self.chunk = self.vir_half // 2
-        self.chunks = 4 * self.bands // KY
-        self.tiles = self.chunks // 2 + 1
-        self.pairs = self.chunk * self.chunks
+        self.pairs = 2 * self.vir_half * self.bands // KY
+        self.full = self.pairs // LANES
+        self.share = LANES // KX
 
     @staticmethod
     def fit(cells, aux, blocks, occ_coeff, vir_coeff):
@@ -120,13 +119,13 @@
             and aux == 2
             and blocks.shape[1] == KY
             and occ % KX == 0
-            and occ // KX % 2 == 1
             and basis > LANES
             and HALF_LANES // 2 <= basis % LANES <= HALF_LANES // 2 + SEGMENT // 2
             and SUBLANES <= occ // KX < 2 * SUBLANES
             and occ // KX - SUBLANES <= basis // LANES * (LANES // SEGMENT)
-            and half % 2 == 0
-            and HALF_LANES - 8 < half // 2 <= HALF_LANES
+            and HALF_LANES < half <= LANES
+            and 2 * half * (occ // KX) % KY == 0
+            and 2 * half * (occ // KX) // KY % LANES <= LANES // KX
         )
 
 
@@ -287,7 +286,9 @@
 
 def band_kernel(sz, place_ref, *refs):
     halves, rights, outs = refs[:KY], refs[KY : KY + KX], refs[KY + KX : 2 * KY + KX]
-    left_ref, band_ref, tile_ref = refs[2 * KY + KX :]
+    left_ref, band_ref, tile_ref, pack_ref = refs[2 * KY + KX :]
+    wide = lax.broadcasted_iota(jnp.int32, (2 * KY, LANES), 1)
+    ends = [None] * KY
     seat = place_ref[1]
     count = KY * sz.rows
     row = lax.broadcasted_iota(jnp.int32, (SUBLANES, LANES), 0)
@@ -338,14 +339,30 @@
                     tile_ref[2 * i + h, part * KY : (part + 1) * KY] = band_ref[
                         h, part, pl.ds(i, KY, stride=sz.rows)
                     ]
-        for step in range(KY):
-            first = (step ^ seat) * sz.chunks // 2
-            for n in range(sz.tiles):
-                outs[step][k, n] = tile_ref[first + n]
+        for target in range(KY):
+            for first in range(0, sz.pairs, LANES):
+                last = min(first + LANES, sz.pairs)
+                value = None
+                begin, end = target * sz.pairs + first, target * sz.pairs + last
+                for tile in range(begin // sz.vir_half, (end - 1) // sz.vir_half + 1):
+                    offset = tile * sz.vir_half - begin
+                    moved = pltpu.roll(tile_ref[tile], offset % LANES, 1) if offset % LANES else tile_ref[tile]
+                    value = moved if value is None else jnp.where(wide < offset, value, moved)
+                if last - first == LANES:
+                    pack_ref[target, k * sz.full + first // LANES] = value
+                else:
+                    moved = pltpu.roll(value, k * sz.share, 1) if k else value
+                    ends[target] = moved if k == 0 else jnp.where(wide < k * sz.share, ends[target], moved)
+    for target in range(KY):
+        if ends[target] is not None:
+            pack_ref[target, KX * sz.full] = ends[target]
+    for step in range(KY):
+        outs[step][...] = pack_ref[step ^ seat]
 
 
 def band_product(sz, place, halves, rights):
-    shape = jax.ShapeDtypeStruct((KX, sz.tiles, 2 * KY, LANES), F32)
+    count = KX * sz.full + (sz.pairs % LANES > 0)
+    shape = jax.ShapeDtypeStruct((count, 2 * KY, LANES), F32)
     whole = pl.BlockSpec(memory_space=pltpu.VMEM)
     scalars = pl.BlockSpec(memory_space=pltpu.SMEM)
     return pl.pallas_call(
@@ -357,6 +374,7 @@
             pltpu.VMEM((KX, KY, sz.tail + 1, SUBLANES, LANES), F32),
             pltpu.VMEM((2, 2, KY * sz.rows, LANES), F32),
             pltpu.VMEM((2 * sz.bands, 2 * KY, LANES), F32),
+            pltpu.VMEM((KY, count, 2 * KY, LANES), F32),
         ],
         compiler_params=pltpu.CompilerParams(vmem_limit_bytes=32 << 20),
         cost_estimate=cost(10000000000),
@@ -367,45 +385,28 @@
     sources, out_hbm = refs[:KY], refs[KY]
     row_ref, out_ref, sems = refs[KY + 1 :]
     plane, seat = place_ref[0], place_ref[1]
-    lane = lax.broadcasted_iota(jnp.int32, (2 * KY, LANES), 1)
     cells = KX * KY
     starts = list(range(0, sz.pairs, LANES))
     pieces = [starts[i : i + PIECE] for i in range(0, len(starts), PIECE)]
-    targets = [
-        transfer_ref[(k ^ plane) * KY + (step ^ seat)] for step in range(KY) for k in range(KX)
-    ]
-
-    def piece_copy(index):
-        first = pieces[index][0]
-        span = pl.ds(first, min(pieces[index][-1] + LANES, sz.pairs) - first)
-        return pltpu.make_async_copy(out_ref.at[:, span], out_hbm.at[:, span], sems.at[index])
-
-    def place_rows(odd):
-        for index, piece in enumerate(pieces):
-            for first in piece:
-                last = min(first + LANES, sz.pairs)
-                for source, row in enumerate(targets):
-                    step, k = divmod(source, KX)
-                    value = None
-                    for u in range(first // sz.chunk, (last - 1) // sz.chunk + 1):
-                        tile = sources[step][k, (u + odd) // 2]
-                        shift = (sz.chunk * u - HALF_LANES * (u + odd)) % LANES
-                        moved = pltpu.roll(tile, shift, 1) if shift else tile
-                        value = moved if value is None else jnp.where(lane < sz.chunk * u - first, value, moved)
-                    row_ref[first // LANES, pl.ds(row, 2 * KY, stride=cells)] = value
-                out_ref[:, first:last] = row_ref[first // LANES, :, : last - first]
-            piece_copy(index).start()
-
-    @pl.when(seat % 2 == 0)
-    def _():
-        place_rows(0)
-
-    @pl.when(seat % 2 == 1)
-    def _():
-        place_rows(1)
-
-    for index in range(len(pieces)):
-        piece_copy(index).wait()
+    copies = []
+    for index, piece in enumerate(pieces):
+        for first in piece:
+            last = min(first + LANES, sz.pairs)
+            for step in range(KY):
+                for k in range(KX):
+                    row = transfer_ref[(k ^ plane) * KY + (step ^ seat)]
+                    if last - first == LANES:
+                        tile = sources[step][k * sz.full + first // LANES]
+                    else:
+                        tile = sources[step][KX * sz.full]
+                        tile = pltpu.roll(tile, LANES - k * sz.share, 1) if k else tile
+                    row_ref[first // LANES, pl.ds(row, 2 * KY, stride=cells)] = tile
+            out_ref[:, first:last] = row_ref[first // LANES, :, : last - first]
+        span = pl.ds(piece[0], min(piece[-1] + LANES, sz.pairs) - piece[0])
+        copies.append(pltpu.make_async_copy(out_ref.at[:, span], out_hbm.at[:, span], sems.at[index]))
+        copies[-1].start()
+    for copy in copies:
+        copy.wait()
 
 
 def regroup(sz, place, transfer_index, sources):
@@ -429,11 +430,9 @@
 
 def spread_kernel(sz, in_ref, *refs):
     out_ref = refs[-1]
-    low_lanes = lax.broadcasted_iota(jnp.int32, (sz.basis, LANES), 1) < HALF_LANES
     fill = jnp.zeros((sz.basis, LANES - sz.vir_half), F32)
     for part in range(2):
-        value = jnp.concatenate([in_ref[:, part], fill], axis=1)
-        out_ref[part] = jnp.where(low_lanes, value, pltpu.roll(value, HALF_LANES - sz.chunk, 1))
+        out_ref[part] = jnp.concatenate([in_ref[:, part], fill], axis=1)
 
 
 def spread(sz, value, flops, *after):

time: 53.2 us -> 52.8 us (level)
  no operation moved by 1% of the time
where the time goes in v5:
time: 52.8 us; the launch traced here: 52.5 us
  waiting for transfers between devices  24.6 us (47%)
  starting transfers between devices  16.7 us (32%)
  Pallas kernels  11 us (21%)
    ppermute x9, waiting for transfers between devices, swap(): return lax.ppermute(value, 'cell', [(d, d ^ step) for d in range(KX * KY)])  13.3 us
    all_to_all x1, waiting for transfers between devices, by_planes(): lax.all_to_all(sent, 'cell', split_axis=0, concat_axis=0, tiled=True)  9.81 us
    ppermute x9, starting transfers between devices, swap(): return lax.ppermute(value, 'cell', [(d, d ^ step) for d in range(KX * KY)])  9.54 us
    all_to_all x1, starting transfers between devices, by_planes(): lax.all_to_all(sent, 'cell', split_axis=0, concat_axis=0, tiled=True)  6.47 us
    pallas_call x1, Pallas kernels, half_bands(): pl.pallas_call(functools.partial(half_kernel, sz), out_shape=jax.ShapeDty...  3.57 us
    pallas_call x4, Pallas kernels, columns(): pl.pallas_call(functools.partial(columns_kernel, sz), out_shape=jax.Shape...  2.79 us
    pallas_call x1, Pallas kernels, band_product(): pl.pallas_call(functools.partial(band_kernel, sz), out_shape=[shape] * KY...  1.73 us
    pallas_call x1, Pallas kernels, regroup(): pl.pallas_call(functools.partial(regroup_kernel, sz), out_shape=jax.Shape...  1.53 us
  transfers between devices with their start and end apart: 14, of which 8 were waited for; matrix products, arithmetic and copies ran while one was open for 0% of the time, Pallas kernels for 15%

profile of v5, /device:TPU:16, one launch (start us, length us, event | category | flops | bytes accessed | tf_op | source)
XLA Modules:
  0.0 52.5 jit_solution(12264531602049555965)
XLA Ops:
  0.0 1.9 %collective-permute-start.3 = (f32[300,2,120]{2,1,0:T(2,128)}, f32[300,2,120]{2,1,0:T(2,128)S(1)}, u32[]{:S(2)}, u32[]{:S(2)}) collective-permute-start(f32[300,2,120]{2,1,0:T(2,128)} %bitcast.13), channel_id=1, source_target_pairs={{0,8},{2,10},{4,12},{6,14},{8,0},{10,2},{12,4},{14,6},{16,24},{18,... | collective-permute-start | bytes 864008 | tf_op jit(solution)/shard_map/ppermute | solution.py:495
  1.9 3.6 %shard_map.55 = f32[4,4,9,8,128]{4,3,2,1,0:T(8,128)} custom-call(f32[300,4,300]{2,1,0:T(4,128)} %bitcast.16, f32[60,2,300]{2,1,0:T(2,128)} %bitcast.17), custom_call_target="tpu_custom_call" | custom-call | flops 99999997952 | bytes 1000000000 | tf_op jit(solution)/shard_map/pallas_call | solution.py:187
  5.5 0.0 copy-start.1
  5.5 6.5 %all-to-all-start = ((f32[16,9,8,128]{3,2,1,0:T(8,128)}), f32[16,9,8,128]{3,2,1,0:T(8,128)S(1)}, u32[]{:S(2)}, u32[]{:S(2)}) async-start(f32[16,9,8,128]{3,2,1,0:T(8,128)} %bitcast.15), calls=%async_computation | async-start | bytes 1179648 | tf_op jit(solution)/shard_map/all_to_all | solution.py:511
  12.0 0.1 pad_add_fusion.place_ref
  12.0 4.8 %collective-permute-done.3.in_ref = f32[300,2,120]{2,1,0:T(2,128)S(1)} collective-permute-done((f32[300,2,120]{2,1,0:T(2,128)}, f32[300,2,120]{2,1,0:T(2,128)S(1)}, u32[]{:S(2)}, u32[]{:S(2)}) %collective-permute-start.3) | collective-permute-done | bytes 288032 | tf_op jit(solution)/shard_map/ppermute | solution.py:495
  16.8 0.2 shard_map.57.refs_0_.own_ref
  17.0 0.1 collective-permute-start.5
  17.1 0.2 shard_map.58.own_ref
  17.3 0.5 %collective-permute-start.4 = (f32[2,300,128]{2,1,0:T(8,128)S(1)}, f32[2,300,128]{2,1,0:T(8,128)S(1)}, u32[]{:S(2)}, u32[]{:S(2)}) collective-permute-start(f32[2,300,128]{2,1,0:T(8,128)S(1)} %shard_map.58.own_ref), channel_id=1, source_target_pairs={{0,1},{1,0},{2,3},{3,2},{4,5},{5,4},{6,7},{7,6},{8,9},{9,8},{10,11... | collective-permute-start | bytes 921608 | tf_op jit(solution)/shard_map/ppermute | solution.py:499
  17.8 0.2 shard_map.61.own_ref
  18.0 0.5 collective-permute-start.8
  18.6 0.6 %collective-permute-done.4.other_ref = f32[2,300,128]{2,1,0:T(8,128)S(1)} collective-permute-done((f32[2,300,128]{2,1,0:T(8,128)S(1)}, f32[2,300,128]{2,1,0:T(8,128)S(1)}, u32[]{:S(2)}, u32[]{:S(2)}) %collective-permute-start.4) | collective-permute-done | bytes 307232 | tf_op jit(solution)/shard_map/ppermute | solution.py:499
  19.1 0.7 %shard_map.59.refs_4_ = bf16[704,512]{1,0:T(8,128)(2,1)S(1)} custom-call(s32[3]{0:T(128)S(1)} %pad_add_fusion.place_ref, f32[2,300,128]{2,1,0:T(8,128)S(1)} %shard_map.58.own_ref, f32[2,300,128]{2,1,0:T(8,128)S(1)} %collective-permute-done.4.other_ref), custom_call_target="tpu_custom_call" | custom-call | flops 10000000000 | bytes 100000000 | tf_op jit(solution)/shard_map/pallas_call | solution.py:484
  19.9 0.7 %shard_map.60.refs_5_ = bf16[704,512]{1,0:T(8,128)(2,1)S(1)} custom-call(s32[3]{0:T(128)S(1)} %pad_add_fusion.place_ref, f32[2,300,128]{2,1,0:T(8,128)S(1)} %shard_map.57.refs_0_.own_ref, f32[2,300,128]{2,1,0:T(8,128)S(1)} %collective-permute-done.5.other_ref), custom_call_target="tpu_custom_call" | custom-call | flops 10000000000 | bytes 100000000 | tf_op jit(solution)/shard_map/pallas_call | solution.py:484
  20.6 9.8 %all-to-all-done.cells_ref = f32[16,9,8,128]{3,2,1,0:T(8,128)S(1)} async-done(((f32[16,9,8,128]{3,2,1,0:T(8,128)}), f32[16,9,8,128]{3,2,1,0:T(8,128)S(1)}, u32[]{:S(2)}, u32[]{:S(2)}) %all-to-all-start) | async-done | bytes 589856 | tf_op jit(solution)/shard_map/all_to_all | solution.py:511
  30.4 0.8 %shard_map.56 = (f32[4,9,8,128]{3,2,1,0:T(8,128)S(1)}, f32[4,9,8,128]{3,2,1,0:T(8,128)S(1)}, f32[4,9,8,128]{3,2,1,0:T(8,128)S(1)}, f32[4,9,8,128]{3,2,1,0:T(8,128)S(1)}) custom-call(s32[3]{0:T(128)S(1)} %pad_add_fusion.place_ref, s32[3,16]{1,0:T(4,128)S(1)} %copy-done.2, f32[16,9,8,128]{3,2,1,0:T(8,128)S(1)} %all-to-all-done.cells_ref), custom_call_target="tpu_custom_call" | custom-call | flops 99999997952 | bytes 1000000000 | tf_op jit(solution)/shard_map/pallas_call | solution.py:273
  31.2 1.6 %collective-permute-start = (f32[4,9,8,128]{3,2,1,0:T(8,128)S(1)}, f32[4,9,8,128]{3,2,1,0:T(8,128)S(1)}, u32[]{:S(2)}, u32[]{:S(2)}) collective-permute-start(f32[4,9,8,128]{3,2,1,0:T(8,128)S(1)} %get-tuple-element.14), channel_id=1, source_target_pairs={{0,2},{2,0},{4,6},{6,4},{8,10},{10,8},{12,14},{14,12},{16,18},{18,... | collective-permute-start | bytes 442376 | tf_op jit(solution)/shard_map/ppermute | solution.py:495
  32.8 2.0 %collective-permute-start.2 = (f32[4,9,8,128]{3,2,1,0:T(8,128)S(1)}, f32[4,9,8,128]{3,2,1,0:T(8,128)S(1)}, u32[]{:S(2)}, u32[]{:S(2)}) collective-permute-start(f32[4,9,8,128]{3,2,1,0:T(8,128)S(1)} %get-tuple-element.16), channel_id=1, source_target_pairs={{0,6},{2,4},{4,2},{6,0},{8,14},{10,12},{12,10},{14,8},{16,22},{18,... | collective-permute-start | bytes 442376 | tf_op jit(solution)/shard_map/ppermute | solution.py:495
  34.8 0.1 collective-permute-start.9
  34.9 0.7 %shard_map.62.refs_6_ = bf16[704,512]{1,0:T(8,128)(2,1)S(1)} custom-call(s32[3]{0:T(128)S(1)} %pad_add_fusion.place_ref, f32[2,300,128]{2,1,0:T(8,128)S(1)} %shard_map.61.own_ref, f32[2,300,128]{2,1,0:T(8,128)S(1)} %collective-permute-done.7.other_ref), custom_call_target="tpu_custom_call" | custom-call | flops 10000000000 | bytes 100000000 | tf_op jit(solution)/shard_map/pallas_call | solution.py:484
  35.6 0.9 %collective-permute-done.9.other_ref = f32[2,300,128]{2,1,0:T(8,128)S(1)} collective-permute-done((f32[2,300,128]{2,1,0:T(8,128)S(1)}, f32[2,300,128]{2,1,0:T(8,128)S(1)}, u32[]{:S(2)}, u32[]{:S(2)}) %collective-permute-start.9) | collective-permute-done | bytes 307232 | tf_op jit(solution)/shard_map/ppermute | solution.py:499
  36.5 0.7 %shard_map.64.refs_7_ = bf16[704,512]{1,0:T(8,128)(2,1)S(1)} custom-call(s32[3]{0:T(128)S(1)} %pad_add_fusion.place_ref, f32[2,300,128]{2,1,0:T(8,128)S(1)} %shard_map.63.own_ref, f32[2,300,128]{2,1,0:T(8,128)S(1)} %collective-permute-done.9.other_ref), custom_call_target="tpu_custom_call" | custom-call | flops 1000000000 | bytes 10000000 | tf_op jit(solution)/shard_map/pallas_call | solution.py:484
  37.2 0.6 %collective-permute-done.refs_1_ = f32[4,9,8,128]{3,2,1,0:T(8,128)S(1)} collective-permute-done((f32[4,9,8,128]{3,2,1,0:T(8,128)S(1)}, f32[4,9,8,128]{3,2,1,0:T(8,128)S(1)}, u32[]{:S(2)}, u32[]{:S(2)}) %collective-permute-start) | collective-permute-done | bytes 147488 | tf_op jit(solution)/shard_map/ppermute | solution.py:495
  37.7 3.7 %collective-permute-done.1.refs_2_ = f32[4,9,8,128]{3,2,1,0:T(8,128)S(1)} collective-permute-done((f32[4,9,8,128]{3,2,1,0:T(8,128)S(1)}, f32[4,9,8,128]{3,2,1,0:T(8,128)S(1)}, u32[]{:S(2)}, u32[]{:S(2)}) %collective-permute-start.1) | collective-permute-done | bytes 147488 | tf_op jit(solution)/shard_map/ppermute | solution.py:495
  41.4 1.7 %shard_map.65 = (f32[29,8,128]{2,1,0:T(8,128)S(1)}, f32[29,8,128]{2,1,0:T(8,128)S(1)}, f32[29,8,128]{2,1,0:T(8,128)S(1)}, f32[29,8,128]{2,1,0:T(8,128)S(1)}) custom-call(s32[3]{0:T(128)S(1)} %pad_add_fusion.place_ref, f32[4,9,8,128]{3,2,1,0:T(8,128)S(1)} %get-tuple-element.13.refs_0_, f32[4,9,8,128]{3,2,1,0:T(8,128)S(1)} %collective-permute-done.refs_1_, ...), custom_call_target="tpu_custom_call" | custom-call | flops 10000000000 | bytes 100000000 | tf_op jit(solution)/shard_map/pallas_call | solution.py:368
  43.2 0.6 %collective-permute-start.10 = (f32[29,8,128]{2,1,0:T(8,128)S(1)}, f32[29,8,128]{2,1,0:T(8,128)S(1)}, u32[]{:S(2)}, u32[]{:S(2)}) collective-permute-start(f32[29,8,128]{2,1,0:T(8,128)S(1)} %get-tuple-element.18), channel_id=1, source_target_pairs={{0,2},{2,0},{4,6},{6,4},{8,10},{10,8},{12,14},{14,12},{16,18},{18,... | collective-permute-start | bytes 356360 | tf_op jit(solution)/shard_map/ppermute | solution.py:495
  43.8 1.2 %collective-permute-start.11 = (f32[29,8,128]{2,1,0:T(8,128)S(1)}, f32[29,8,128]{2,1,0:T(8,128)S(1)}, u32[]{:S(2)}, u32[]{:S(2)}) collective-permute-start(f32[29,8,128]{2,1,0:T(8,128)S(1)} %get-tuple-element.19), channel_id=1, source_target_pairs={{0,4},{2,6},{4,0},{6,2},{8,12},{10,14},{12,8},{14,10},{16,20},{18,... | collective-permute-start | bytes 356360 | tf_op jit(solution)/shard_map/ppermute | solution.py:495
  45.0 1.7 %collective-permute-start.12 = (f32[29,8,128]{2,1,0:T(8,128)S(1)}, f32[29,8,128]{2,1,0:T(8,128)S(1)}, u32[]{:S(2)}, u32[]{:S(2)}) collective-permute-start(f32[29,8,128]{2,1,0:T(8,128)S(1)} %get-tuple-element.20), channel_id=1, source_target_pairs={{0,6},{2,4},{4,2},{6,0},{8,14},{10,12},{12,10},{14,8},{16,22},{18,... | collective-permute-start | bytes 356360 | tf_op jit(solution)/shard_map/ppermute | solution.py:495
  46.7 2.1 %collective-permute-done.10.refs_1_ = f32[29,8,128]{2,1,0:T(8,128)S(1)} collective-permute-done((f32[29,8,128]{2,1,0:T(8,128)S(1)}, f32[29,8,128]{2,1,0:T(8,128)S(1)}, u32[]{:S(2)}, u32[]{:S(2)}) %collective-permute-start.10) | collective-permute-done | bytes 118816 | tf_op jit(solution)/shard_map/ppermute | solution.py:495
  48.8 2.2 %collective-permute-done.11.refs_2_ = f32[29,8,128]{2,1,0:T(8,128)S(1)} collective-permute-done((f32[29,8,128]{2,1,0:T(8,128)S(1)}, f32[29,8,128]{2,1,0:T(8,128)S(1)}, u32[]{:S(2)}, u32[]{:S(2)}) %collective-permute-start.11) | collective-permute-done | bytes 118816 | tf_op jit(solution)/shard_map/ppermute | solution.py:495
  51.0 1.5 %shard_map.66 = f32[128,900]{1,0:T(8,128)} custom-call(s32[3]{0:T(128)S(1)} %pad_add_fusion.place_ref, s32[16]{0:T(128)S(1)} %copy-done, f32[29,8,128]{2,1,0:T(8,128)S(1)} %get-tuple-element.17.refs_0_, f32[29,8,128]{2,1,0:T(8,128)S(1)} %collective-permute-done.10.refs_1_, f32[29,8,128]{2,1,0:T(8,128)S(1)} %collective-permute-done.11.refs_2_, ...), custom_call_target="tpu_custom_call" | custom-call | tf_op jit(solution)/shard_map/pallas_call | solution.py:417
  (15 shorter events, 0.1 us)
Async XLA Ops:
  0.0 17.8 %collective-permute-start.6 = (f32[300,2,120]{2,1,0:T(2,128)}, f32[300,2,120]{2,1,0:T(2,128)S(1)}, u32[]{:S(2)}, u32[]{:S(2)}) collective-permute-start(f32[300,2,120]{2,1,0:T(2,128)} %bitcast.12), channel_id=1, source_target_pairs={{0,16},{2,18},{4,20},{6,22},{8,24},{10,26},{12,28},{14,30},{16,0},... | collective-permute-start | bytes 864008 | tf_op jit(solution)/shard_map/ppermute | solution.py:495
  0.0 16.8 %collective-permute-start.3 = (f32[300,2,120]{2,1,0:T(2,128)}, f32[300,2,120]{2,1,0:T(2,128)S(1)}, u32[]{:S(2)}, u32[]{:S(2)}) collective-permute-start(f32[300,2,120]{2,1,0:T(2,128)} %bitcast.13), channel_id=1, source_target_pairs={{0,8},{2,10},{4,12},{6,14},{8,0},{10,2},{12,4},{14,6},{16,24},{18,... | collective-permute-start | bytes 864008 | tf_op jit(solution)/shard_map/ppermute | solution.py:495
  5.5 11.6 %copy-start.1 = (f32[1,2,300,120]{3,1,2,0:T(2,128)S(1)}, f32[1,2,300,120]{3,1,2,0:T(2,128)}, u32[]{:S(2)}) copy-start(f32[1,2,300,120]{3,1,2,0:T(2,128)} %param.8) | copy-start | bytes 864004
  5.5 24.9 %all-to-all-start = ((f32[16,9,8,128]{3,2,1,0:T(8,128)}), f32[16,9,8,128]{3,2,1,0:T(8,128)S(1)}, u32[]{:S(2)}, u32[]{:S(2)}) async-start(f32[16,9,8,128]{3,2,1,0:T(8,128)} %bitcast.15), calls=%async_computation | async-start | bytes 1179648 | tf_op jit(solution)/shard_map/all_to_all | solution.py:511
  17.0 2.8 %collective-permute-start.5 = (f32[2,300,128]{2,1,0:T(8,128)S(1)}, f32[2,300,128]{2,1,0:T(8,128)S(1)}, u32[]{:S(2)}, u32[]{:S(2)}) collective-permute-start(f32[2,300,128]{2,1,0:T(8,128)S(1)} %shard_map.57.refs_0_.own_ref), channel_id=1, source_target_pairs={{0,1},{1,0},{2,3},{3,2},{4,5},{5,4},{6,7},{7,6},{8,9},{9,8},{10,11... | collective-permute-start | bytes 921608 | tf_op jit(solution)/shard_map/ppermute | solution.py:499
  17.3 1.8 %collective-permute-start.4 = (f32[2,300,128]{2,1,0:T(8,128)S(1)}, f32[2,300,128]{2,1,0:T(8,128)S(1)}, u32[]{:S(2)}, u32[]{:S(2)}) collective-permute-start(f32[2,300,128]{2,1,0:T(8,128)S(1)} %shard_map.58.own_ref), channel_id=1, source_target_pairs={{0,1},{1,0},{2,3},{3,2},{4,5},{5,4},{6,7},{7,6},{8,9},{9,8},{10,11... | collective-permute-start | bytes 921608 | tf_op jit(solution)/shard_map/ppermute | solution.py:499
  18.0 16.7 %collective-permute-start.8 = (f32[2,300,128]{2,1,0:T(8,128)S(1)}, f32[2,300,128]{2,1,0:T(8,128)S(1)}, u32[]{:S(2)}, u32[]{:S(2)}) collective-permute-start(f32[2,300,128]{2,1,0:T(8,128)S(1)} %shard_map.61.own_ref), channel_id=1, source_target_pairs={{0,8},{2,10},{4,12},{6,14},{8,0},{10,2},{12,4},{14,6},{16,24},{18,... | collective-permute-start | bytes 921608 | tf_op jit(solution)/shard_map/ppermute | solution.py:495
  18.5 16.3 %collective-permute-start.7 = (f32[2,300,128]{2,1,0:T(8,128)S(1)}, f32[2,300,128]{2,1,0:T(8,128)S(1)}, u32[]{:S(2)}, u32[]{:S(2)}) collective-permute-start(f32[2,300,128]{2,1,0:T(8,128)S(1)} %shard_map.61.own_ref), channel_id=1, source_target_pairs={{0,1},{1,0},{2,3},{3,2},{4,5},{5,4},{6,7},{7,6},{8,9},{9,8},{10,11... | collective-permute-start | bytes 921608 | tf_op jit(solution)/shard_map/ppermute | solution.py:499
  19.8 10.5 %copy-start.2 = (s32[3,16]{1,0:T(4,128)S(1)}, s32[3,16]{1,0:T(4,128)}, u32[]{:S(2)}) copy-start(s32[3,16]{1,0:T(4,128)} %offset_ref.1) | copy-start | bytes 580
  31.2 6.5 %collective-permute-start = (f32[4,9,8,128]{3,2,1,0:T(8,128)S(1)}, f32[4,9,8,128]{3,2,1,0:T(8,128)S(1)}, u32[]{:S(2)}, u32[]{:S(2)}) collective-permute-start(f32[4,9,8,128]{3,2,1,0:T(8,128)S(1)} %get-tuple-element.14), channel_id=1, source_target_pairs={{0,2},{2,0},{4,6},{6,4},{8,10},{10,8},{12,14},{14,12},{16,18},{18,... | collective-permute-start | bytes 442376 | tf_op jit(solution)/shard_map/ppermute | solution.py:495
  32.8 8.6 %collective-permute-start.1 = (f32[4,9,8,128]{3,2,1,0:T(8,128)S(1)}, f32[4,9,8,128]{3,2,1,0:T(8,128)S(1)}, u32[]{:S(2)}, u32[]{:S(2)}) collective-permute-start(f32[4,9,8,128]{3,2,1,0:T(8,128)S(1)} %get-tuple-element.15), channel_id=1, source_target_pairs={{0,4},{2,6},{4,0},{6,2},{8,12},{10,14},{12,8},{14,10},{16,20},{18,... | collective-permute-start | bytes 442376 | tf_op jit(solution)/shard_map/ppermute | solution.py:495
  32.8 8.6 %collective-permute-start.2 = (f32[4,9,8,128]{3,2,1,0:T(8,128)S(1)}, f32[4,9,8,128]{3,2,1,0:T(8,128)S(1)}, u32[]{:S(2)}, u32[]{:S(2)}) collective-permute-start(f32[4,9,8,128]{3,2,1,0:T(8,128)S(1)} %get-tuple-element.16), channel_id=1, source_target_pairs={{0,6},{2,4},{4,2},{6,0},{8,14},{10,12},{12,10},{14,8},{16,22},{18,... | collective-permute-start | bytes 442376 | tf_op jit(solution)/shard_map/ppermute | solution.py:495
  34.8 1.7 %collective-permute-start.9 = (f32[2,300,128]{2,1,0:T(8,128)S(1)}, f32[2,300,128]{2,1,0:T(8,128)S(1)}, u32[]{:S(2)}, u32[]{:S(2)}) collective-permute-start(f32[2,300,128]{2,1,0:T(8,128)S(1)} %shard_map.63.own_ref), channel_id=1, source_target_pairs={{0,1},{1,0},{2,3},{3,2},{4,5},{5,4},{6,7},{7,6},{8,9},{9,8},{10,11... | collective-permute-start | bytes 921608 | tf_op jit(solution)/shard_map/ppermute | solution.py:499
  37.2 13.8 %copy-start = (s32[16]{0:T(128)S(1)}, s32[16]{0:T(128)}, u32[]{:S(2)}) copy-start(s32[16]{0:T(128)} %transfer_ref.1) | copy-start | bytes 196
  43.2 5.6 %collective-permute-start.10 = (f32[29,8,128]{2,1,0:T(8,128)S(1)}, f32[29,8,128]{2,1,0:T(8,128)S(1)}, u32[]{:S(2)}, u32[]{:S(2)}) collective-permute-start(f32[29,8,128]{2,1,0:T(8,128)S(1)} %get-tuple-element.18), channel_id=1, source_target_pairs={{0,2},{2,0},{4,6},{6,4},{8,10},{10,8},{12,14},{14,12},{16,18},{18,... | collective-permute-start | bytes 356360 | tf_op jit(solution)/shard_map/ppermute | solution.py:495
  43.8 7.2 %collective-permute-start.11 = (f32[29,8,128]{2,1,0:T(8,128)S(1)}, f32[29,8,128]{2,1,0:T(8,128)S(1)}, u32[]{:S(2)}, u32[]{:S(2)}) collective-permute-start(f32[29,8,128]{2,1,0:T(8,128)S(1)} %get-tuple-element.19), channel_id=1, source_target_pairs={{0,4},{2,6},{4,0},{6,2},{8,12},{10,14},{12,8},{14,10},{16,20},{18,... | collective-permute-start | bytes 356360 | tf_op jit(solution)/shard_map/ppermute | solution.py:495
  45.0 6.0 %collective-permute-start.12 = (f32[29,8,128]{2,1,0:T(8,128)S(1)}, f32[29,8,128]{2,1,0:T(8,128)S(1)}, u32[]{:S(2)}, u32[]{:S(2)}) collective-permute-start(f32[29,8,128]{2,1,0:T(8,128)S(1)} %get-tuple-element.20), channel_id=1, source_target_pairs={{0,6},{2,4},{4,2},{6,0},{8,14},{10,12},{12,10},{14,8},{16,22},{18,... | collective-permute-start | bytes 356360 | tf_op jit(solution)/shard_map/ppermute | solution.py:495

commit v6 on v5

--- a/solution.py
+++ b/solution.py
@@ -13,7 +13,9 @@
 LANES = 128
 HALF_LANES = 64
 SEGMENT = 32
-PIECE = 4
+PIECE = 2
+OUT = (0, 1, 2, 3)
+BACK = (0, 3, 2, 1)
 SUBLANES = 8
 SEGMENTS = LANES // SEGMENT
 BF16 = jnp.bfloat16
@@ -262,8 +264,8 @@
         grid_ref[b, a ^ plane, sz.tail] = value
 
     transform(load_rest, turn_rest, store_rest)
-    for step in range(KY):
-        outs[step][...] = grid_ref[step ^ seat]
+    for out_ref, step in zip(outs, OUT):
+        out_ref[...] = grid_ref[step ^ seat]
 
 
 def lattice_sum(sz, place, cell_offsets, cells):
@@ -294,8 +296,8 @@
     row = lax.broadcasted_iota(jnp.int32, (SUBLANES, LANES), 0)
     lane = lax.broadcasted_iota(jnp.int32, (SUBLANES, LANES), 1)
     low_lanes = lax.broadcasted_iota(jnp.int32, (2 * count, LANES), 1) < HALF_LANES
-    for step in range(KY):
-        left_ref[:, step ^ seat] = halves[step][...]
+    for place, step in enumerate(OUT):
+        left_ref[:, step ^ seat] = halves[place][...]
 
     for k in range(KX):
         left = left_ref[k]
@@ -356,8 +358,8 @@
     for target in range(KY):
         if ends[target] is not None:
             pack_ref[target, KX * sz.full] = ends[target]
-    for step in range(KY):
-        outs[step][...] = pack_ref[step ^ seat]
+    for out_ref, step in zip(outs, BACK):
+        out_ref[...] = pack_ref[step ^ seat]
 
 
 def band_product(sz, place, halves, rights):
@@ -392,13 +394,13 @@
     for index, piece in enumerate(pieces):
         for first in piece:
             last = min(first + LANES, sz.pairs)
-            for step in range(KY):
+            for source, step in enumerate(BACK):
                 for k in range(KX):
                     row = transfer_ref[(k ^ plane) * KY + (step ^ seat)]
                     if last - first == LANES:
-                        tile = sources[step][k * sz.full + first // LANES]
+                        tile = sources[source][k * sz.full + first // LANES]
                     else:
-                        tile = sources[step][KX * sz.full]
+                        tile = sources[source][KX * sz.full]
                         tile = pltpu.roll(tile, LANES - k * sz.share, 1) if k else tile
                     row_ref[first // LANES, pl.ds(row, 2 * KY, stride=cells)] = tile
             out_ref[:, first:last] = row_ref[first // LANES, :, : last - first]
@@ -510,7 +512,7 @@
     sent = half_bands(sz, blocks, occ_coeff).reshape(KX * KY, sz.tail + 1, SUBLANES, LANES)
     cells = lax.all_to_all(sent, "cell", split_axis=0, concat_axis=0, tiled=True)
     points = list(lattice_sum(sz, place, cell_offsets, cells))
-    halves = [points[0]] + [swap(points[s], s) for s in range(1, KY)]
+    halves = [points[0]] + [swap(part, step) for part, step in zip(points[1:], OUT[1:])]
     ours = spread(sz, home, 3000000000, beside)
     if 1 == 1:
         corner = copied(corner, points[0])
@@ -519,7 +521,7 @@
     rights = [columns(sz, place, v, swap_cores(v), 10000000000) for v in (ours, beside, across)]
     rights.append(columns(sz, place, corner, swap_cores(corner), 1000000000))
     bands = band_product(sz, place, halves, rights)
-    sources = [bands[0]] + [swap(bands[s], s) for s in range(1, KY)]
+    sources = [bands[0]] + [swap(band, step) for band, step in zip(bands[1:], BACK[1:])]
     out = regroup(sz, place, transfer_index, sources)
     return out.reshape(2, sz.slab, KX * KY, sz.pairs)
 

time: 52.8 us -> 52.6 us (level)
  no operation moved by 1% of the time
where the time goes in v6:
time: 52.6 us; the launch traced here: 52.3 us
  waiting for transfers between devices  24.4 us (46%)
  starting transfers between devices  16.7 us (32%)
  Pallas kernels  11 us (21%)
    ppermute x9, waiting for transfers between devices, swap(): return lax.ppermute(value, 'cell', [(d, d ^ step) for d in range(KX * KY)])  13.1 us
    all_to_all x1, waiting for transfers between devices, by_planes(): lax.all_to_all(sent, 'cell', split_axis=0, concat_axis=0, tiled=True)  9.81 us
    ppermute x9, starting transfers between devices, swap(): return lax.ppermute(value, 'cell', [(d, d ^ step) for d in range(KX * KY)])  9.54 us
    all_to_all x1, starting transfers between devices, by_planes(): lax.all_to_all(sent, 'cell', split_axis=0, concat_axis=0, tiled=True)  6.47 us
    pallas_call x1, Pallas kernels, half_bands(): pl.pallas_call(functools.partial(half_kernel, sz), out_shape=jax.ShapeDty...  3.57 us
    pallas_call x4, Pallas kernels, columns(): pl.pallas_call(functools.partial(columns_kernel, sz), out_shape=jax.Shape...  2.79 us
    pallas_call x1, Pallas kernels, band_product(): pl.pallas_call(functools.partial(band_kernel, sz), out_shape=[shape] * KY...  1.74 us
    pallas_call x1, Pallas kernels, regroup(): pl.pallas_call(functools.partial(regroup_kernel, sz), out_shape=jax.Shape...  1.51 us
  transfers between devices with their start and end apart: 14, of which 8 were waited for; matrix products, arithmetic and copies ran while one was open for 0% of the time, Pallas kernels for 15%

profile of v6, /device:TPU:16, one launch (start us, length us, event | category | flops | bytes accessed | tf_op | source)
XLA Modules:
  0.0 52.3 jit_solution(8655449458837471194)
XLA Ops:
  0.0 1.9 %collective-permute-start.3 = (f32[300,2,120]{2,1,0:T(2,128)}, f32[300,2,120]{2,1,0:T(2,128)S(1)}, u32[]{:S(2)}, u32[]{:S(2)}) collective-permute-start(f32[300,2,120]{2,1,0:T(2,128)} %bitcast.13), channel_id=1, source_target_pairs={{0,8},{2,10},{4,12},{6,14},{8,0},{10,2},{12,4},{14,6},{16,24},{18,... | collective-permute-start | bytes 864008 | tf_op jit(solution)/shard_map/ppermute | solution.py:497
  1.9 3.6 %shard_map.55 = f32[4,4,9,8,128]{4,3,2,1,0:T(8,128)} custom-call(f32[300,4,300]{2,1,0:T(4,128)} %bitcast.16, f32[60,2,300]{2,1,0:T(2,128)} %bitcast.17), custom_call_target="tpu_custom_call" | custom-call | flops 99999997952 | bytes 1000000000 | tf_op jit(solution)/shard_map/pallas_call | solution.py:189
  5.5 0.0 copy-start.1
  5.5 6.5 %all-to-all-start = ((f32[16,9,8,128]{3,2,1,0:T(8,128)}), f32[16,9,8,128]{3,2,1,0:T(8,128)S(1)}, u32[]{:S(2)}, u32[]{:S(2)}) async-start(f32[16,9,8,128]{3,2,1,0:T(8,128)} %bitcast.15), calls=%async_computation | async-start | bytes 1179648 | tf_op jit(solution)/shard_map/all_to_all | solution.py:513
  12.0 0.1 pad_add_fusion.place_ref
  12.0 4.8 %collective-permute-done.3.in_ref = f32[300,2,120]{2,1,0:T(2,128)S(1)} collective-permute-done((f32[300,2,120]{2,1,0:T(2,128)}, f32[300,2,120]{2,1,0:T(2,128)S(1)}, u32[]{:S(2)}, u32[]{:S(2)}) %collective-permute-start.3) | collective-permute-done | bytes 288032 | tf_op jit(solution)/shard_map/ppermute | solution.py:497
  16.8 0.2 shard_map.57.refs_0_.own_ref
  17.0 0.1 collective-permute-start.5
  17.1 0.2 shard_map.58.own_ref
  17.3 0.5 %collective-permute-start.4 = (f32[2,300,128]{2,1,0:T(8,128)S(1)}, f32[2,300,128]{2,1,0:T(8,128)S(1)}, u32[]{:S(2)}, u32[]{:S(2)}) collective-permute-start(f32[2,300,128]{2,1,0:T(8,128)S(1)} %shard_map.58.own_ref), channel_id=1, source_target_pairs={{0,1},{1,0},{2,3},{3,2},{4,5},{5,4},{6,7},{7,6},{8,9},{9,8},{10,11... | collective-permute-start | bytes 921608 | tf_op jit(solution)/shard_map/ppermute | solution.py:501
  17.8 0.2 shard_map.61.own_ref
  18.0 0.5 collective-permute-start.8
  18.6 0.6 %collective-permute-done.4.other_ref = f32[2,300,128]{2,1,0:T(8,128)S(1)} collective-permute-done((f32[2,300,128]{2,1,0:T(8,128)S(1)}, f32[2,300,128]{2,1,0:T(8,128)S(1)}, u32[]{:S(2)}, u32[]{:S(2)}) %collective-permute-start.4) | collective-permute-done | bytes 307232 | tf_op jit(solution)/shard_map/ppermute | solution.py:501
  19.1 0.7 %shard_map.59.refs_4_ = bf16[704,512]{1,0:T(8,128)(2,1)S(1)} custom-call(s32[3]{0:T(128)S(1)} %pad_add_fusion.place_ref, f32[2,300,128]{2,1,0:T(8,128)S(1)} %shard_map.58.own_ref, f32[2,300,128]{2,1,0:T(8,128)S(1)} %collective-permute-done.4.other_ref), custom_call_target="tpu_custom_call" | custom-call | flops 10000000000 | bytes 100000000 | tf_op jit(solution)/shard_map/pallas_call | solution.py:486
  19.9 0.7 %shard_map.60.refs_5_ = bf16[704,512]{1,0:T(8,128)(2,1)S(1)} custom-call(s32[3]{0:T(128)S(1)} %pad_add_fusion.place_ref, f32[2,300,128]{2,1,0:T(8,128)S(1)} %shard_map.57.refs_0_.own_ref, f32[2,300,128]{2,1,0:T(8,128)S(1)} %collective-permute-done.5.other_ref), custom_call_target="tpu_custom_call" | custom-call | flops 10000000000 | bytes 100000000 | tf_op jit(solution)/shard_map/pallas_call | solution.py:486
  20.6 9.8 %all-to-all-done.cells_ref = f32[16,9,8,128]{3,2,1,0:T(8,128)S(1)} async-done(((f32[16,9,8,128]{3,2,1,0:T(8,128)}), f32[16,9,8,128]{3,2,1,0:T(8,128)S(1)}, u32[]{:S(2)}, u32[]{:S(2)}) %all-to-all-start) | async-done | bytes 589856 | tf_op jit(solution)/shard_map/all_to_all | solution.py:513
  30.4 0.8 %shard_map.56 = (f32[4,9,8,128]{3,2,1,0:T(8,128)S(1)}, f32[4,9,8,128]{3,2,1,0:T(8,128)S(1)}, f32[4,9,8,128]{3,2,1,0:T(8,128)S(1)}, f32[4,9,8,128]{3,2,1,0:T(8,128)S(1)}) custom-call(s32[3]{0:T(128)S(1)} %pad_add_fusion.place_ref, s32[3,16]{1,0:T(4,128)S(1)} %copy-done.2, f32[16,9,8,128]{3,2,1,0:T(8,128)S(1)} %all-to-all-done.cells_ref), custom_call_target="tpu_custom_call" | custom-call | flops 99999997952 | bytes 1000000000 | tf_op jit(solution)/shard_map/pallas_call | solution.py:275
  31.2 1.6 %collective-permute-start = (f32[4,9,8,128]{3,2,1,0:T(8,128)S(1)}, f32[4,9,8,128]{3,2,1,0:T(8,128)S(1)}, u32[]{:S(2)}, u32[]{:S(2)}) collective-permute-start(f32[4,9,8,128]{3,2,1,0:T(8,128)S(1)} %get-tuple-element.14), channel_id=1, source_target_pairs={{0,2},{2,0},{4,6},{6,4},{8,10},{10,8},{12,14},{14,12},{16,18},{18,... | collective-permute-start | bytes 442376 | tf_op jit(solution)/shard_map/ppermute | solution.py:497
  32.8 2.0 %collective-permute-start.2 = (f32[4,9,8,128]{3,2,1,0:T(8,128)S(1)}, f32[4,9,8,128]{3,2,1,0:T(8,128)S(1)}, u32[]{:S(2)}, u32[]{:S(2)}) collective-permute-start(f32[4,9,8,128]{3,2,1,0:T(8,128)S(1)} %get-tuple-element.16), channel_id=1, source_target_pairs={{0,6},{2,4},{4,2},{6,0},{8,14},{10,12},{12,10},{14,8},{16,22},{18,... | collective-permute-start | bytes 442376 | tf_op jit(solution)/shard_map/ppermute | solution.py:497
  34.8 0.1 collective-permute-start.9
  34.9 0.7 %shard_map.62.refs_6_ = bf16[704,512]{1,0:T(8,128)(2,1)S(1)} custom-call(s32[3]{0:T(128)S(1)} %pad_add_fusion.place_ref, f32[2,300,128]{2,1,0:T(8,128)S(1)} %shard_map.61.own_ref, f32[2,300,128]{2,1,0:T(8,128)S(1)} %collective-permute-done.7.other_ref), custom_call_target="tpu_custom_call" | custom-call | flops 10000000000 | bytes 100000000 | tf_op jit(solution)/shard_map/pallas_call | solution.py:486
  35.6 0.9 %collective-permute-done.9.other_ref = f32[2,300,128]{2,1,0:T(8,128)S(1)} collective-permute-done((f32[2,300,128]{2,1,0:T(8,128)S(1)}, f32[2,300,128]{2,1,0:T(8,128)S(1)}, u32[]{:S(2)}, u32[]{:S(2)}) %collective-permute-start.9) | collective-permute-done | bytes 307232 | tf_op jit(solution)/shard_map/ppermute | solution.py:501
  36.5 0.7 %shard_map.64.refs_7_ = bf16[704,512]{1,0:T(8,128)(2,1)S(1)} custom-call(s32[3]{0:T(128)S(1)} %pad_add_fusion.place_ref, f32[2,300,128]{2,1,0:T(8,128)S(1)} %shard_map.63.own_ref, f32[2,300,128]{2,1,0:T(8,128)S(1)} %collective-permute-done.9.other_ref), custom_call_target="tpu_custom_call" | custom-call | flops 1000000000 | bytes 10000000 | tf_op jit(solution)/shard_map/pallas_call | solution.py:486
  37.2 0.6 %collective-permute-done.refs_1_ = f32[4,9,8,128]{3,2,1,0:T(8,128)S(1)} collective-permute-done((f32[4,9,8,128]{3,2,1,0:T(8,128)S(1)}, f32[4,9,8,128]{3,2,1,0:T(8,128)S(1)}, u32[]{:S(2)}, u32[]{:S(2)}) %collective-permute-start) | collective-permute-done | bytes 147488 | tf_op jit(solution)/shard_map/ppermute | solution.py:497
  37.7 3.7 %collective-permute-done.1.refs_2_ = f32[4,9,8,128]{3,2,1,0:T(8,128)S(1)} collective-permute-done((f32[4,9,8,128]{3,2,1,0:T(8,128)S(1)}, f32[4,9,8,128]{3,2,1,0:T(8,128)S(1)}, u32[]{:S(2)}, u32[]{:S(2)}) %collective-permute-start.1) | collective-permute-done | bytes 147488 | tf_op jit(solution)/shard_map/ppermute | solution.py:497
  41.4 1.7 %shard_map.65 = (f32[29,8,128]{2,1,0:T(8,128)S(1)}, f32[29,8,128]{2,1,0:T(8,128)S(1)}, f32[29,8,128]{2,1,0:T(8,128)S(1)}, f32[29,8,128]{2,1,0:T(8,128)S(1)}) custom-call(s32[3]{0:T(128)S(1)} %pad_add_fusion.place_ref, f32[4,9,8,128]{3,2,1,0:T(8,128)S(1)} %get-tuple-element.13.refs_0_, f32[4,9,8,128]{3,2,1,0:T(8,128)S(1)} %collective-permute-done.refs_1_, ...), custom_call_target="tpu_custom_call" | custom-call | flops 10000000000 | bytes 100000000 | tf_op jit(solution)/shard_map/pallas_call | solution.py:370
  43.2 1.2 %collective-permute-start.10 = (f32[29,8,128]{2,1,0:T(8,128)S(1)}, f32[29,8,128]{2,1,0:T(8,128)S(1)}, u32[]{:S(2)}, u32[]{:S(2)}) collective-permute-start(f32[29,8,128]{2,1,0:T(8,128)S(1)} %get-tuple-element.18), channel_id=1, source_target_pairs={{0,6},{2,4},{4,2},{6,0},{8,14},{10,12},{12,10},{14,8},{16,22},{18,... | collective-permute-start | bytes 356360 | tf_op jit(solution)/shard_map/ppermute | solution.py:497
  44.4 0.8 %collective-permute-start.11 = (f32[29,8,128]{2,1,0:T(8,128)S(1)}, f32[29,8,128]{2,1,0:T(8,128)S(1)}, u32[]{:S(2)}, u32[]{:S(2)}) collective-permute-start(f32[29,8,128]{2,1,0:T(8,128)S(1)} %get-tuple-element.19), channel_id=1, source_target_pairs={{0,4},{2,6},{4,0},{6,2},{8,12},{10,14},{12,8},{14,10},{16,20},{18,... | collective-permute-start | bytes 356360 | tf_op jit(solution)/shard_map/ppermute | solution.py:497
  45.2 1.5 %collective-permute-start.12 = (f32[29,8,128]{2,1,0:T(8,128)S(1)}, f32[29,8,128]{2,1,0:T(8,128)S(1)}, u32[]{:S(2)}, u32[]{:S(2)}) collective-permute-start(f32[29,8,128]{2,1,0:T(8,128)S(1)} %get-tuple-element.20), channel_id=1, source_target_pairs={{0,2},{2,0},{4,6},{6,4},{8,10},{10,8},{12,14},{14,12},{16,18},{18,... | collective-permute-start | bytes 356360 | tf_op jit(solution)/shard_map/ppermute | solution.py:497
  46.7 3.0 %collective-permute-done.10.refs_1_ = f32[29,8,128]{2,1,0:T(8,128)S(1)} collective-permute-done((f32[29,8,128]{2,1,0:T(8,128)S(1)}, f32[29,8,128]{2,1,0:T(8,128)S(1)}, u32[]{:S(2)}, u32[]{:S(2)}) %collective-permute-start.10) | collective-permute-done | bytes 118816 | tf_op jit(solution)/shard_map/ppermute | solution.py:497
  49.7 1.1 %collective-permute-done.11.refs_2_ = f32[29,8,128]{2,1,0:T(8,128)S(1)} collective-permute-done((f32[29,8,128]{2,1,0:T(8,128)S(1)}, f32[29,8,128]{2,1,0:T(8,128)S(1)}, u32[]{:S(2)}, u32[]{:S(2)}) %collective-permute-start.11) | collective-permute-done | bytes 118816 | tf_op jit(solution)/shard_map/ppermute | solution.py:497
  50.8 1.5 %shard_map.66 = f32[128,900]{1,0:T(8,128)} custom-call(s32[3]{0:T(128)S(1)} %pad_add_fusion.place_ref, s32[16]{0:T(128)S(1)} %copy-done, f32[29,8,128]{2,1,0:T(8,128)S(1)} %get-tuple-element.17.refs_0_, f32[29,8,128]{2,1,0:T(8,128)S(1)} %collective-permute-done.10.refs_1_, f32[29,8,128]{2,1,0:T(8,128)S(1)} %collective-permute-done.11.refs_2_, ...), custom_call_target="tpu_custom_call" | custom-call | tf_op jit(solution)/shard_map/pallas_call | solution.py:419
  (15 shorter events, 0.1 us)
Async XLA Ops:
  0.0 17.8 %collective-permute-start.6 = (f32[300,2,120]{2,1,0:T(2,128)}, f32[300,2,120]{2,1,0:T(2,128)S(1)}, u32[]{:S(2)}, u32[]{:S(2)}) collective-permute-start(f32[300,2,120]{2,1,0:T(2,128)} %bitcast.12), channel_id=1, source_target_pairs={{0,16},{2,18},{4,20},{6,22},{8,24},{10,26},{12,28},{14,30},{16,0},... | collective-permute-start | bytes 864008 | tf_op jit(solution)/shard_map/ppermute | solution.py:497
  0.0 16.8 %collective-permute-start.3 = (f32[300,2,120]{2,1,0:T(2,128)}, f32[300,2,120]{2,1,0:T(2,128)S(1)}, u32[]{:S(2)}, u32[]{:S(2)}) collective-permute-start(f32[300,2,120]{2,1,0:T(2,128)} %bitcast.13), channel_id=1, source_target_pairs={{0,8},{2,10},{4,12},{6,14},{8,0},{10,2},{12,4},{14,6},{16,24},{18,... | collective-permute-start | bytes 864008 | tf_op jit(solution)/shard_map/ppermute | solution.py:497
  5.5 11.6 %copy-start.1 = (f32[1,2,300,120]{3,1,2,0:T(2,128)S(1)}, f32[1,2,300,120]{3,1,2,0:T(2,128)}, u32[]{:S(2)}) copy-start(f32[1,2,300,120]{3,1,2,0:T(2,128)} %param.8) | copy-start | bytes 864004
  5.5 24.9 %all-to-all-start = ((f32[16,9,8,128]{3,2,1,0:T(8,128)}), f32[16,9,8,128]{3,2,1,0:T(8,128)S(1)}, u32[]{:S(2)}, u32[]{:S(2)}) async-start(f32[16,9,8,128]{3,2,1,0:T(8,128)} %bitcast.15), calls=%async_computation | async-start | bytes 1179648 | tf_op jit(solution)/shard_map/all_to_all | solution.py:513
  17.0 2.8 %collective-permute-start.5 = (f32[2,300,128]{2,1,0:T(8,128)S(1)}, f32[2,300,128]{2,1,0:T(8,128)S(1)}, u32[]{:S(2)}, u32[]{:S(2)}) collective-permute-start(f32[2,300,128]{2,1,0:T(8,128)S(1)} %shard_map.57.refs_0_.own_ref), channel_id=1, source_target_pairs={{0,1},{1,0},{2,3},{3,2},{4,5},{5,4},{6,7},{7,6},{8,9},{9,8},{10,11... | collective-permute-start | bytes 921608 | tf_op jit(solution)/shard_map/ppermute | solution.py:501
  17.3 1.8 %collective-permute-start.4 = (f32[2,300,128]{2,1,0:T(8,128)S(1)}, f32[2,300,128]{2,1,0:T(8,128)S(1)}, u32[]{:S(2)}, u32[]{:S(2)}) collective-permute-start(f32[2,300,128]{2,1,0:T(8,128)S(1)} %shard_map.58.own_ref), channel_id=1, source_target_pairs={{0,1},{1,0},{2,3},{3,2},{4,5},{5,4},{6,7},{7,6},{8,9},{9,8},{10,11... | collective-permute-start | bytes 921608 | tf_op jit(solution)/shard_map/ppermute | solution.py:501
  18.0 16.7 %collective-permute-start.8 = (f32[2,300,128]{2,1,0:T(8,128)S(1)}, f32[2,300,128]{2,1,0:T(8,128)S(1)}, u32[]{:S(2)}, u32[]{:S(2)}) collective-permute-start(f32[2,300,128]{2,1,0:T(8,128)S(1)} %shard_map.61.own_ref), channel_id=1, source_target_pairs={{0,8},{2,10},{4,12},{6,14},{8,0},{10,2},{12,4},{14,6},{16,24},{18,... | collective-permute-start | bytes 921608 | tf_op jit(solution)/shard_map/ppermute | solution.py:497
  18.5 16.3 %collective-permute-start.7 = (f32[2,300,128]{2,1,0:T(8,128)S(1)}, f32[2,300,128]{2,1,0:T(8,128)S(1)}, u32[]{:S(2)}, u32[]{:S(2)}) collective-permute-start(f32[2,300,128]{2,1,0:T(8,128)S(1)} %shard_map.61.own_ref), channel_id=1, source_target_pairs={{0,1},{1,0},{2,3},{3,2},{4,5},{5,4},{6,7},{7,6},{8,9},{9,8},{10,11... | collective-permute-start | bytes 921608 | tf_op jit(solution)/shard_map/ppermute | solution.py:501
  19.8 10.5 %copy-start.2 = (s32[3,16]{1,0:T(4,128)S(1)}, s32[3,16]{1,0:T(4,128)}, u32[]{:S(2)}) copy-start(s32[3,16]{1,0:T(4,128)} %offset_ref.1) | copy-start | bytes 580
  31.2 6.5 %collective-permute-start = (f32[4,9,8,128]{3,2,1,0:T(8,128)S(1)}, f32[4,9,8,128]{3,2,1,0:T(8,128)S(1)}, u32[]{:S(2)}, u32[]{:S(2)}) collective-permute-start(f32[4,9,8,128]{3,2,1,0:T(8,128)S(1)} %get-tuple-element.14), channel_id=1, source_target_pairs={{0,2},{2,0},{4,6},{6,4},{8,10},{10,8},{12,14},{14,12},{16,18},{18,... | collective-permute-start | bytes 442376 | tf_op jit(solution)/shard_map/ppermute | solution.py:497
  32.8 8.6 %collective-permute-start.1 = (f32[4,9,8,128]{3,2,1,0:T(8,128)S(1)}, f32[4,9,8,128]{3,2,1,0:T(8,128)S(1)}, u32[]{:S(2)}, u32[]{:S(2)}) collective-permute-start(f32[4,9,8,128]{3,2,1,0:T(8,128)S(1)} %get-tuple-element.15), channel_id=1, source_target_pairs={{0,4},{2,6},{4,0},{6,2},{8,12},{10,14},{12,8},{14,10},{16,20},{18,... | collective-permute-start | bytes 442376 | tf_op jit(solution)/shard_map/ppermute | solution.py:497
  32.8 8.6 %collective-permute-start.2 = (f32[4,9,8,128]{3,2,1,0:T(8,128)S(1)}, f32[4,9,8,128]{3,2,1,0:T(8,128)S(1)}, u32[]{:S(2)}, u32[]{:S(2)}) collective-permute-start(f32[4,9,8,128]{3,2,1,0:T(8,128)S(1)} %get-tuple-element.16), channel_id=1, source_target_pairs={{0,6},{2,4},{4,2},{6,0},{8,14},{10,12},{12,10},{14,8},{16,22},{18,... | collective-permute-start | bytes 442376 | tf_op jit(solution)/shard_map/ppermute | solution.py:497
  34.8 1.7 %collective-permute-start.9 = (f32[2,300,128]{2,1,0:T(8,128)S(1)}, f32[2,300,128]{2,1,0:T(8,128)S(1)}, u32[]{:S(2)}, u32[]{:S(2)}) collective-permute-start(f32[2,300,128]{2,1,0:T(8,128)S(1)} %shard_map.63.own_ref), channel_id=1, source_target_pairs={{0,1},{1,0},{2,3},{3,2},{4,5},{5,4},{6,7},{7,6},{8,9},{9,8},{10,11... | collective-permute-start | bytes 921608 | tf_op jit(solution)/shard_map/ppermute | solution.py:501
  37.2 13.6 %copy-start = (s32[16]{0:T(128)S(1)}, s32[16]{0:T(128)}, u32[]{:S(2)}) copy-start(s32[16]{0:T(128)} %transfer_ref.1) | copy-start | bytes 196
  43.2 6.5 %collective-permute-start.10 = (f32[29,8,128]{2,1,0:T(8,128)S(1)}, f32[29,8,128]{2,1,0:T(8,128)S(1)}, u32[]{:S(2)}, u32[]{:S(2)}) collective-permute-start(f32[29,8,128]{2,1,0:T(8,128)S(1)} %get-tuple-element.18), channel_id=1, source_target_pairs={{0,6},{2,4},{4,2},{6,0},{8,14},{10,12},{12,10},{14,8},{16,22},{18,... | collective-permute-start | bytes 356360 | tf_op jit(solution)/shard_map/ppermute | solution.py:497
  44.4 6.4 %collective-permute-start.11 = (f32[29,8,128]{2,1,0:T(8,128)S(1)}, f32[29,8,128]{2,1,0:T(8,128)S(1)}, u32[]{:S(2)}, u32[]{:S(2)}) collective-permute-start(f32[29,8,128]{2,1,0:T(8,128)S(1)} %get-tuple-element.19), channel_id=1, source_target_pairs={{0,4},{2,6},{4,0},{6,2},{8,12},{10,14},{12,8},{14,10},{16,20},{18,... | collective-permute-start | bytes 356360 | tf_op jit(solution)/shard_map/ppermute | solution.py:497
  45.2 5.6 %collective-permute-start.12 = (f32[29,8,128]{2,1,0:T(8,128)S(1)}, f32[29,8,128]{2,1,0:T(8,128)S(1)}, u32[]{:S(2)}, u32[]{:S(2)}) collective-permute-start(f32[29,8,128]{2,1,0:T(8,128)S(1)} %get-tuple-element.20), channel_id=1, source_target_pairs={{0,2},{2,0},{4,6},{6,4},{8,10},{10,8},{12,14},{14,12},{16,18},{18,... | collective-permute-start | bytes 356360 | tf_op jit(solution)/shard_map/ppermute | solution.py:497

commit v7 on v6

--- a/solution.py
+++ b/solution.py
@@ -200,7 +200,7 @@
             pltpu.SemaphoreType.DMA((sz.slab,)),
         ],
         compiler_params=pltpu.CompilerParams(vmem_limit_bytes=60 << 20),
-        cost_estimate=cost(100000000000),
+        cost_estimate=cost(10**11),
     )(blocks[0].transpose(1, 0, 2), occ_coeff.transpose(2, 0, 1))
 
 
@@ -282,7 +282,7 @@
             pltpu.SMEM((KX * KY,), jnp.int32),
         ],
         compiler_params=pltpu.CompilerParams(vmem_limit_bytes=32 << 20),
-        cost_estimate=cost(100000000000),
+        cost_estimate=cost(10**11),
     )(place, cell_offsets, cells)
 
 
@@ -379,7 +379,7 @@
             pltpu.VMEM((KY, count, 2 * KY, LANES), F32),
         ],
         compiler_params=pltpu.CompilerParams(vmem_limit_bytes=32 << 20),
-        cost_estimate=cost(10000000000),
+        cost_estimate=cost(10**10),
     )(place, *halves, *rights)
 
 
@@ -506,20 +506,17 @@
     me = lax.axis_index("cell")
     place = jnp.stack([me // KY, me % KY, lax.axis_index("aux")]).astype(jnp.int32)
     home = vir_coeff[0].transpose(1, 0, 2)
-    across = spread(sz, swap(home, 2 * KY), 10000000000)
-    beside = spread(sz, swap(home, KY), 100000000)
+    across = spread(sz, swap(home, 2 * KY), 10**10)
+    beside = spread(sz, swap(home, KY), 10**8)
     corner = swap(across, KY)
     sent = half_bands(sz, blocks, occ_coeff).reshape(KX * KY, sz.tail + 1, SUBLANES, LANES)
     cells = lax.all_to_all(sent, "cell", split_axis=0, concat_axis=0, tiled=True)
     points = list(lattice_sum(sz, place, cell_offsets, cells))
     halves = [points[0]] + [swap(part, step) for part, step in zip(points[1:], OUT[1:])]
-    ours = spread(sz, home, 3000000000, beside)
-    if 1 == 1:
-        corner = copied(corner, points[0])
-    if 1 in (2, 3):
-        corner = copied(corner, halves[1 - 1])
-    rights = [columns(sz, place, v, swap_cores(v), 10000000000) for v in (ours, beside, across)]
-    rights.append(columns(sz, place, corner, swap_cores(corner), 1000000000))
+    ours = spread(sz, home, 3 * 10**9, beside)
+    corner = copied(corner, points[0])
+    rights = [columns(sz, place, v, swap_cores(v), 10**10) for v in (ours, beside, across)]
+    rights.append(columns(sz, place, corner, swap_cores(corner), 10**9))
     bands = band_product(sz, place, halves, rights)
     sources = [bands[0]] + [swap(band, step) for band, step in zip(bands[1:], BACK[1:])]
     out = regroup(sz, place, transfer_index, sources)

time: 52.6 us -> 52.6 us (level)
  no operation moved by 1% of the time
where the time goes in v7:
time: 52.6 us; the launch traced here: 52.3 us
  waiting for transfers between devices  24.4 us (46%)
  starting transfers between devices  16.7 us (32%)
  Pallas kernels  11 us (21%)
    ppermute x9, waiting for transfers between devices, swap(): return lax.ppermute(value, 'cell', [(d, d ^ step) for d in range(KX * KY)])  13.1 us
    all_to_all x1, waiting for transfers between devices, by_planes(): lax.all_to_all(sent, 'cell', split_axis=0, concat_axis=0, tiled=True)  9.81 us
    ppermute x9, starting transfers between devices, swap(): return lax.ppermute(value, 'cell', [(d, d ^ step) for d in range(KX * KY)])  9.54 us
    all_to_all x1, starting transfers between devices, by_planes(): lax.all_to_all(sent, 'cell', split_axis=0, concat_axis=0, tiled=True)  6.47 us
    pallas_call x1, Pallas kernels, half_bands(): pl.pallas_call(functools.partial(half_kernel, sz), out_shape=jax.ShapeDty...  3.57 us
    pallas_call x4, Pallas kernels, columns(): pl.pallas_call(functools.partial(columns_kernel, sz), out_shape=jax.Shape...  2.79 us
    pallas_call x1, Pallas kernels, band_product(): pl.pallas_call(functools.partial(band_kernel, sz), out_shape=[shape] * KY...  1.74 us
    pallas_call x1, Pallas kernels, regroup(): pl.pallas_call(functools.partial(regroup_kernel, sz), out_shape=jax.Shape...  1.51 us
  transfers between devices with their start and end apart: 14, of which 8 were waited for; matrix products, arithmetic and copies ran while one was open for 0% of the time, Pallas kernels for 15%

profile of v7, /device:TPU:16, one launch (start us, length us, event | category | flops | bytes accessed | tf_op | source)
XLA Modules:
  0.0 52.3 jit_solution(8655449458837471194)
XLA Ops:
  0.0 1.9 %collective-permute-start.3 = (f32[300,2,120]{2,1,0:T(2,128)}, f32[300,2,120]{2,1,0:T(2,128)S(1)}, u32[]{:S(2)}, u32[]{:S(2)}) collective-permute-start(f32[300,2,120]{2,1,0:T(2,128)} %bitcast.13), channel_id=1, source_target_pairs={{0,8},{2,10},{4,12},{6,14},{8,0},{10,2},{12,4},{14,6},{16,24},{18,... | collective-permute-start | bytes 864008 | tf_op jit(solution)/shard_map/ppermute | solution.py:497
  1.9 3.6 %shard_map.55 = f32[4,4,9,8,128]{4,3,2,1,0:T(8,128)} custom-call(f32[300,4,300]{2,1,0:T(4,128)} %bitcast.16, f32[60,2,300]{2,1,0:T(2,128)} %bitcast.17), custom_call_target="tpu_custom_call" | custom-call | flops 99999997952 | bytes 1000000000 | tf_op jit(solution)/shard_map/pallas_call | solution.py:189
  5.5 6.5 %all-to-all-start = ((f32[16,9,8,128]{3,2,1,0:T(8,128)}), f32[16,9,8,128]{3,2,1,0:T(8,128)S(1)}, u32[]{:S(2)}, u32[]{:S(2)}) async-start(f32[16,9,8,128]{3,2,1,0:T(8,128)} %bitcast.15), calls=%async_computation | async-start | bytes 1179648 | tf_op jit(solution)/shard_map/all_to_all | solution.py:513
  12.0 0.1 pad_add_fusion.place_ref
  12.0 4.8 %collective-permute-done.3.in_ref = f32[300,2,120]{2,1,0:T(2,128)S(1)} collective-permute-done((f32[300,2,120]{2,1,0:T(2,128)}, f32[300,2,120]{2,1,0:T(2,128)S(1)}, u32[]{:S(2)}, u32[]{:S(2)}) %collective-permute-start.3) | collective-permute-done | bytes 288032 | tf_op jit(solution)/shard_map/ppermute | solution.py:497
  16.8 0.2 shard_map.57.refs_0_.own_ref
  17.0 0.1 collective-permute-start.5
  17.1 0.2 shard_map.58.own_ref
  17.3 0.5 %collective-permute-start.4 = (f32[2,300,128]{2,1,0:T(8,128)S(1)}, f32[2,300,128]{2,1,0:T(8,128)S(1)}, u32[]{:S(2)}, u32[]{:S(2)}) collective-permute-start(f32[2,300,128]{2,1,0:T(8,128)S(1)} %shard_map.58.own_ref), channel_id=1, source_target_pairs={{0,1},{1,0},{2,3},{3,2},{4,5},{5,4},{6,7},{7,6},{8,9},{9,8},{10,11... | collective-permute-start | bytes 921608 | tf_op jit(solution)/shard_map/ppermute | solution.py:501
  17.8 0.2 shard_map.61.own_ref
  18.0 0.5 collective-permute-start.8
  18.6 0.6 %collective-permute-done.4.other_ref = f32[2,300,128]{2,1,0:T(8,128)S(1)} collective-permute-done((f32[2,300,128]{2,1,0:T(8,128)S(1)}, f32[2,300,128]{2,1,0:T(8,128)S(1)}, u32[]{:S(2)}, u32[]{:S(2)}) %collective-permute-start.4) | collective-permute-done | bytes 307232 | tf_op jit(solution)/shard_map/ppermute | solution.py:501
  19.1 0.7 %shard_map.59.refs_4_ = bf16[704,512]{1,0:T(8,128)(2,1)S(1)} custom-call(s32[3]{0:T(128)S(1)} %pad_add_fusion.place_ref, f32[2,300,128]{2,1,0:T(8,128)S(1)} %shard_map.58.own_ref, f32[2,300,128]{2,1,0:T(8,128)S(1)} %collective-permute-done.4.other_ref), custom_call_target="tpu_custom_call" | custom-call | flops 10000000000 | bytes 100000000 | tf_op jit(solution)/shard_map/pallas_call | solution.py:486
  19.9 0.7 %shard_map.60.refs_5_ = bf16[704,512]{1,0:T(8,128)(2,1)S(1)} custom-call(s32[3]{0:T(128)S(1)} %pad_add_fusion.place_ref, f32[2,300,128]{2,1,0:T(8,128)S(1)} %shard_map.57.refs_0_.own_ref, f32[2,300,128]{2,1,0:T(8,128)S(1)} %collective-permute-done.5.other_ref), custom_call_target="tpu_custom_call" | custom-call | flops 10000000000 | bytes 100000000 | tf_op jit(solution)/shard_map/pallas_call | solution.py:486
  20.6 9.8 %all-to-all-done.cells_ref = f32[16,9,8,128]{3,2,1,0:T(8,128)S(1)} async-done(((f32[16,9,8,128]{3,2,1,0:T(8,128)}), f32[16,9,8,128]{3,2,1,0:T(8,128)S(1)}, u32[]{:S(2)}, u32[]{:S(2)}) %all-to-all-start) | async-done | bytes 589856 | tf_op jit(solution)/shard_map/all_to_all | solution.py:513
  30.4 0.8 %shard_map.56 = (f32[4,9,8,128]{3,2,1,0:T(8,128)S(1)}, f32[4,9,8,128]{3,2,1,0:T(8,128)S(1)}, f32[4,9,8,128]{3,2,1,0:T(8,128)S(1)}, f32[4,9,8,128]{3,2,1,0:T(8,128)S(1)}) custom-call(s32[3]{0:T(128)S(1)} %pad_add_fusion.place_ref, s32[3,16]{1,0:T(4,128)S(1)} %copy-done.2, f32[16,9,8,128]{3,2,1,0:T(8,128)S(1)} %all-to-all-done.cells_ref), custom_call_target="tpu_custom_call" | custom-call | flops 99999997952 | bytes 1000000000 | tf_op jit(solution)/shard_map/pallas_call | solution.py:275
  31.2 1.6 %collective-permute-start = (f32[4,9,8,128]{3,2,1,0:T(8,128)S(1)}, f32[4,9,8,128]{3,2,1,0:T(8,128)S(1)}, u32[]{:S(2)}, u32[]{:S(2)}) collective-permute-start(f32[4,9,8,128]{3,2,1,0:T(8,128)S(1)} %get-tuple-element.14), channel_id=1, source_target_pairs={{0,2},{2,0},{4,6},{6,4},{8,10},{10,8},{12,14},{14,12},{16,18},{18,... | collective-permute-start | bytes 442376 | tf_op jit(solution)/shard_map/ppermute | solution.py:497
  32.8 2.0 %collective-permute-start.2 = (f32[4,9,8,128]{3,2,1,0:T(8,128)S(1)}, f32[4,9,8,128]{3,2,1,0:T(8,128)S(1)}, u32[]{:S(2)}, u32[]{:S(2)}) collective-permute-start(f32[4,9,8,128]{3,2,1,0:T(8,128)S(1)} %get-tuple-element.16), channel_id=1, source_target_pairs={{0,6},{2,4},{4,2},{6,0},{8,14},{10,12},{12,10},{14,8},{16,22},{18,... | collective-permute-start | bytes 442376 | tf_op jit(solution)/shard_map/ppermute | solution.py:497
  34.8 0.1 collective-permute-start.9
  34.9 0.7 %shard_map.62.refs_6_ = bf16[704,512]{1,0:T(8,128)(2,1)S(1)} custom-call(s32[3]{0:T(128)S(1)} %pad_add_fusion.place_ref, f32[2,300,128]{2,1,0:T(8,128)S(1)} %shard_map.61.own_ref, f32[2,300,128]{2,1,0:T(8,128)S(1)} %collective-permute-done.7.other_ref), custom_call_target="tpu_custom_call" | custom-call | flops 10000000000 | bytes 100000000 | tf_op jit(solution)/shard_map/pallas_call | solution.py:486
  35.6 0.9 %collective-permute-done.9.other_ref = f32[2,300,128]{2,1,0:T(8,128)S(1)} collective-permute-done((f32[2,300,128]{2,1,0:T(8,128)S(1)}, f32[2,300,128]{2,1,0:T(8,128)S(1)}, u32[]{:S(2)}, u32[]{:S(2)}) %collective-permute-start.9) | collective-permute-done | bytes 307232 | tf_op jit(solution)/shard_map/ppermute | solution.py:501
  36.5 0.7 %shard_map.64.refs_7_ = bf16[704,512]{1,0:T(8,128)(2,1)S(1)} custom-call(s32[3]{0:T(128)S(1)} %pad_add_fusion.place_ref, f32[2,300,128]{2,1,0:T(8,128)S(1)} %shard_map.63.own_ref, f32[2,300,128]{2,1,0:T(8,128)S(1)} %collective-permute-done.9.other_ref), custom_call_target="tpu_custom_call" | custom-call | flops 1000000000 | bytes 10000000 | tf_op jit(solution)/shard_map/pallas_call | solution.py:486
  37.2 0.0 copy-start
  37.2 0.6 %collective-permute-done.refs_1_ = f32[4,9,8,128]{3,2,1,0:T(8,128)S(1)} collective-permute-done((f32[4,9,8,128]{3,2,1,0:T(8,128)S(1)}, f32[4,9,8,128]{3,2,1,0:T(8,128)S(1)}, u32[]{:S(2)}, u32[]{:S(2)}) %collective-permute-start) | collective-permute-done | bytes 147488 | tf_op jit(solution)/shard_map/ppermute | solution.py:497
  37.7 3.7 %collective-permute-done.1.refs_2_ = f32[4,9,8,128]{3,2,1,0:T(8,128)S(1)} collective-permute-done((f32[4,9,8,128]{3,2,1,0:T(8,128)S(1)}, f32[4,9,8,128]{3,2,1,0:T(8,128)S(1)}, u32[]{:S(2)}, u32[]{:S(2)}) %collective-permute-start.1) | collective-permute-done | bytes 147488 | tf_op jit(solution)/shard_map/ppermute | solution.py:497
  41.4 1.7 %shard_map.65 = (f32[29,8,128]{2,1,0:T(8,128)S(1)}, f32[29,8,128]{2,1,0:T(8,128)S(1)}, f32[29,8,128]{2,1,0:T(8,128)S(1)}, f32[29,8,128]{2,1,0:T(8,128)S(1)}) custom-call(s32[3]{0:T(128)S(1)} %pad_add_fusion.place_ref, f32[4,9,8,128]{3,2,1,0:T(8,128)S(1)} %get-tuple-element.13.refs_0_, f32[4,9,8,128]{3,2,1,0:T(8,128)S(1)} %collective-permute-done.refs_1_, ...), custom_call_target="tpu_custom_call" | custom-call | flops 10000000000 | bytes 100000000 | tf_op jit(solution)/shard_map/pallas_call | solution.py:370
  43.2 1.2 %collective-permute-start.10 = (f32[29,8,128]{2,1,0:T(8,128)S(1)}, f32[29,8,128]{2,1,0:T(8,128)S(1)}, u32[]{:S(2)}, u32[]{:S(2)}) collective-permute-start(f32[29,8,128]{2,1,0:T(8,128)S(1)} %get-tuple-element.18), channel_id=1, source_target_pairs={{0,6},{2,4},{4,2},{6,0},{8,14},{10,12},{12,10},{14,8},{16,22},{18,... | collective-permute-start | bytes 356360 | tf_op jit(solution)/shard_map/ppermute | solution.py:497
  44.4 0.8 %collective-permute-start.11 = (f32[29,8,128]{2,1,0:T(8,128)S(1)}, f32[29,8,128]{2,1,0:T(8,128)S(1)}, u32[]{:S(2)}, u32[]{:S(2)}) collective-permute-start(f32[29,8,128]{2,1,0:T(8,128)S(1)} %get-tuple-element.19), channel_id=1, source_target_pairs={{0,4},{2,6},{4,0},{6,2},{8,12},{10,14},{12,8},{14,10},{16,20},{18,... | collective-permute-start | bytes 356360 | tf_op jit(solution)/shard_map/ppermute | solution.py:497
  45.2 1.5 %collective-permute-start.12 = (f32[29,8,128]{2,1,0:T(8,128)S(1)}, f32[29,8,128]{2,1,0:T(8,128)S(1)}, u32[]{:S(2)}, u32[]{:S(2)}) collective-permute-start(f32[29,8,128]{2,1,0:T(8,128)S(1)} %get-tuple-element.20), channel_id=1, source_target_pairs={{0,2},{2,0},{4,6},{6,4},{8,10},{10,8},{12,14},{14,12},{16,18},{18,... | collective-permute-start | bytes 356360 | tf_op jit(solution)/shard_map/ppermute | solution.py:497
  46.7 3.0 %collective-permute-done.10.refs_1_ = f32[29,8,128]{2,1,0:T(8,128)S(1)} collective-permute-done((f32[29,8,128]{2,1,0:T(8,128)S(1)}, f32[29,8,128]{2,1,0:T(8,128)S(1)}, u32[]{:S(2)}, u32[]{:S(2)}) %collective-permute-start.10) | collective-permute-done | bytes 118816 | tf_op jit(solution)/shard_map/ppermute | solution.py:497
  49.7 1.1 %collective-permute-done.11.refs_2_ = f32[29,8,128]{2,1,0:T(8,128)S(1)} collective-permute-done((f32[29,8,128]{2,1,0:T(8,128)S(1)}, f32[29,8,128]{2,1,0:T(8,128)S(1)}, u32[]{:S(2)}, u32[]{:S(2)}) %collective-permute-start.11) | collective-permute-done | bytes 118816 | tf_op jit(solution)/shard_map/ppermute | solution.py:497
  50.8 1.5 %shard_map.66 = f32[128,900]{1,0:T(8,128)} custom-call(s32[3]{0:T(128)S(1)} %pad_add_fusion.place_ref, s32[16]{0:T(128)S(1)} %copy-done, f32[29,8,128]{2,1,0:T(8,128)S(1)} %get-tuple-element.17.refs_0_, f32[29,8,128]{2,1,0:T(8,128)S(1)} %collective-permute-done.10.refs_1_, f32[29,8,128]{2,1,0:T(8,128)S(1)} %collective-permute-done.11.refs_2_, ...), custom_call_target="tpu_custom_call" | custom-call | tf_op jit(solution)/shard_map/pallas_call | solution.py:419
  (15 shorter events, 0.1 us)
Async XLA Ops:
  0.0 17.8 %collective-permute-start.6 = (f32[300,2,120]{2,1,0:T(2,128)}, f32[300,2,120]{2,1,0:T(2,128)S(1)}, u32[]{:S(2)}, u32[]{:S(2)}) collective-permute-start(f32[300,2,120]{2,1,0:T(2,128)} %bitcast.12), channel_id=1, source_target_pairs={{0,16},{2,18},{4,20},{6,22},{8,24},{10,26},{12,28},{14,30},{16,0},... | collective-permute-start | bytes 864008 | tf_op jit(solution)/shard_map/ppermute | solution.py:497
  0.0 16.8 %collective-permute-start.3 = (f32[300,2,120]{2,1,0:T(2,128)}, f32[300,2,120]{2,1,0:T(2,128)S(1)}, u32[]{:S(2)}, u32[]{:S(2)}) collective-permute-start(f32[300,2,120]{2,1,0:T(2,128)} %bitcast.13), channel_id=1, source_target_pairs={{0,8},{2,10},{4,12},{6,14},{8,0},{10,2},{12,4},{14,6},{16,24},{18,... | collective-permute-start | bytes 864008 | tf_op jit(solution)/shard_map/ppermute | solution.py:497
  5.5 11.6 %copy-start.1 = (f32[1,2,300,120]{3,1,2,0:T(2,128)S(1)}, f32[1,2,300,120]{3,1,2,0:T(2,128)}, u32[]{:S(2)}) copy-start(f32[1,2,300,120]{3,1,2,0:T(2,128)} %param.8) | copy-start | bytes 864004
  5.5 24.9 %all-to-all-start = ((f32[16,9,8,128]{3,2,1,0:T(8,128)}), f32[16,9,8,128]{3,2,1,0:T(8,128)S(1)}, u32[]{:S(2)}, u32[]{:S(2)}) async-start(f32[16,9,8,128]{3,2,1,0:T(8,128)} %bitcast.15), calls=%async_computation | async-start | bytes 1179648 | tf_op jit(solution)/shard_map/all_to_all | solution.py:513
  17.0 2.8 %collective-permute-start.5 = (f32[2,300,128]{2,1,0:T(8,128)S(1)}, f32[2,300,128]{2,1,0:T(8,128)S(1)}, u32[]{:S(2)}, u32[]{:S(2)}) collective-permute-start(f32[2,300,128]{2,1,0:T(8,128)S(1)} %shard_map.57.refs_0_.own_ref), channel_id=1, source_target_pairs={{0,1},{1,0},{2,3},{3,2},{4,5},{5,4},{6,7},{7,6},{8,9},{9,8},{10,11... | collective-permute-start | bytes 921608 | tf_op jit(solution)/shard_map/ppermute | solution.py:501
  17.3 1.8 %collective-permute-start.4 = (f32[2,300,128]{2,1,0:T(8,128)S(1)}, f32[2,300,128]{2,1,0:T(8,128)S(1)}, u32[]{:S(2)}, u32[]{:S(2)}) collective-permute-start(f32[2,300,128]{2,1,0:T(8,128)S(1)} %shard_map.58.own_ref), channel_id=1, source_target_pairs={{0,1},{1,0},{2,3},{3,2},{4,5},{5,4},{6,7},{7,6},{8,9},{9,8},{10,11... | collective-permute-start | bytes 921608 | tf_op jit(solution)/shard_map/ppermute | solution.py:501
  18.0 16.7 %collective-permute-start.8 = (f32[2,300,128]{2,1,0:T(8,128)S(1)}, f32[2,300,128]{2,1,0:T(8,128)S(1)}, u32[]{:S(2)}, u32[]{:S(2)}) collective-permute-start(f32[2,300,128]{2,1,0:T(8,128)S(1)} %shard_map.61.own_ref), channel_id=1, source_target_pairs={{0,8},{2,10},{4,12},{6,14},{8,0},{10,2},{12,4},{14,6},{16,24},{18,... | collective-permute-start | bytes 921608 | tf_op jit(solution)/shard_map/ppermute | solution.py:497
  18.5 16.3 %collective-permute-start.7 = (f32[2,300,128]{2,1,0:T(8,128)S(1)}, f32[2,300,128]{2,1,0:T(8,128)S(1)}, u32[]{:S(2)}, u32[]{:S(2)}) collective-permute-start(f32[2,300,128]{2,1,0:T(8,128)S(1)} %shard_map.61.own_ref), channel_id=1, source_target_pairs={{0,1},{1,0},{2,3},{3,2},{4,5},{5,4},{6,7},{7,6},{8,9},{9,8},{10,11... | collective-permute-start | bytes 921608 | tf_op jit(solution)/shard_map/ppermute | solution.py:501
  19.8 10.5 %copy-start.2 = (s32[3,16]{1,0:T(4,128)S(1)}, s32[3,16]{1,0:T(4,128)}, u32[]{:S(2)}) copy-start(s32[3,16]{1,0:T(4,128)} %offset_ref.1) | copy-start | bytes 580
  31.2 6.5 %collective-permute-start = (f32[4,9,8,128]{3,2,1,0:T(8,128)S(1)}, f32[4,9,8,128]{3,2,1,0:T(8,128)S(1)}, u32[]{:S(2)}, u32[]{:S(2)}) collective-permute-start(f32[4,9,8,128]{3,2,1,0:T(8,128)S(1)} %get-tuple-element.14), channel_id=1, source_target_pairs={{0,2},{2,0},{4,6},{6,4},{8,10},{10,8},{12,14},{14,12},{16,18},{18,... | collective-permute-start | bytes 442376 | tf_op jit(solution)/shard_map/ppermute | solution.py:497
  32.8 8.6 %collective-permute-start.1 = (f32[4,9,8,128]{3,2,1,0:T(8,128)S(1)}, f32[4,9,8,128]{3,2,1,0:T(8,128)S(1)}, u32[]{:S(2)}, u32[]{:S(2)}) collective-permute-start(f32[4,9,8,128]{3,2,1,0:T(8,128)S(1)} %get-tuple-element.15), channel_id=1, source_target_pairs={{0,4},{2,6},{4,0},{6,2},{8,12},{10,14},{12,8},{14,10},{16,20},{18,... | collective-permute-start | bytes 442376 | tf_op jit(solution)/shard_map/ppermute | solution.py:497
  32.8 8.6 %collective-permute-start.2 = (f32[4,9,8,128]{3,2,1,0:T(8,128)S(1)}, f32[4,9,8,128]{3,2,1,0:T(8,128)S(1)}, u32[]{:S(2)}, u32[]{:S(2)}) collective-permute-start(f32[4,9,8,128]{3,2,1,0:T(8,128)S(1)} %get-tuple-element.16), channel_id=1, source_target_pairs={{0,6},{2,4},{4,2},{6,0},{8,14},{10,12},{12,10},{14,8},{16,22},{18,... | collective-permute-start | bytes 442376 | tf_op jit(solution)/shard_map/ppermute | solution.py:497
  34.8 1.7 %collective-permute-start.9 = (f32[2,300,128]{2,1,0:T(8,128)S(1)}, f32[2,300,128]{2,1,0:T(8,128)S(1)}, u32[]{:S(2)}, u32[]{:S(2)}) collective-permute-start(f32[2,300,128]{2,1,0:T(8,128)S(1)} %shard_map.63.own_ref), channel_id=1, source_target_pairs={{0,1},{1,0},{2,3},{3,2},{4,5},{5,4},{6,7},{7,6},{8,9},{9,8},{10,11... | collective-permute-start | bytes 921608 | tf_op jit(solution)/shard_map/ppermute | solution.py:501
  37.2 13.6 %copy-start = (s32[16]{0:T(128)S(1)}, s32[16]{0:T(128)}, u32[]{:S(2)}) copy-start(s32[16]{0:T(128)} %transfer_ref.1) | copy-start | bytes 196
  43.2 6.5 %collective-permute-start.10 = (f32[29,8,128]{2,1,0:T(8,128)S(1)}, f32[29,8,128]{2,1,0:T(8,128)S(1)}, u32[]{:S(2)}, u32[]{:S(2)}) collective-permute-start(f32[29,8,128]{2,1,0:T(8,128)S(1)} %get-tuple-element.18), channel_id=1, source_target_pairs={{0,6},{2,4},{4,2},{6,0},{8,14},{10,12},{12,10},{14,8},{16,22},{18,... | collective-permute-start | bytes 356360 | tf_op jit(solution)/shard_map/ppermute | solution.py:497
  44.4 6.4 %collective-permute-start.11 = (f32[29,8,128]{2,1,0:T(8,128)S(1)}, f32[29,8,128]{2,1,0:T(8,128)S(1)}, u32[]{:S(2)}, u32[]{:S(2)}) collective-permute-start(f32[29,8,128]{2,1,0:T(8,128)S(1)} %get-tuple-element.19), channel_id=1, source_target_pairs={{0,4},{2,6},{4,0},{6,2},{8,12},{10,14},{12,8},{14,10},{16,20},{18,... | collective-permute-start | bytes 356360 | tf_op jit(solution)/shard_map/ppermute | solution.py:497
  45.2 5.6 %collective-permute-start.12 = (f32[29,8,128]{2,1,0:T(8,128)S(1)}, f32[29,8,128]{2,1,0:T(8,128)S(1)}, u32[]{:S(2)}, u32[]{:S(2)}) collective-permute-start(f32[29,8,128]{2,1,0:T(8,128)S(1)} %get-tuple-element.20), channel_id=1, source_target_pairs={{0,2},{2,0},{4,6},{6,4},{8,10},{10,8},{12,14},{14,12},{16,18},{18,... | collective-permute-start | bytes 356360 | tf_op jit(solution)/shard_map/ppermute | solution.py:497

commit v8 on v7

--- a/solution.py
+++ b/solution.py
@@ -506,7 +506,7 @@
     me = lax.axis_index("cell")
     place = jnp.stack([me // KY, me % KY, lax.axis_index("aux")]).astype(jnp.int32)
     home = vir_coeff[0].transpose(1, 0, 2)
-    across = spread(sz, swap(home, 2 * KY), 10**10)
+    across = spread(sz, swap(home, 3 * KY), 10**10)
     beside = spread(sz, swap(home, KY), 10**8)
     corner = swap(across, KY)
     sent = half_bands(sz, blocks, occ_coeff).reshape(KX * KY, sz.tail + 1, SUBLANES, LANES)
@@ -516,7 +516,7 @@
     ours = spread(sz, home, 3 * 10**9, beside)
     corner = copied(corner, points[0])
     rights = [columns(sz, place, v, swap_cores(v), 10**10) for v in (ours, beside, across)]
-    rights.append(columns(sz, place, corner, swap_cores(corner), 10**9))
+    rights.insert(2, columns(sz, place, corner, swap_cores(corner), 10**9))
     bands = band_product(sz, place, halves, rights)
     sources = [bands[0]] + [swap(band, step) for band, step in zip(bands[1:], BACK[1:])]
     out = regroup(sz, place, transfer_index, sources)

time: 52.6 us -> 51.4 us (0.977)
  the two profiles are of different devices: /device:TPU:16 before, /device:TPU:0 now
where the time goes in v8:
time: 51.4 us; the launch traced here: 51.2 us
  waiting for transfers between devices  21.2 us (41%)
  starting transfers between devices  18.7 us (36%)
  Pallas kernels  11 us (21%)
    ppermute x9, waiting for transfers between devices, swap(): return lax.ppermute(value, 'cell', [(d, d ^ step) for d in range(KX * KY)])  13.9 us
    ppermute x9, starting transfers between devices, swap(): return lax.ppermute(value, 'cell', [(d, d ^ step) for d in range(KX * KY)])  12.5 us
    all_to_all x1, waiting for transfers between devices, by_planes(): lax.all_to_all(sent, 'cell', split_axis=0, concat_axis=0, tiled=True)  5.7 us
    all_to_all x1, starting transfers between devices, by_planes(): lax.all_to_all(sent, 'cell', split_axis=0, concat_axis=0, tiled=True)  5.42 us
    pallas_call x1, Pallas kernels, half_bands(): pl.pallas_call(functools.partial(half_kernel, sz), out_shape=jax.ShapeDty...  3.57 us
    pallas_call x4, Pallas kernels, columns(): pl.pallas_call(functools.partial(columns_kernel, sz), out_shape=jax.Shape...  2.79 us
    pallas_call x1, Pallas kernels, band_product(): pl.pallas_call(functools.partial(band_kernel, sz), out_shape=[shape] * KY...  1.73 us
    ppermute x4, waiting for transfers between devices, swap_cores(): return lax.ppermute(value, 'aux', [(0, 1), (1, 0)])  1.56 us
  transfers between devices with their start and end apart: 14, of which 9 were waited for; matrix products, arithmetic and copies ran while one was open for 0% of the time, Pallas kernels for 15%

profile of v8, /device:TPU:0, one launch (start us, length us, event | category | flops | bytes accessed | tf_op | source)
XLA Modules:
  0.0 51.2 jit_solution(8742643659557233085)
XLA Ops:
  0.0 5.0 %collective-permute-start.6 = (f32[300,2,120]{2,1,0:T(2,128)}, f32[300,2,120]{2,1,0:T(2,128)S(1)}, u32[]{:S(2)}, u32[]{:S(2)}) collective-permute-start(f32[300,2,120]{2,1,0:T(2,128)} %bitcast.12), channel_id=1, source_target_pairs={{0,24},{2,26},{4,28},{6,30},{8,16},{10,18},{12,20},{14,22},{16,8},... | collective-permute-start | bytes 864008 | tf_op jit(solution)/shard_map/ppermute | solution.py:497
  5.1 3.6 %shard_map.55 = f32[4,4,9,8,128]{4,3,2,1,0:T(8,128)} custom-call(f32[300,4,300]{2,1,0:T(4,128)} %bitcast.16, f32[60,2,300]{2,1,0:T(2,128)} %bitcast.17), custom_call_target="tpu_custom_call" | custom-call | flops 99999997952 | bytes 1000000000 | tf_op jit(solution)/shard_map/pallas_call | solution.py:189
  8.6 5.4 %all-to-all-start = ((f32[16,9,8,128]{3,2,1,0:T(8,128)}), f32[16,9,8,128]{3,2,1,0:T(8,128)S(1)}, u32[]{:S(2)}, u32[]{:S(2)}) async-start(f32[16,9,8,128]{3,2,1,0:T(8,128)} %bitcast.15), calls=%async_computation | async-start | bytes 1179648 | tf_op jit(solution)/shard_map/all_to_all | solution.py:513
  14.1 0.1 pad_add_fusion.place_ref
  14.2 7.5 %collective-permute-done.3.in_ref = f32[300,2,120]{2,1,0:T(2,128)S(1)} collective-permute-done((f32[300,2,120]{2,1,0:T(2,128)}, f32[300,2,120]{2,1,0:T(2,128)S(1)}, u32[]{:S(2)}, u32[]{:S(2)}) %collective-permute-start.3) | collective-permute-done | bytes 288032 | tf_op jit(solution)/shard_map/ppermute | solution.py:497
  21.7 0.2 shard_map.57.refs_0_.own_ref
  22.0 0.2 shard_map.58.own_ref
  22.2 0.5 %collective-permute-start.4 = (f32[2,300,128]{2,1,0:T(8,128)S(1)}, f32[2,300,128]{2,1,0:T(8,128)S(1)}, u32[]{:S(2)}, u32[]{:S(2)}) collective-permute-start(f32[2,300,128]{2,1,0:T(8,128)S(1)} %shard_map.58.own_ref), channel_id=1, source_target_pairs={{0,1},{1,0},{2,3},{3,2},{4,5},{5,4},{6,7},{7,6},{8,9},{9,8},{10,11... | collective-permute-start | bytes 921608 | tf_op jit(solution)/shard_map/ppermute | solution.py:501
  22.7 0.2 shard_map.61.own_ref
  22.9 0.1 collective-permute-start.9
  23.0 0.3 collective-permute-start.7
  23.3 0.7 %collective-permute-done.4.other_ref = f32[2,300,128]{2,1,0:T(8,128)S(1)} collective-permute-done((f32[2,300,128]{2,1,0:T(8,128)S(1)}, f32[2,300,128]{2,1,0:T(8,128)S(1)}, u32[]{:S(2)}, u32[]{:S(2)}) %collective-permute-start.4) | collective-permute-done | bytes 307232 | tf_op jit(solution)/shard_map/ppermute | solution.py:501
  24.0 0.7 %shard_map.59.refs_4_ = bf16[704,512]{1,0:T(8,128)(2,1)S(1)} custom-call(s32[3]{0:T(128)S(1)} %pad_add_fusion.place_ref, f32[2,300,128]{2,1,0:T(8,128)S(1)} %shard_map.58.own_ref, f32[2,300,128]{2,1,0:T(8,128)S(1)} %collective-permute-done.4.other_ref), custom_call_target="tpu_custom_call" | custom-call | flops 10000000000 | bytes 100000000 | tf_op jit(solution)/shard_map/pallas_call | solution.py:486
  24.7 0.7 %shard_map.60.refs_5_ = bf16[704,512]{1,0:T(8,128)(2,1)S(1)} custom-call(s32[3]{0:T(128)S(1)} %pad_add_fusion.place_ref, f32[2,300,128]{2,1,0:T(8,128)S(1)} %shard_map.57.refs_0_.own_ref, f32[2,300,128]{2,1,0:T(8,128)S(1)} %collective-permute-done.5.other_ref), custom_call_target="tpu_custom_call" | custom-call | flops 10000000000 | bytes 100000000 | tf_op jit(solution)/shard_map/pallas_call | solution.py:486
  25.5 5.7 %all-to-all-done.cells_ref = f32[16,9,8,128]{3,2,1,0:T(8,128)S(1)} async-done(((f32[16,9,8,128]{3,2,1,0:T(8,128)}), f32[16,9,8,128]{3,2,1,0:T(8,128)S(1)}, u32[]{:S(2)}, u32[]{:S(2)}) %all-to-all-start) | async-done | bytes 589856 | tf_op jit(solution)/shard_map/all_to_all | solution.py:513
  31.2 0.8 %shard_map.56 = (f32[4,9,8,128]{3,2,1,0:T(8,128)S(1)}, f32[4,9,8,128]{3,2,1,0:T(8,128)S(1)}, f32[4,9,8,128]{3,2,1,0:T(8,128)S(1)}, f32[4,9,8,128]{3,2,1,0:T(8,128)S(1)}) custom-call(s32[3]{0:T(128)S(1)} %pad_add_fusion.place_ref, s32[3,16]{1,0:T(4,128)S(1)} %copy-done.2, f32[16,9,8,128]{3,2,1,0:T(8,128)S(1)} %all-to-all-done.cells_ref), custom_call_target="tpu_custom_call" | custom-call | flops 99999997952 | bytes 1000000000 | tf_op jit(solution)/shard_map/pallas_call | solution.py:275
  32.0 1.1 %collective-permute-start = (f32[4,9,8,128]{3,2,1,0:T(8,128)S(1)}, f32[4,9,8,128]{3,2,1,0:T(8,128)S(1)}, u32[]{:S(2)}, u32[]{:S(2)}) collective-permute-start(f32[4,9,8,128]{3,2,1,0:T(8,128)S(1)} %get-tuple-element.14), channel_id=1, source_target_pairs={{0,2},{2,0},{4,6},{6,4},{8,10},{10,8},{12,14},{14,12},{16,18},{18,... | collective-permute-start | bytes 442376 | tf_op jit(solution)/shard_map/ppermute | solution.py:497
  33.0 1.0 %collective-permute-start.1 = (f32[4,9,8,128]{3,2,1,0:T(8,128)S(1)}, f32[4,9,8,128]{3,2,1,0:T(8,128)S(1)}, u32[]{:S(2)}, u32[]{:S(2)}) collective-permute-start(f32[4,9,8,128]{3,2,1,0:T(8,128)S(1)} %get-tuple-element.15), channel_id=1, source_target_pairs={{0,4},{2,6},{4,0},{6,2},{8,12},{10,14},{12,8},{14,10},{16,20},{18,... | collective-permute-start | bytes 442376 | tf_op jit(solution)/shard_map/ppermute | solution.py:497
  34.0 1.5 %collective-permute-start.2 = (f32[4,9,8,128]{3,2,1,0:T(8,128)S(1)}, f32[4,9,8,128]{3,2,1,0:T(8,128)S(1)}, u32[]{:S(2)}, u32[]{:S(2)}) collective-permute-start(f32[4,9,8,128]{3,2,1,0:T(8,128)S(1)} %get-tuple-element.16), channel_id=1, source_target_pairs={{0,6},{2,4},{4,2},{6,0},{8,14},{10,12},{12,10},{14,8},{16,22},{18,... | collective-permute-start | bytes 442376 | tf_op jit(solution)/shard_map/ppermute | solution.py:497
  35.6 0.7 %shard_map.64.refs_7_ = bf16[704,512]{1,0:T(8,128)(2,1)S(1)} custom-call(s32[3]{0:T(128)S(1)} %pad_add_fusion.place_ref, f32[2,300,128]{2,1,0:T(8,128)S(1)} %shard_map.61.own_ref, f32[2,300,128]{2,1,0:T(8,128)S(1)} %collective-permute-done.9.other_ref), custom_call_target="tpu_custom_call" | custom-call | flops 10000000000 | bytes 100000000 | tf_op jit(solution)/shard_map/pallas_call | solution.py:486
  36.4 0.9 %collective-permute-done.8.other_ref = f32[2,300,128]{2,1,0:T(8,128)S(1)} collective-permute-done((f32[2,300,128]{2,1,0:T(8,128)S(1)}, f32[2,300,128]{2,1,0:T(8,128)S(1)}, u32[]{:S(2)}, u32[]{:S(2)}) %collective-permute-start.8) | collective-permute-done | bytes 307232 | tf_op jit(solution)/shard_map/ppermute | solution.py:501
  37.2 0.7 %shard_map.63.refs_6_ = bf16[704,512]{1,0:T(8,128)(2,1)S(1)} custom-call(s32[3]{0:T(128)S(1)} %pad_add_fusion.place_ref, f32[2,300,128]{2,1,0:T(8,128)S(1)} %shard_map.62.own_ref, f32[2,300,128]{2,1,0:T(8,128)S(1)} %collective-permute-done.8.other_ref), custom_call_target="tpu_custom_call" | custom-call | flops 1000000000 | bytes 10000000 | tf_op jit(solution)/shard_map/pallas_call | solution.py:486
  38.0 0.3 collective-permute-done.1.refs_2_
  38.3 1.8 %collective-permute-done.2.refs_3_ = f32[4,9,8,128]{3,2,1,0:T(8,128)S(1)} collective-permute-done((f32[4,9,8,128]{3,2,1,0:T(8,128)S(1)}, f32[4,9,8,128]{3,2,1,0:T(8,128)S(1)}, u32[]{:S(2)}, u32[]{:S(2)}) %collective-permute-start.2) | collective-permute-done | bytes 147488 | tf_op jit(solution)/shard_map/ppermute | solution.py:497
  40.0 1.7 %shard_map.65 = (f32[29,8,128]{2,1,0:T(8,128)S(1)}, f32[29,8,128]{2,1,0:T(8,128)S(1)}, f32[29,8,128]{2,1,0:T(8,128)S(1)}, f32[29,8,128]{2,1,0:T(8,128)S(1)}) custom-call(s32[3]{0:T(128)S(1)} %pad_add_fusion.place_ref, f32[4,9,8,128]{3,2,1,0:T(8,128)S(1)} %get-tuple-element.13.refs_0_, f32[4,9,8,128]{3,2,1,0:T(8,128)S(1)} %collective-permute-done.refs_1_, ...), custom_call_target="tpu_custom_call" | custom-call | flops 10000000000 | bytes 100000000 | tf_op jit(solution)/shard_map/pallas_call | solution.py:370
  41.8 1.7 %collective-permute-start.10 = (f32[29,8,128]{2,1,0:T(8,128)S(1)}, f32[29,8,128]{2,1,0:T(8,128)S(1)}, u32[]{:S(2)}, u32[]{:S(2)}) collective-permute-start(f32[29,8,128]{2,1,0:T(8,128)S(1)} %get-tuple-element.18), channel_id=1, source_target_pairs={{0,6},{2,4},{4,2},{6,0},{8,14},{10,12},{12,10},{14,8},{16,22},{18,... | collective-permute-start | bytes 356360 | tf_op jit(solution)/shard_map/ppermute | solution.py:497
  43.5 1.3 %collective-permute-start.11 = (f32[29,8,128]{2,1,0:T(8,128)S(1)}, f32[29,8,128]{2,1,0:T(8,128)S(1)}, u32[]{:S(2)}, u32[]{:S(2)}) collective-permute-start(f32[29,8,128]{2,1,0:T(8,128)S(1)} %get-tuple-element.19), channel_id=1, source_target_pairs={{0,4},{2,6},{4,0},{6,2},{8,12},{10,14},{12,8},{14,10},{16,20},{18,... | collective-permute-start | bytes 356360 | tf_op jit(solution)/shard_map/ppermute | solution.py:497
  44.8 0.5 %collective-permute-start.12 = (f32[29,8,128]{2,1,0:T(8,128)S(1)}, f32[29,8,128]{2,1,0:T(8,128)S(1)}, u32[]{:S(2)}, u32[]{:S(2)}) collective-permute-start(f32[29,8,128]{2,1,0:T(8,128)S(1)} %get-tuple-element.20), channel_id=1, source_target_pairs={{0,2},{2,0},{4,6},{6,4},{8,10},{10,8},{12,14},{14,12},{16,18},{18,... | collective-permute-start | bytes 356360 | tf_op jit(solution)/shard_map/ppermute | solution.py:497
  45.3 3.0 %collective-permute-done.10.refs_1_ = f32[29,8,128]{2,1,0:T(8,128)S(1)} collective-permute-done((f32[29,8,128]{2,1,0:T(8,128)S(1)}, f32[29,8,128]{2,1,0:T(8,128)S(1)}, u32[]{:S(2)}, u32[]{:S(2)}) %collective-permute-start.10) | collective-permute-done | bytes 118816 | tf_op jit(solution)/shard_map/ppermute | solution.py:497
  48.4 0.8 %collective-permute-done.11.refs_2_ = f32[29,8,128]{2,1,0:T(8,128)S(1)} collective-permute-done((f32[29,8,128]{2,1,0:T(8,128)S(1)}, f32[29,8,128]{2,1,0:T(8,128)S(1)}, u32[]{:S(2)}, u32[]{:S(2)}) %collective-permute-start.11) | collective-permute-done | bytes 118816 | tf_op jit(solution)/shard_map/ppermute | solution.py:497
  49.2 0.5 collective-permute-done.12.refs_3_
  49.6 1.5 %shard_map.66 = f32[128,900]{1,0:T(8,128)} custom-call(s32[3]{0:T(128)S(1)} %pad_add_fusion.place_ref, s32[16]{0:T(128)S(1)} %copy-done, f32[29,8,128]{2,1,0:T(8,128)S(1)} %get-tuple-element.17.refs_0_, f32[29,8,128]{2,1,0:T(8,128)S(1)} %collective-permute-done.10.refs_1_, f32[29,8,128]{2,1,0:T(8,128)S(1)} %collective-permute-done.11.refs_2_, ...), custom_call_target="tpu_custom_call" | custom-call | tf_op jit(solution)/shard_map/pallas_call | solution.py:419
  (15 shorter events, 0.2 us)
Async XLA Ops:
  0.0 22.7 %collective-permute-start.6 = (f32[300,2,120]{2,1,0:T(2,128)}, f32[300,2,120]{2,1,0:T(2,128)S(1)}, u32[]{:S(2)}, u32[]{:S(2)}) collective-permute-start(f32[300,2,120]{2,1,0:T(2,128)} %bitcast.12), channel_id=1, source_target_pairs={{0,24},{2,26},{4,28},{6,30},{8,16},{10,18},{12,20},{14,22},{16,8},... | collective-permute-start | bytes 864008 | tf_op jit(solution)/shard_map/ppermute | solution.py:497
  5.0 16.7 %collective-permute-start.3 = (f32[300,2,120]{2,1,0:T(2,128)}, f32[300,2,120]{2,1,0:T(2,128)S(1)}, u32[]{:S(2)}, u32[]{:S(2)}) collective-permute-start(f32[300,2,120]{2,1,0:T(2,128)} %bitcast.13), channel_id=1, source_target_pairs={{0,8},{2,10},{4,12},{6,14},{8,0},{10,2},{12,4},{14,6},{16,24},{18,... | collective-permute-start | bytes 864008 | tf_op jit(solution)/shard_map/ppermute | solution.py:497
  8.6 13.3 %copy-start.1 = (f32[1,2,300,120]{3,1,2,0:T(2,128)S(1)}, f32[1,2,300,120]{3,1,2,0:T(2,128)}, u32[]{:S(2)}) copy-start(f32[1,2,300,120]{3,1,2,0:T(2,128)} %param.8) | copy-start | bytes 864004
  8.6 22.5 %all-to-all-start = ((f32[16,9,8,128]{3,2,1,0:T(8,128)}), f32[16,9,8,128]{3,2,1,0:T(8,128)S(1)}, u32[]{:S(2)}, u32[]{:S(2)}) async-start(f32[16,9,8,128]{3,2,1,0:T(8,128)} %bitcast.15), calls=%async_computation | async-start | bytes 1179648 | tf_op jit(solution)/shard_map/all_to_all | solution.py:513
  21.9 2.8 %collective-permute-start.5 = (f32[2,300,128]{2,1,0:T(8,128)S(1)}, f32[2,300,128]{2,1,0:T(8,128)S(1)}, u32[]{:S(2)}, u32[]{:S(2)}) collective-permute-start(f32[2,300,128]{2,1,0:T(8,128)S(1)} %shard_map.57.refs_0_.own_ref), channel_id=1, source_target_pairs={{0,1},{1,0},{2,3},{3,2},{4,5},{5,4},{6,7},{7,6},{8,9},{9,8},{10,11... | collective-permute-start | bytes 921608 | tf_op jit(solution)/shard_map/ppermute | solution.py:501
  22.2 1.8 %collective-permute-start.4 = (f32[2,300,128]{2,1,0:T(8,128)S(1)}, f32[2,300,128]{2,1,0:T(8,128)S(1)}, u32[]{:S(2)}, u32[]{:S(2)}) collective-permute-start(f32[2,300,128]{2,1,0:T(8,128)S(1)} %shard_map.58.own_ref), channel_id=1, source_target_pairs={{0,1},{1,0},{2,3},{3,2},{4,5},{5,4},{6,7},{7,6},{8,9},{9,8},{10,11... | collective-permute-start | bytes 921608 | tf_op jit(solution)/shard_map/ppermute | solution.py:501
  22.9 12.7 %collective-permute-start.9 = (f32[2,300,128]{2,1,0:T(8,128)S(1)}, f32[2,300,128]{2,1,0:T(8,128)S(1)}, u32[]{:S(2)}, u32[]{:S(2)}) collective-permute-start(f32[2,300,128]{2,1,0:T(8,128)S(1)} %shard_map.61.own_ref), channel_id=1, source_target_pairs={{0,1},{1,0},{2,3},{3,2},{4,5},{5,4},{6,7},{7,6},{8,9},{9,8},{10,11... | collective-permute-start | bytes 921608 | tf_op jit(solution)/shard_map/ppermute | solution.py:501
  23.0 12.5 %collective-permute-start.7 = (f32[2,300,128]{2,1,0:T(8,128)S(1)}, f32[2,300,128]{2,1,0:T(8,128)S(1)}, u32[]{:S(2)}, u32[]{:S(2)}) collective-permute-start(f32[2,300,128]{2,1,0:T(8,128)S(1)} %shard_map.61.own_ref), channel_id=1, source_target_pairs={{0,8},{2,10},{4,12},{6,14},{8,0},{10,2},{12,4},{14,6},{16,24},{18,... | collective-permute-start | bytes 921608 | tf_op jit(solution)/shard_map/ppermute | solution.py:497
  24.7 6.4 %copy-start.2 = (s32[3,16]{1,0:T(4,128)S(1)}, s32[3,16]{1,0:T(4,128)}, u32[]{:S(2)}) copy-start(s32[3,16]{1,0:T(4,128)} %offset_ref.1) | copy-start | bytes 580
  32.0 6.0 %collective-permute-start = (f32[4,9,8,128]{3,2,1,0:T(8,128)S(1)}, f32[4,9,8,128]{3,2,1,0:T(8,128)S(1)}, u32[]{:S(2)}, u32[]{:S(2)}) collective-permute-start(f32[4,9,8,128]{3,2,1,0:T(8,128)S(1)} %get-tuple-element.14), channel_id=1, source_target_pairs={{0,2},{2,0},{4,6},{6,4},{8,10},{10,8},{12,14},{14,12},{16,18},{18,... | collective-permute-start | bytes 442376 | tf_op jit(solution)/shard_map/ppermute | solution.py:497
  33.0 5.2 %collective-permute-start.1 = (f32[4,9,8,128]{3,2,1,0:T(8,128)S(1)}, f32[4,9,8,128]{3,2,1,0:T(8,128)S(1)}, u32[]{:S(2)}, u32[]{:S(2)}) collective-permute-start(f32[4,9,8,128]{3,2,1,0:T(8,128)S(1)} %get-tuple-element.15), channel_id=1, source_target_pairs={{0,4},{2,6},{4,0},{6,2},{8,12},{10,14},{12,8},{14,10},{16,20},{18,... | collective-permute-start | bytes 442376 | tf_op jit(solution)/shard_map/ppermute | solution.py:497
  34.0 6.0 %collective-permute-start.2 = (f32[4,9,8,128]{3,2,1,0:T(8,128)S(1)}, f32[4,9,8,128]{3,2,1,0:T(8,128)S(1)}, u32[]{:S(2)}, u32[]{:S(2)}) collective-permute-start(f32[4,9,8,128]{3,2,1,0:T(8,128)S(1)} %get-tuple-element.16), channel_id=1, source_target_pairs={{0,6},{2,4},{4,2},{6,0},{8,14},{10,12},{12,10},{14,8},{16,22},{18,... | collective-permute-start | bytes 442376 | tf_op jit(solution)/shard_map/ppermute | solution.py:497
  35.6 1.7 %collective-permute-start.8 = (f32[2,300,128]{2,1,0:T(8,128)S(1)}, f32[2,300,128]{2,1,0:T(8,128)S(1)}, u32[]{:S(2)}, u32[]{:S(2)}) collective-permute-start(f32[2,300,128]{2,1,0:T(8,128)S(1)} %shard_map.62.own_ref), channel_id=1, source_target_pairs={{0,1},{1,0},{2,3},{3,2},{4,5},{5,4},{6,7},{7,6},{8,9},{9,8},{10,11... | collective-permute-start | bytes 921608 | tf_op jit(solution)/shard_map/ppermute | solution.py:501
  37.9 11.7 %copy-start = (s32[16]{0:T(128)S(1)}, s32[16]{0:T(128)}, u32[]{:S(2)}) copy-start(s32[16]{0:T(128)} %transfer_ref.1) | copy-start | bytes 196
  41.8 6.6 %collective-permute-start.10 = (f32[29,8,128]{2,1,0:T(8,128)S(1)}, f32[29,8,128]{2,1,0:T(8,128)S(1)}, u32[]{:S(2)}, u32[]{:S(2)}) collective-permute-start(f32[29,8,128]{2,1,0:T(8,128)S(1)} %get-tuple-element.18), channel_id=1, source_target_pairs={{0,6},{2,4},{4,2},{6,0},{8,14},{10,12},{12,10},{14,8},{16,22},{18,... | collective-permute-start | bytes 356360 | tf_op jit(solution)/shard_map/ppermute | solution.py:497
  43.5 5.7 %collective-permute-start.11 = (f32[29,8,128]{2,1,0:T(8,128)S(1)}, f32[29,8,128]{2,1,0:T(8,128)S(1)}, u32[]{:S(2)}, u32[]{:S(2)}) collective-permute-start(f32[29,8,128]{2,1,0:T(8,128)S(1)} %get-tuple-element.19), channel_id=1, source_target_pairs={{0,4},{2,6},{4,0},{6,2},{8,12},{10,14},{12,8},{14,10},{16,20},{18,... | collective-permute-start | bytes 356360 | tf_op jit(solution)/shard_map/ppermute | solution.py:497
  44.8 4.8 %collective-permute-start.12 = (f32[29,8,128]{2,1,0:T(8,128)S(1)}, f32[29,8,128]{2,1,0:T(8,128)S(1)}, u32[]{:S(2)}, u32[]{:S(2)}) collective-permute-start(f32[29,8,128]{2,1,0:T(8,128)S(1)} %get-tuple-element.20), channel_id=1, source_target_pairs={{0,2},{2,0},{4,6},{6,4},{8,10},{10,8},{12,14},{14,12},{16,18},{18,... | collective-permute-start | bytes 356360 | tf_op jit(solution)/shard_map/ppermute | solution.py:497

commit v9 on v8

--- a/solution.py
+++ b/solution.py
@@ -15,7 +15,7 @@
 SEGMENT = 32
 PIECE = 2
 OUT = (0, 1, 2, 3)
-BACK = (0, 3, 2, 1)
+BACK = (0, 3, 1, 2)
 SUBLANES = 8
 SEGMENTS = LANES // SEGMENT
 BF16 = jnp.bfloat16

time: 51.4 us -> 51 us (level)
  no operation moved by 1% of the time
where the time goes in v9:
time: 51 us; the launch traced here: 50.7 us
  waiting for transfers between devices  20.8 us (41%)
  starting transfers between devices  18.7 us (37%)
  Pallas kernels  11 us (22%)
    ppermute x9, waiting for transfers between devices, swap(): return lax.ppermute(value, 'cell', [(d, d ^ step) for d in range(KX * KY)])  13.5 us
    ppermute x9, starting transfers between devices, swap(): return lax.ppermute(value, 'cell', [(d, d ^ step) for d in range(KX * KY)])  12.5 us
    all_to_all x1, waiting for transfers between devices, by_planes(): lax.all_to_all(sent, 'cell', split_axis=0, concat_axis=0, tiled=True)  5.7 us
    all_to_all x1, starting transfers between devices, by_planes(): lax.all_to_all(sent, 'cell', split_axis=0, concat_axis=0, tiled=True)  5.42 us
    pallas_call x1, Pallas kernels, half_bands(): pl.pallas_call(functools.partial(half_kernel, sz), out_shape=jax.ShapeDty...  3.57 us
    pallas_call x4, Pallas kernels, columns(): pl.pallas_call(functools.partial(columns_kernel, sz), out_shape=jax.Shape...  2.79 us
    pallas_call x1, Pallas kernels, band_product(): pl.pallas_call(functools.partial(band_kernel, sz), out_shape=[shape] * KY...  1.73 us
    ppermute x4, waiting for transfers between devices, swap_cores(): return lax.ppermute(value, 'aux', [(0, 1), (1, 0)])  1.56 us
  transfers between devices with their start and end apart: 14, of which 9 were waited for; matrix products, arithmetic and copies ran while one was open for 0% of the time, Pallas kernels for 15%

profile of v9, /device:TPU:0, one launch (start us, length us, event | category | flops | bytes accessed | tf_op | source)
XLA Modules:
  0.0 50.7 jit_solution(10560737770545904463)
XLA Ops:
  0.0 5.0 %collective-permute-start.6 = (f32[300,2,120]{2,1,0:T(2,128)}, f32[300,2,120]{2,1,0:T(2,128)S(1)}, u32[]{:S(2)}, u32[]{:S(2)}) collective-permute-start(f32[300,2,120]{2,1,0:T(2,128)} %bitcast.12), channel_id=1, source_target_pairs={{0,24},{2,26},{4,28},{6,30},{8,16},{10,18},{12,20},{14,22},{16,8},... | collective-permute-start | bytes 864008 | tf_op jit(solution)/shard_map/ppermute | solution.py:497
  5.1 3.6 %shard_map.55 = f32[4,4,9,8,128]{4,3,2,1,0:T(8,128)} custom-call(f32[300,4,300]{2,1,0:T(4,128)} %bitcast.16, f32[60,2,300]{2,1,0:T(2,128)} %bitcast.17), custom_call_target="tpu_custom_call" | custom-call | flops 99999997952 | bytes 1000000000 | tf_op jit(solution)/shard_map/pallas_call | solution.py:189
  8.6 5.4 %all-to-all-start = ((f32[16,9,8,128]{3,2,1,0:T(8,128)}), f32[16,9,8,128]{3,2,1,0:T(8,128)S(1)}, u32[]{:S(2)}, u32[]{:S(2)}) async-start(f32[16,9,8,128]{3,2,1,0:T(8,128)} %bitcast.15), calls=%async_computation | async-start | bytes 1179648 | tf_op jit(solution)/shard_map/all_to_all | solution.py:513
  14.1 0.1 pad_add_fusion.place_ref
  14.2 7.5 %collective-permute-done.3.in_ref = f32[300,2,120]{2,1,0:T(2,128)S(1)} collective-permute-done((f32[300,2,120]{2,1,0:T(2,128)}, f32[300,2,120]{2,1,0:T(2,128)S(1)}, u32[]{:S(2)}, u32[]{:S(2)}) %collective-permute-start.3) | collective-permute-done | bytes 288032 | tf_op jit(solution)/shard_map/ppermute | solution.py:497
  21.7 0.2 shard_map.57.refs_0_.own_ref
  22.0 0.2 shard_map.58.own_ref
  22.2 0.5 %collective-permute-start.4 = (f32[2,300,128]{2,1,0:T(8,128)S(1)}, f32[2,300,128]{2,1,0:T(8,128)S(1)}, u32[]{:S(2)}, u32[]{:S(2)}) collective-permute-start(f32[2,300,128]{2,1,0:T(8,128)S(1)} %shard_map.58.own_ref), channel_id=1, source_target_pairs={{0,1},{1,0},{2,3},{3,2},{4,5},{5,4},{6,7},{7,6},{8,9},{9,8},{10,11... | collective-permute-start | bytes 921608 | tf_op jit(solution)/shard_map/ppermute | solution.py:501
  22.7 0.2 shard_map.61.own_ref
  22.9 0.1 collective-permute-start.9
  23.0 0.3 collective-permute-start.7
  23.3 0.7 %collective-permute-done.4.other_ref = f32[2,300,128]{2,1,0:T(8,128)S(1)} collective-permute-done((f32[2,300,128]{2,1,0:T(8,128)S(1)}, f32[2,300,128]{2,1,0:T(8,128)S(1)}, u32[]{:S(2)}, u32[]{:S(2)}) %collective-permute-start.4) | collective-permute-done | bytes 307232 | tf_op jit(solution)/shard_map/ppermute | solution.py:501
  24.0 0.7 %shard_map.59.refs_4_ = bf16[704,512]{1,0:T(8,128)(2,1)S(1)} custom-call(s32[3]{0:T(128)S(1)} %pad_add_fusion.place_ref, f32[2,300,128]{2,1,0:T(8,128)S(1)} %shard_map.58.own_ref, f32[2,300,128]{2,1,0:T(8,128)S(1)} %collective-permute-done.4.other_ref), custom_call_target="tpu_custom_call" | custom-call | flops 10000000000 | bytes 100000000 | tf_op jit(solution)/shard_map/pallas_call | solution.py:486
  24.7 0.7 %shard_map.60.refs_5_ = bf16[704,512]{1,0:T(8,128)(2,1)S(1)} custom-call(s32[3]{0:T(128)S(1)} %pad_add_fusion.place_ref, f32[2,300,128]{2,1,0:T(8,128)S(1)} %shard_map.57.refs_0_.own_ref, f32[2,300,128]{2,1,0:T(8,128)S(1)} %collective-permute-done.5.other_ref), custom_call_target="tpu_custom_call" | custom-call | flops 10000000000 | bytes 100000000 | tf_op jit(solution)/shard_map/pallas_call | solution.py:486
  25.5 5.7 %all-to-all-done.cells_ref = f32[16,9,8,128]{3,2,1,0:T(8,128)S(1)} async-done(((f32[16,9,8,128]{3,2,1,0:T(8,128)}), f32[16,9,8,128]{3,2,1,0:T(8,128)S(1)}, u32[]{:S(2)}, u32[]{:S(2)}) %all-to-all-start) | async-done | bytes 589856 | tf_op jit(solution)/shard_map/all_to_all | solution.py:513
  31.2 0.8 %shard_map.56 = (f32[4,9,8,128]{3,2,1,0:T(8,128)S(1)}, f32[4,9,8,128]{3,2,1,0:T(8,128)S(1)}, f32[4,9,8,128]{3,2,1,0:T(8,128)S(1)}, f32[4,9,8,128]{3,2,1,0:T(8,128)S(1)}) custom-call(s32[3]{0:T(128)S(1)} %pad_add_fusion.place_ref, s32[3,16]{1,0:T(4,128)S(1)} %copy-done.2, f32[16,9,8,128]{3,2,1,0:T(8,128)S(1)} %all-to-all-done.cells_ref), custom_call_target="tpu_custom_call" | custom-call | flops 99999997952 | bytes 1000000000 | tf_op jit(solution)/shard_map/pallas_call | solution.py:275
  32.0 1.1 %collective-permute-start = (f32[4,9,8,128]{3,2,1,0:T(8,128)S(1)}, f32[4,9,8,128]{3,2,1,0:T(8,128)S(1)}, u32[]{:S(2)}, u32[]{:S(2)}) collective-permute-start(f32[4,9,8,128]{3,2,1,0:T(8,128)S(1)} %get-tuple-element.14), channel_id=1, source_target_pairs={{0,2},{2,0},{4,6},{6,4},{8,10},{10,8},{12,14},{14,12},{16,18},{18,... | collective-permute-start | bytes 442376 | tf_op jit(solution)/shard_map/ppermute | solution.py:497
  33.0 1.0 %collective-permute-start.1 = (f32[4,9,8,128]{3,2,1,0:T(8,128)S(1)}, f32[4,9,8,128]{3,2,1,0:T(8,128)S(1)}, u32[]{:S(2)}, u32[]{:S(2)}) collective-permute-start(f32[4,9,8,128]{3,2,1,0:T(8,128)S(1)} %get-tuple-element.15), channel_id=1, source_target_pairs={{0,4},{2,6},{4,0},{6,2},{8,12},{10,14},{12,8},{14,10},{16,20},{18,... | collective-permute-start | bytes 442376 | tf_op jit(solution)/shard_map/ppermute | solution.py:497
  34.0 1.5 %collective-permute-start.2 = (f32[4,9,8,128]{3,2,1,0:T(8,128)S(1)}, f32[4,9,8,128]{3,2,1,0:T(8,128)S(1)}, u32[]{:S(2)}, u32[]{:S(2)}) collective-permute-start(f32[4,9,8,128]{3,2,1,0:T(8,128)S(1)} %get-tuple-element.16), channel_id=1, source_target_pairs={{0,6},{2,4},{4,2},{6,0},{8,14},{10,12},{12,10},{14,8},{16,22},{18,... | collective-permute-start | bytes 442376 | tf_op jit(solution)/shard_map/ppermute | solution.py:497
  35.6 0.7 %shard_map.64.refs_7_ = bf16[704,512]{1,0:T(8,128)(2,1)S(1)} custom-call(s32[3]{0:T(128)S(1)} %pad_add_fusion.place_ref, f32[2,300,128]{2,1,0:T(8,128)S(1)} %shard_map.61.own_ref, f32[2,300,128]{2,1,0:T(8,128)S(1)} %collective-permute-done.9.other_ref), custom_call_target="tpu_custom_call" | custom-call | flops 10000000000 | bytes 100000000 | tf_op jit(solution)/shard_map/pallas_call | solution.py:486
  36.4 0.9 %collective-permute-done.8.other_ref = f32[2,300,128]{2,1,0:T(8,128)S(1)} collective-permute-done((f32[2,300,128]{2,1,0:T(8,128)S(1)}, f32[2,300,128]{2,1,0:T(8,128)S(1)}, u32[]{:S(2)}, u32[]{:S(2)}) %collective-permute-start.8) | collective-permute-done | bytes 307232 | tf_op jit(solution)/shard_map/ppermute | solution.py:501
  37.2 0.7 %shard_map.63.refs_6_ = bf16[704,512]{1,0:T(8,128)(2,1)S(1)} custom-call(s32[3]{0:T(128)S(1)} %pad_add_fusion.place_ref, f32[2,300,128]{2,1,0:T(8,128)S(1)} %shard_map.62.own_ref, f32[2,300,128]{2,1,0:T(8,128)S(1)} %collective-permute-done.8.other_ref), custom_call_target="tpu_custom_call" | custom-call | flops 1000000000 | bytes 10000000 | tf_op jit(solution)/shard_map/pallas_call | solution.py:486
  38.0 0.3 collective-permute-done.1.refs_2_
  38.3 1.8 %collective-permute-done.2.refs_3_ = f32[4,9,8,128]{3,2,1,0:T(8,128)S(1)} collective-permute-done((f32[4,9,8,128]{3,2,1,0:T(8,128)S(1)}, f32[4,9,8,128]{3,2,1,0:T(8,128)S(1)}, u32[]{:S(2)}, u32[]{:S(2)}) %collective-permute-start.2) | collective-permute-done | bytes 147488 | tf_op jit(solution)/shard_map/ppermute | solution.py:497
  40.0 1.7 %shard_map.65 = (f32[29,8,128]{2,1,0:T(8,128)S(1)}, f32[29,8,128]{2,1,0:T(8,128)S(1)}, f32[29,8,128]{2,1,0:T(8,128)S(1)}, f32[29,8,128]{2,1,0:T(8,128)S(1)}) custom-call(s32[3]{0:T(128)S(1)} %pad_add_fusion.place_ref, f32[4,9,8,128]{3,2,1,0:T(8,128)S(1)} %get-tuple-element.13.refs_0_, f32[4,9,8,128]{3,2,1,0:T(8,128)S(1)} %collective-permute-done.refs_1_, ...), custom_call_target="tpu_custom_call" | custom-call | flops 10000000000 | bytes 100000000 | tf_op jit(solution)/shard_map/pallas_call | solution.py:370
  41.8 1.7 %collective-permute-start.10 = (f32[29,8,128]{2,1,0:T(8,128)S(1)}, f32[29,8,128]{2,1,0:T(8,128)S(1)}, u32[]{:S(2)}, u32[]{:S(2)}) collective-permute-start(f32[29,8,128]{2,1,0:T(8,128)S(1)} %get-tuple-element.18), channel_id=1, source_target_pairs={{0,6},{2,4},{4,2},{6,0},{8,14},{10,12},{12,10},{14,8},{16,22},{18,... | collective-permute-start | bytes 356360 | tf_op jit(solution)/shard_map/ppermute | solution.py:497
  43.5 0.9 %collective-permute-start.11 = (f32[29,8,128]{2,1,0:T(8,128)S(1)}, f32[29,8,128]{2,1,0:T(8,128)S(1)}, u32[]{:S(2)}, u32[]{:S(2)}) collective-permute-start(f32[29,8,128]{2,1,0:T(8,128)S(1)} %get-tuple-element.19), channel_id=1, source_target_pairs={{0,2},{2,0},{4,6},{6,4},{8,10},{10,8},{12,14},{14,12},{16,18},{18,... | collective-permute-start | bytes 356360 | tf_op jit(solution)/shard_map/ppermute | solution.py:497
  44.4 0.9 %collective-permute-start.12 = (f32[29,8,128]{2,1,0:T(8,128)S(1)}, f32[29,8,128]{2,1,0:T(8,128)S(1)}, u32[]{:S(2)}, u32[]{:S(2)}) collective-permute-start(f32[29,8,128]{2,1,0:T(8,128)S(1)} %get-tuple-element.20), channel_id=1, source_target_pairs={{0,4},{2,6},{4,0},{6,2},{8,12},{10,14},{12,8},{14,10},{16,20},{18,... | collective-permute-start | bytes 356360 | tf_op jit(solution)/shard_map/ppermute | solution.py:497
  45.3 2.2 %collective-permute-done.10.refs_1_ = f32[29,8,128]{2,1,0:T(8,128)S(1)} collective-permute-done((f32[29,8,128]{2,1,0:T(8,128)S(1)}, f32[29,8,128]{2,1,0:T(8,128)S(1)}, u32[]{:S(2)}, u32[]{:S(2)}) %collective-permute-start.10) | collective-permute-done | bytes 118816 | tf_op jit(solution)/shard_map/ppermute | solution.py:497
  47.6 0.9 %collective-permute-done.11.refs_2_ = f32[29,8,128]{2,1,0:T(8,128)S(1)} collective-permute-done((f32[29,8,128]{2,1,0:T(8,128)S(1)}, f32[29,8,128]{2,1,0:T(8,128)S(1)}, u32[]{:S(2)}, u32[]{:S(2)}) %collective-permute-start.11) | collective-permute-done | bytes 118816 | tf_op jit(solution)/shard_map/ppermute | solution.py:497
  48.5 0.8 %collective-permute-done.12.refs_3_ = f32[29,8,128]{2,1,0:T(8,128)S(1)} collective-permute-done((f32[29,8,128]{2,1,0:T(8,128)S(1)}, f32[29,8,128]{2,1,0:T(8,128)S(1)}, u32[]{:S(2)}, u32[]{:S(2)}) %collective-permute-start.12) | collective-permute-done | bytes 118816 | tf_op jit(solution)/shard_map/ppermute | solution.py:497
  49.2 1.5 %shard_map.66 = f32[128,900]{1,0:T(8,128)} custom-call(s32[3]{0:T(128)S(1)} %pad_add_fusion.place_ref, s32[16]{0:T(128)S(1)} %copy-done, f32[29,8,128]{2,1,0:T(8,128)S(1)} %get-tuple-element.17.refs_0_, f32[29,8,128]{2,1,0:T(8,128)S(1)} %collective-permute-done.10.refs_1_, f32[29,8,128]{2,1,0:T(8,128)S(1)} %collective-permute-done.11.refs_2_, ...), custom_call_target="tpu_custom_call" | custom-call | tf_op jit(solution)/shard_map/pallas_call | solution.py:419
  (15 shorter events, 0.2 us)
Async XLA Ops:
  0.0 22.7 %collective-permute-start.6 = (f32[300,2,120]{2,1,0:T(2,128)}, f32[300,2,120]{2,1,0:T(2,128)S(1)}, u32[]{:S(2)}, u32[]{:S(2)}) collective-permute-start(f32[300,2,120]{2,1,0:T(2,128)} %bitcast.12), channel_id=1, source_target_pairs={{0,24},{2,26},{4,28},{6,30},{8,16},{10,18},{12,20},{14,22},{16,8},... | collective-permute-start | bytes 864008 | tf_op jit(solution)/shard_map/ppermute | solution.py:497
  5.0 16.7 %collective-permute-start.3 = (f32[300,2,120]{2,1,0:T(2,128)}, f32[300,2,120]{2,1,0:T(2,128)S(1)}, u32[]{:S(2)}, u32[]{:S(2)}) collective-permute-start(f32[300,2,120]{2,1,0:T(2,128)} %bitcast.13), channel_id=1, source_target_pairs={{0,8},{2,10},{4,12},{6,14},{8,0},{10,2},{12,4},{14,6},{16,24},{18,... | collective-permute-start | bytes 864008 | tf_op jit(solution)/shard_map/ppermute | solution.py:497
  8.6 13.3 %copy-start.1 = (f32[1,2,300,120]{3,1,2,0:T(2,128)S(1)}, f32[1,2,300,120]{3,1,2,0:T(2,128)}, u32[]{:S(2)}) copy-start(f32[1,2,300,120]{3,1,2,0:T(2,128)} %param.8) | copy-start | bytes 864004
  8.6 22.5 %all-to-all-start = ((f32[16,9,8,128]{3,2,1,0:T(8,128)}), f32[16,9,8,128]{3,2,1,0:T(8,128)S(1)}, u32[]{:S(2)}, u32[]{:S(2)}) async-start(f32[16,9,8,128]{3,2,1,0:T(8,128)} %bitcast.15), calls=%async_computation | async-start | bytes 1179648 | tf_op jit(solution)/shard_map/all_to_all | solution.py:513
  21.9 2.8 %collective-permute-start.5 = (f32[2,300,128]{2,1,0:T(8,128)S(1)}, f32[2,300,128]{2,1,0:T(8,128)S(1)}, u32[]{:S(2)}, u32[]{:S(2)}) collective-permute-start(f32[2,300,128]{2,1,0:T(8,128)S(1)} %shard_map.57.refs_0_.own_ref), channel_id=1, source_target_pairs={{0,1},{1,0},{2,3},{3,2},{4,5},{5,4},{6,7},{7,6},{8,9},{9,8},{10,11... | collective-permute-start | bytes 921608 | tf_op jit(solution)/shard_map/ppermute | solution.py:501
  22.2 1.8 %collective-permute-start.4 = (f32[2,300,128]{2,1,0:T(8,128)S(1)}, f32[2,300,128]{2,1,0:T(8,128)S(1)}, u32[]{:S(2)}, u32[]{:S(2)}) collective-permute-start(f32[2,300,128]{2,1,0:T(8,128)S(1)} %shard_map.58.own_ref), channel_id=1, source_target_pairs={{0,1},{1,0},{2,3},{3,2},{4,5},{5,4},{6,7},{7,6},{8,9},{9,8},{10,11... | collective-permute-start | bytes 921608 | tf_op jit(solution)/shard_map/ppermute | solution.py:501
  22.9 12.7 %collective-permute-start.9 = (f32[2,300,128]{2,1,0:T(8,128)S(1)}, f32[2,300,128]{2,1,0:T(8,128)S(1)}, u32[]{:S(2)}, u32[]{:S(2)}) collective-permute-start(f32[2,300,128]{2,1,0:T(8,128)S(1)} %shard_map.61.own_ref), channel_id=1, source_target_pairs={{0,1},{1,0},{2,3},{3,2},{4,5},{5,4},{6,7},{7,6},{8,9},{9,8},{10,11... | collective-permute-start | bytes 921608 | tf_op jit(solution)/shard_map/ppermute | solution.py:501
  23.0 12.5 %collective-permute-start.7 = (f32[2,300,128]{2,1,0:T(8,128)S(1)}, f32[2,300,128]{2,1,0:T(8,128)S(1)}, u32[]{:S(2)}, u32[]{:S(2)}) collective-permute-start(f32[2,300,128]{2,1,0:T(8,128)S(1)} %shard_map.61.own_ref), channel_id=1, source_target_pairs={{0,8},{2,10},{4,12},{6,14},{8,0},{10,2},{12,4},{14,6},{16,24},{18,... | collective-permute-start | bytes 921608 | tf_op jit(solution)/shard_map/ppermute | solution.py:497
  24.7 6.4 %copy-start.2 = (s32[3,16]{1,0:T(4,128)S(1)}, s32[3,16]{1,0:T(4,128)}, u32[]{:S(2)}) copy-start(s32[3,16]{1,0:T(4,128)} %offset_ref.1) | copy-start | bytes 580
  32.0 6.0 %collective-permute-start = (f32[4,9,8,128]{3,2,1,0:T(8,128)S(1)}, f32[4,9,8,128]{3,2,1,0:T(8,128)S(1)}, u32[]{:S(2)}, u32[]{:S(2)}) collective-permute-start(f32[4,9,8,128]{3,2,1,0:T(8,128)S(1)} %get-tuple-element.14), channel_id=1, source_target_pairs={{0,2},{2,0},{4,6},{6,4},{8,10},{10,8},{12,14},{14,12},{16,18},{18,... | collective-permute-start | bytes 442376 | tf_op jit(solution)/shard_map/ppermute | solution.py:497
  33.0 5.2 %collective-permute-start.1 = (f32[4,9,8,128]{3,2,1,0:T(8,128)S(1)}, f32[4,9,8,128]{3,2,1,0:T(8,128)S(1)}, u32[]{:S(2)}, u32[]{:S(2)}) collective-permute-start(f32[4,9,8,128]{3,2,1,0:T(8,128)S(1)} %get-tuple-element.15), channel_id=1, source_target_pairs={{0,4},{2,6},{4,0},{6,2},{8,12},{10,14},{12,8},{14,10},{16,20},{18,... | collective-permute-start | bytes 442376 | tf_op jit(solution)/shard_map/ppermute | solution.py:497
  34.0 6.0 %collective-permute-start.2 = (f32[4,9,8,128]{3,2,1,0:T(8,128)S(1)}, f32[4,9,8,128]{3,2,1,0:T(8,128)S(1)}, u32[]{:S(2)}, u32[]{:S(2)}) collective-permute-start(f32[4,9,8,128]{3,2,1,0:T(8,128)S(1)} %get-tuple-element.16), channel_id=1, source_target_pairs={{0,6},{2,4},{4,2},{6,0},{8,14},{10,12},{12,10},{14,8},{16,22},{18,... | collective-permute-start | bytes 442376 | tf_op jit(solution)/shard_map/ppermute | solution.py:497
  35.6 1.7 %collective-permute-start.8 = (f32[2,300,128]{2,1,0:T(8,128)S(1)}, f32[2,300,128]{2,1,0:T(8,128)S(1)}, u32[]{:S(2)}, u32[]{:S(2)}) collective-permute-start(f32[2,300,128]{2,1,0:T(8,128)S(1)} %shard_map.62.own_ref), channel_id=1, source_target_pairs={{0,1},{1,0},{2,3},{3,2},{4,5},{5,4},{6,7},{7,6},{8,9},{9,8},{10,11... | collective-permute-start | bytes 921608 | tf_op jit(solution)/shard_map/ppermute | solution.py:501
  37.9 11.3 %copy-start = (s32[16]{0:T(128)S(1)}, s32[16]{0:T(128)}, u32[]{:S(2)}) copy-start(s32[16]{0:T(128)} %transfer_ref.1) | copy-start | bytes 196
  41.8 5.8 %collective-permute-start.10 = (f32[29,8,128]{2,1,0:T(8,128)S(1)}, f32[29,8,128]{2,1,0:T(8,128)S(1)}, u32[]{:S(2)}, u32[]{:S(2)}) collective-permute-start(f32[29,8,128]{2,1,0:T(8,128)S(1)} %get-tuple-element.18), channel_id=1, source_target_pairs={{0,6},{2,4},{4,2},{6,0},{8,14},{10,12},{12,10},{14,8},{16,22},{18,... | collective-permute-start | bytes 356360 | tf_op jit(solution)/shard_map/ppermute | solution.py:497
  43.5 5.0 %collective-permute-start.11 = (f32[29,8,128]{2,1,0:T(8,128)S(1)}, f32[29,8,128]{2,1,0:T(8,128)S(1)}, u32[]{:S(2)}, u32[]{:S(2)}) collective-permute-start(f32[29,8,128]{2,1,0:T(8,128)S(1)} %get-tuple-element.19), channel_id=1, source_target_pairs={{0,2},{2,0},{4,6},{6,4},{8,10},{10,8},{12,14},{14,12},{16,18},{18,... | collective-permute-start | bytes 356360 | tf_op jit(solution)/shard_map/ppermute | solution.py:497
  44.4 4.8 %collective-permute-start.12 = (f32[29,8,128]{2,1,0:T(8,128)S(1)}, f32[29,8,128]{2,1,0:T(8,128)S(1)}, u32[]{:S(2)}, u32[]{:S(2)}) collective-permute-start(f32[29,8,128]{2,1,0:T(8,128)S(1)} %get-tuple-element.20), channel_id=1, source_target_pairs={{0,4},{2,6},{4,0},{6,2},{8,12},{10,14},{12,8},{14,10},{16,20},{18,... | collective-permute-start | bytes 356360 | tf_op jit(solution)/shard_map/ppermute | solution.py:497
